TPU v7x, 256 devices: a whole 4x4x8 slice. The times are simulated.
256 devices in a mesh: row: 16 (over y_hi, x, core), col: 16 (over y_lo, z).
Axes of the slice: x: 4, y: 4 (y_hi: 2, y_lo: 2; y = y_hi * 2 + y_lo), z: 8, core: 2. Of those that a mesh axis runs over, the one named last changes fastest.
Arguments:
- a_stored: float32 [4096, 65536], P('row', 'col'), may hold values from -6 to 6
- b_stored: float32 [65536, 4096], P('row', 'col'), may hold values from -0.0546875 to 0.0546875
Outputs:
- product: float32 [4096, 4096], P('row', 'col')
All inputs are finite; a program needn't handle non-finite values.
Results may differ from a plain program's by a relative error of at most 0.0003.
Values sent between devices are 32-bit elements; how exact they have to be, the bound alone decides.
No kernel may reach another device: no remote copies, remote signals or barrier semaphores. Data moves between devices by JAX's collectives and lax.ppermute only.
A program may use at most 128 MiB of HBM per device.

v0:
```python
import jax
import jax.numpy as jnp
from jax import lax
from jax.sharding import PartitionSpec as P

CBLK = 128
STEPS = 2


def from_behind(block, axis, distance):
    devices = range(lax.axis_size(axis))
    route = [((i - distance) % len(devices), i) for i in devices]
    return lax.ppermute(block, axis, route)


def multiply(left, right):
    return jnp.dot(left, right, precision=lax.Precision.HIGHEST, preferred_element_type=jnp.float32)


def on_device(a_stored, b_stored):
    col_count = lax.axis_size("col")
    row_count = lax.axis_size("row")
    kblocks = min(row_count, col_count)
    row_index = lax.axis_index("row")
    col_index = lax.axis_index("col")
    rows_a, width_a = a_stored.shape
    height_b, cols_b = b_stored.shape
    blocks_a = width_a // (CBLK * kblocks)
    blocks_b = height_b // (CBLK * kblocks)
    grouped_a = a_stored.reshape(rows_a, kblocks, blocks_a, CBLK)
    grouped_b = b_stored.reshape(kblocks, blocks_b, CBLK, cols_b)
    wanted = (row_index + jnp.arange(col_count, dtype=jnp.int32)) % kblocks
    chosen = jnp.take(grouped_a, wanted, axis=1)
    a_block = lax.all_to_all(
        jnp.transpose(chosen, (0, 2, 1, 3)).reshape(rows_a, blocks_a, col_count * CBLK),
        "col",
        split_axis=2,
        concat_axis=2,
        tiled=True,
    ).reshape(rows_a, -1)
    wanted = (col_index + jnp.arange(row_count, dtype=jnp.int32)) % kblocks
    chosen = jnp.take(grouped_b, wanted, axis=0)
    b_block = lax.all_to_all(
        jnp.transpose(chosen, (1, 0, 2, 3)).reshape(blocks_b, row_count * CBLK, cols_b),
        "row",
        split_axis=1,
        concat_axis=1,
        tiled=True,
    ).reshape(-1, cols_b)
    total = multiply(a_block, b_block)
    for shifts in range(STEPS):
        a_block = from_behind(a_block, "col", -1)
        b_block = from_behind(b_block, "row", -1)
        total = total + multiply(a_block, b_block)
    return total


def solution(mesh):
    return jax.shard_map(
        on_device,
        mesh=mesh,
        in_specs=(P("row", "col"), P("row", "col")),
        out_specs=P("row", "col"),
        check_vma=False,
    )
```

profile of v0, /device:TPU:6, one launch (start us, length us, event | category | flops | bytes accessed | tf_op | source)
XLA Modules:
  0.0 438.3 jit_solution(14753808365088705088)
XLA Ops:
  0.0 4.9 %gather_fusion.1 = f32[16,2,128,256]{3,2,1,0:T(8,128)} fusion(f32[16,2,128,256]{3,2,1,0:T(8,128)} %bitcast.23, s32[1024]{0:T(1024)S(1)} %pad_clamp_fusion), kind=kCustom, calls=%fused_computation.1 | custom fusion | bytes 8388672 | tf_op jit(solution)/shard_map/jit(_take)/gather | solution.py:42
  5.0 2.7 select_bitcast_fusion.1
  7.7 0.4 copy.20
  8.1 12.2 %copy.21 = f32[2,2048,256]{2,0,1:T(2,128)} copy(f32[2,2048,256]{2,1,0:T(8,128)S(1)} %bitcast.20) | data formatting | bytes 8388608 | tf_op jit(solution)/shard_map/reshape | solution.py:44
  20.4 7.4 %all-to-all-start.1 = ((f32[2,2048,256]{2,0,1:T(2,128)}), f32[2,2048,256]{2,0,1:T(2,128)}, u32[]{:S(2)}, u32[]{:S(2)}) async-start(f32[2,2048,256]{2,0,1:T(2,128)} %copy.21), calls=%async_computation.1 | async-start | bytes 8388608 | tf_op jit(solution)/shard_map/all_to_all | solution.py:43
  27.8 5.6 %copy.16 = f32[256,4096]{0,1:T(8,128)} copy(f32[256,4096]{1,0:T(8,128)} %param.2) | data formatting | bytes 8388608 | tf_op args[0]
  33.4 5.3 %copy.17 = f32[256,16,2,128]{3,0,2,1:T(8,128)} copy(f32[256,16,2,128]{0,3,2,1:T(8,128)} %bitcast.22) | data formatting | bytes 8388608 | tf_op jit(solution)/shard_map/reshape | solution.py:30
  38.8 4.9 %gather_fusion = f32[16,256,2,128]{3,1,2,0:T(8,128)} fusion(f32[256,16,2,128]{3,0,2,1:T(8,128)} %copy.17, s32[1024]{0:T(1024)S(1)} %pad_clamp_fusion.1), kind=kCustom, calls=%fused_computation | custom fusion | bytes 8388672 | tf_op jit(solution)/shard_map/jit(_take)/gather | solution.py:33
  43.7 4.7 %select_bitcast_fusion = f32[256,2,16,128]{3,0,1,2:T(8,128)} fusion(f32[16,256,2,128]{3,1,2,0:T(8,128)} %gather_fusion, pred[16]{0:T(512)(128)(4,1)S(1)} %compare_and_fusion.1), kind=kLoop, calls=%fused_computation.2 | loop fusion | flops 1048576 | bytes 8388624 | tf_op jit(solution)/shard_map/jit(_take)/select_n | solution.py:33
  48.5 5.3 %copy.18 = f32[256,2,16,128]{0,3,2,1:T(8,128)} copy(f32[256,2,16,128]{3,0,1,2:T(8,128)} %select_bitcast_fusion) | data formatting | bytes 8388608 | tf_op jit(solution)/shard_map/jit(_take)/select_n | solution.py:33
  53.8 8.8 %copy.19 = f32[256,2,2048]{0,1,2:T(2,128)} copy(f32[256,2,2048]{0,2,1:T(8,128)} %bitcast.21) | data formatting | bytes 8388608 | tf_op jit(solution)/shard_map/reshape | solution.py:35
  62.6 19.1 %all-to-all-done.1 = f32[2,2048,256]{2,0,1:T(2,128)} async-done(((f32[2,2048,256]{2,0,1:T(2,128)}), f32[2,2048,256]{2,0,1:T(2,128)}, u32[]{:S(2)}, u32[]{:S(2)}) %all-to-all-start.1) | async-done | bytes 4194336 | tf_op jit(solution)/shard_map/all_to_all | solution.py:43
  81.7 8.7 %all-to-all-start = ((f32[256,2,2048]{0,1,2:T(2,128)}), f32[256,2,2048]{0,1,2:T(2,128)}, u32[]{:S(2)}, u32[]{:S(2)}) async-start(f32[256,2,2048]{0,1,2:T(2,128)} %copy.19), calls=%async_computation | async-start | bytes 8388608 | tf_op jit(solution)/shard_map/all_to_all | solution.py:34
  90.5 4.5 %copy.23 = f32[2,2048,256]{2,1,0:T(8,128)} copy(f32[2,2048,256]{2,0,1:T(2,128)} %all-to-all-done.1) | data formatting | bytes 8388608 | tf_op jit(solution)/shard_map/all_to_all | solution.py:43
  94.9 1.6 collective-permute-start.1
  96.6 101.2 %all-to-all-done = f32[256,2,2048]{0,1,2:T(2,128)} async-done(((f32[256,2,2048]{0,1,2:T(2,128)}), f32[256,2,2048]{0,1,2:T(2,128)}, u32[]{:S(2)}, u32[]{:S(2)}) %all-to-all-start) | async-done | bytes 4194336 | tf_op jit(solution)/shard_map/all_to_all | solution.py:34
  197.7 2.5 copy.24
  200.3 1.9 collective-permute-start
  202.2 0.0 collective-permute-done.1
  202.2 0.0 collective-permute-start.3
  202.2 134.9 %collective-permute-done = f32[256,4096]{0,1:T(8,128)S(1)} collective-permute-done((f32[256,4096]{0,1:T(8,128)S(1)}, f32[256,4096]{0,1:T(8,128)S(1)}, u32[]{:S(2)}, u32[]{:S(2)}) %collective-permute-start) | collective-permute-done | bytes 4194336 | tf_op jit(solution)/shard_map/ppermute | solution.py:13
  337.1 4.6 %collective-permute-start.2 = (f32[256,4096]{0,1:T(8,128)S(1)}, f32[256,4096]{0,1:T(8,128)S(1)}, u32[]{:S(2)}, u32[]{:S(2)}) collective-permute-start(f32[256,4096]{0,1:T(8,128)S(1)} %collective-permute-done), channel_id=1, source_target_pairs={{1,0},{2,1},{3,2},{4,3},{5,4},{6,5},{7,6},{8,7},{9,8},{10,9},{11,1... | collective-permute-start | bytes 12582920 | tf_op jit(solution)/shard_map/ppermute | solution.py:13
  341.7 10.4 %convolution_bitcast_fusion = f32[256,256]{1,0:T(8,128)S(1)} fusion(f32[256,2,2048]{0,1,2:T(2,128)} %all-to-all-done, f32[2,2048,256]{2,0,1:T(2,128)} %all-to-all-done.1), kind=kOutput, calls=%fused_computation.6 | convolution fusion | flops 3221225472 | bytes 8650752 | tf_op jit(solution)/shard_map/dot_general | solution.py:17
  352.2 8.9 %convolution_add_fusion.1 = f32[256,256]{1,0:T(8,128)S(1)} fusion(f32[256,256]{1,0:T(8,128)S(1)} %convolution_bitcast_fusion, f32[256,4096]{0,1:T(8,128)S(1)} %collective-permute-done, f32[4096,256]{1,0:T(8,128)} %collective-permute-done.1), kind=kOutput, calls=%fused_computation.5 | convolution fusion | flops 3221291008 | bytes 8912896 | tf_op jit(solution)/shard_map/dot_general | solution.py:17
  361.1 0.0 collective-permute-done.3
  361.1 69.7 %collective-permute-done.2 = f32[256,4096]{0,1:T(8,128)S(1)} collective-permute-done((f32[256,4096]{0,1:T(8,128)S(1)}, f32[256,4096]{0,1:T(8,128)S(1)}, u32[]{:S(2)}, u32[]{:S(2)}) %collective-permute-start.2) | collective-permute-done | bytes 4194336 | tf_op jit(solution)/shard_map/ppermute | solution.py:13
  430.9 7.5 %convolution_add_fusion = f32[256,256]{1,0:T(8,128)} fusion(f32[256,256]{1,0:T(8,128)S(1)} %convolution_add_fusion.1, f32[256,4096]{0,1:T(8,128)S(1)} %collective-permute-done.2, f32[4096,256]{1,0:T(8,128)S(1)} %collective-permute-done.3), kind=kOutput, calls=%fused_computation.4 | convolution fusion | flops 3221291008 | bytes 8912896 | tf_op jit(solution)/shard_map/dot_general | solution.py:17
  (6 shorter events, 0.1 us)
Async XLA Ops:
  20.4 61.4 %all-to-all-start.1 = ((f32[2,2048,256]{2,0,1:T(2,128)}), f32[2,2048,256]{2,0,1:T(2,128)}, u32[]{:S(2)}, u32[]{:S(2)}) async-start(f32[2,2048,256]{2,0,1:T(2,128)} %copy.21), calls=%async_computation.1 | async-start | bytes 8388608 | tf_op jit(solution)/shard_map/all_to_all | solution.py:43
  81.7 116.0 %all-to-all-start = ((f32[256,2,2048]{0,1,2:T(2,128)}), f32[256,2,2048]{0,1,2:T(2,128)}, u32[]{:S(2)}, u32[]{:S(2)}) async-start(f32[256,2,2048]{0,1,2:T(2,128)} %copy.19), calls=%async_computation | async-start | bytes 8388608 | tf_op jit(solution)/shard_map/all_to_all | solution.py:34
  94.9 107.3 %collective-permute-start.1 = (f32[4096,256]{1,0:T(8,128)}, f32[4096,256]{1,0:T(8,128)}, u32[]{:S(2)}, u32[]{:S(2)}) collective-permute-start(f32[4096,256]{1,0:T(8,128)} %bitcast.10), channel_id=1, source_target_pairs={{16,0},{32,16},{48,32},{64,48},{80,64},{96,80},{112,96},{128,112},... | collective-permute-start | bytes 12582920 | tf_op jit(solution)/shard_map/ppermute | solution.py:13
  200.3 136.8 %collective-permute-start = (f32[256,4096]{0,1:T(8,128)S(1)}, f32[256,4096]{0,1:T(8,128)S(1)}, u32[]{:S(2)}, u32[]{:S(2)}) collective-permute-start(f32[256,4096]{0,1:T(8,128)S(1)} %bitcast.24), channel_id=1, source_target_pairs={{1,0},{2,1},{3,2},{4,3},{5,4},{6,5},{7,6},{8,7},{9,8},{10,9},{11,1... | collective-permute-start | bytes 12582920 | tf_op jit(solution)/shard_map/ppermute | solution.py:13
  202.2 158.9 %collective-permute-start.3 = (f32[4096,256]{1,0:T(8,128)}, f32[4096,256]{1,0:T(8,128)S(1)}, u32[]{:S(2)}, u32[]{:S(2)}) collective-permute-start(f32[4096,256]{1,0:T(8,128)} %collective-permute-done.1), channel_id=1, source_target_pairs={{16,0},{32,16},{48,32},{64,48},{80,64},{96,80},{112,96},{128,112},... | collective-permute-start | bytes 12582920 | tf_op jit(solution)/shard_map/ppermute | solution.py:13
  337.1 93.8 %collective-permute-start.2 = (f32[256,4096]{0,1:T(8,128)S(1)}, f32[256,4096]{0,1:T(8,128)S(1)}, u32[]{:S(2)}, u32[]{:S(2)}) collective-permute-start(f32[256,4096]{0,1:T(8,128)S(1)} %collective-permute-done), channel_id=1, source_target_pairs={{1,0},{2,1},{3,2},{4,3},{5,4},{6,5},{7,6},{8,7},{9,8},{10,9},{11,1... | collective-permute-start | bytes 12582920 | tf_op jit(solution)/shard_map/ppermute | solution.py:13
where the time goes:
time: 439 us; the launch traced here: 438 us
  waiting for transfers between devices  325 us (74%)
  local copies, waits for them, and re-layouts  54.6 us (12%)
  matrix products  26.8 us (6%)
  starting transfers between devices  24.4 us (6%)
  other arithmetic  7.5 us (2%)
    ppermute x4, waiting for transfers between devices, from_behind(): return lax.ppermute(block, axis, route)  205 us
    all_to_all x1, waiting for transfers between devices, on_device(): lax.all_to_all(jnp.transpose(chosen, (0, 2, 1, 3)).reshape(rows_a, blocks...  101 us
    dot_general x3, matrix products, multiply(): jnp.dot(left, right, precision=lax.Precision.HIGHEST, preferred_element_t...  26.8 us
    all_to_all x1, waiting for transfers between devices, on_device(): lax.all_to_all(jnp.transpose(chosen, (1, 0, 2, 3)).reshape(blocks_b, row_...  19.1 us
    reshape x1, local copies, waits for them, and re-layouts, on_device(): jnp.transpose(chosen, (1, 0, 2, 3))  12.2 us
  transfers between devices with their start and end apart: 6, of which 4 were waited for; matrix products, arithmetic and copies ran while one was open for 14% of the time, Pallas kernels for 0%

commit v1 on v0

v1 whole, which is shorter than its diff:
```python
import functools

import jax
import jax.numpy as jnp
from jax import lax
from jax.experimental import pallas as pl
from jax.experimental.pallas import tpu as pltpu
from jax.sharding import PartitionSpec as P

CBLK = 128
PIECES = 1


def order_body(shift_ref, in_ref, *out_refs):
    del shift_ref
    height = in_ref.shape[0] // len(out_refs)
    for q, out_ref in enumerate(out_refs):
        out_ref[0] = in_ref[q * height : (q + 1) * height, :]


def order_for_rows(b_stored, shift, blocks, pieces):
    height, cols = b_stored.shape
    deep = height // blocks
    part = deep // pieces
    return pl.pallas_call(
        order_body,
        grid_spec=pltpu.PrefetchScalarGridSpec(
            num_scalar_prefetch=1,
            grid=(blocks,),
            in_specs=[pl.BlockSpec((deep, cols), lambda d, shift: ((d + shift[0]) % blocks, 0))],
            out_specs=[pl.BlockSpec((1, part, cols), lambda d, shift: (d, 0, 0))] * pieces,
        ),
        out_shape=[jax.ShapeDtypeStruct((blocks, part, cols), jnp.float32)] * pieces,
        name="order_panel",
    )(shift, b_stored)


def split(value):
    high = value.astype(jnp.bfloat16)
    low = (value - high.astype(jnp.float32)).astype(jnp.bfloat16)
    return high, low


def product_body(blocks, pieces, row_ref, a_ref, *refs):
    panels, out_ref, a_high, a_low = refs[: 3 * pieces], refs[-3], refs[-2], refs[-1]
    j = pl.program_id(0)
    deep = a_ref.shape[1] // blocks

    @pl.when(j == 0)
    def _():
        for k in range(blocks):
            high, low = split(a_ref[:, k * deep : (k + 1) * deep])
            a_high[k] = high
            a_low[k] = low

    total = jnp.zeros(out_ref.shape[1:], jnp.float32)
    dot = functools.partial(jnp.dot, preferred_element_type=jnp.float32)
    for s in range(3):
        k = (row_ref[0] + j + s) % blocks
        panel = jnp.concatenate([ref[0] for ref in panels[s * pieces : (s + 1) * pieces]], axis=0)
        high, low = split(panel)
        total += dot(a_high[k], high) + (dot(a_high[k], low) + dot(a_low[k], high))
    out_ref[0] = total


def partial_products(row_index, a_stored, panels, pieces):
    blocks, part, cols = panels[0].shape
    rows, width = a_stored.shape
    deep = width // blocks
    return pl.pallas_call(
        functools.partial(product_body, blocks, pieces),
        grid_spec=pltpu.PrefetchScalarGridSpec(
            num_scalar_prefetch=1,
            grid=(blocks,),
            in_specs=[pl.BlockSpec((rows, width), lambda j, row: (0, 0))]
            + [pl.BlockSpec((1, part, cols), lambda j, row: (j, 0, 0))] * len(panels),
            out_specs=pl.BlockSpec((1, rows, cols), lambda j, row: (j, 0, 0)),
            scratch_shapes=[pltpu.VMEM((blocks, rows, deep), jnp.bfloat16)] * 2,
        ),
        out_shape=jax.ShapeDtypeStruct((blocks, rows, cols), jnp.float32),
        compiler_params=pltpu.CompilerParams(vmem_limit_bytes=40 * 2**20),
        name="partial_products",
    )(row_index, a_stored, *panels)


def shift_rows(block, distance):
    n = lax.axis_size("row")
    return lax.ppermute(block, "row", [((i - distance) % n, i) for i in range(n)])


def on_device(a_stored, b_stored):
    blocks = lax.axis_size("row")
    row_index = lax.axis_index("row").astype(jnp.int32)
    col_index = lax.axis_index("col").astype(jnp.int32)
    outgoing = order_for_rows(b_stored, (col_index + 1).reshape(1), blocks, PIECES)
    behind, own, ahead = [], [], []
    for piece in outgoing:
        piece = lax.all_to_all(piece, "row", split_axis=0, concat_axis=0, tiled=True)
        piece = lax.all_to_all(piece, "col", split_axis=0, concat_axis=0, tiled=True)
        own.append(piece)
        behind.append(shift_rows(piece, 1))
        ahead.append(shift_rows(piece, -1))
    partial = partial_products(row_index.reshape(1), a_stored, behind + own + ahead, PIECES)
    return lax.psum_scatter(partial, "col", scatter_dimension=0, tiled=True).reshape(partial.shape[1:])


def solution(mesh):
    return jax.shard_map(
        on_device,
        mesh=mesh,
        in_specs=(P("row", "col"), P("row", "col")),
        out_specs=P("row", "col"),
        check_vma=False,
    )
```

time: 439 us -> 334 us (0.76)
  the two profiles are of different devices: /device:TPU:6 before, /device:TPU:8 now
where the time goes in v1:
time: 334 us; the launch traced here: 332 us
  blocking collectives  160 us (48%)
  waiting for transfers between devices  129 us (39%)
  Pallas kernels  24.5 us (7%)
  between operations  13.4 us (4%)
  local copies, waits for them, and re-layouts  4.12 us (1%)
    all_to_all x1, blocking collectives, on_device(): lax.all_to_all(piece, 'col', split_axis=0, concat_axis=0, tiled=True)  102 us
    reduce_scatter x1, waiting for transfers between devices, on_device(): lax.psum_scatter(partial, 'col', scatter_dimension=0, tiled=True)  77.8 us
    all_to_all x1, blocking collectives, on_device(): lax.all_to_all(piece, 'row', split_axis=0, concat_axis=0, tiled=True)  57.8 us
    ppermute x2, waiting for transfers between devices, shift_rows(): lax.ppermute(block, 'row', [((i - distance) % n, i) for i in range(n)])  51.4 us
    pallas_call x1, Pallas kernels, partial_products(): pl.pallas_call(functools.partial(product_body, blocks, pieces), grid_spec...  14.4 us
    pallas_call x1, Pallas kernels, order_for_rows(): pl.pallas_call(order_body, grid_spec=pltpu.PrefetchScalarGridSpec(num_sca...  10.1 us
  transfers between devices with their start and end apart: 3, of which 3 were waited for; matrix products, arithmetic and copies ran while one was open for 0% of the time, Pallas kernels for 0%

profile of v1, /device:TPU:8, one launch (start us, length us, event | category | flops | bytes accessed | tf_op | source)
XLA Modules:
  0.0 331.9 jit_solution(6322295064444582441)
XLA Ops:
  6.5 0.0 reduce-scatter.2.cloned.1.call-start
  6.5 10.1 %order_panel.1 = f32[16,256,256]{2,1,0:T(8,128)} custom-call(s32[1]{0:T(128)} %bitcast.1.shift_ref, f32[4096,256]{1,0:T(8,128)} %in_ref.1), custom_call_target="tpu_custom_call" | custom-call | tf_op jit(solution)/shard_map/order_panel/pallas_call | solution.py:25
  16.6 57.8 %all_to_all.10 = f32[16,256,256]{2,1,0:T(8,128)S(1)} all-to-all(f32[16,256,256]{2,1,0:T(8,128)} %order_panel.1), channel_id=1, replica_groups=mesh['row'=16,'col'=16] {'row'}, dimensions={0} | all-to-all | bytes 8388608 | tf_op jit(solution)/shard_map/all_to_all | solution.py:98
  74.5 102.4 %all_to_all.11.refs_1_ = f32[16,256,256]{2,1,0:T(8,128)} all-to-all(f32[16,256,256]{2,1,0:T(8,128)S(1)} %all_to_all.10), channel_id=1, replica_groups=mesh['row'=16,'col'=16] {'col'}, dimensions={0} | all-to-all | bytes 8388608 | tf_op jit(solution)/shard_map/all_to_all | solution.py:99
  176.9 0.0 collective-permute-start.1
  176.9 0.5 collective-permute-start
  177.4 45.8 %collective-permute-done.1.refs_2_ = f32[16,256,256]{2,1,0:T(8,128)} collective-permute-done((f32[16,256,256]{2,1,0:T(8,128)}, f32[16,256,256]{2,1,0:T(8,128)}, u32[]{:S(2)}, u32[]{:S(2)}) %collective-permute-start.1) | collective-permute-done | bytes 4194336 | tf_op jit(solution)/shard_map/ppermute | solution.py:88
  223.2 5.5 %collective-permute-done.refs_0_ = f32[16,256,256]{2,1,0:T(8,128)} collective-permute-done((f32[16,256,256]{2,1,0:T(8,128)}, f32[16,256,256]{2,1,0:T(8,128)}, u32[]{:S(2)}, u32[]{:S(2)}) %collective-permute-start) | collective-permute-done | bytes 4194336 | tf_op jit(solution)/shard_map/ppermute | solution.py:88
  228.7 0.0 copy-start.1
  228.7 2.2 copy-done.1
  230.9 14.4 %partial_products.1 = f32[16,256,256]{2,1,0:T(8,128)S(1)} custom-call(s32[1]{0:T(128)} %bitcast.row_ref, f32[256,4096]{1,0:T(8,128)S(1)} %copy-done.1, f32[16,256,256]{2,1,0:T(8,128)} %collective-permute-done.refs_0_, f32[16,256,256]{2,1,0:T(8,128)} %all_to_all.11.refs_1_, f32[16,256,256]{2,1,0:T(8,128)} %collective-permute-done.1.refs_2_), custom_call_target="tpu_custom_call" | custom-call | tf_op jit(solution)/shard_map/partial_products/pallas_call | solution.py:70
  245.3 0.0 copy-start
  245.3 1.9 copy-done
  247.3 0.0 reduce-scatter.2.cloned.1.call-update
  247.3 77.8 %reduce-scatter.2.cloned.1.call-done = f32[1,256,256]{2,1,0:T(8,128)} async-done(((f32[16,256,256]{2,1,0:T(8,128)}), f32[1,256,256]{2,1,0:T(8,128)}) %reduce-scatter.2.cloned.1.call-update) | async-done | bytes 262160 | tf_op jit(solution)/shard_map/reduce_scatter | solution.py:104
Async XLA Ops:
  6.5 318.5 %reduce-scatter.2.cloned.1.call-start = ((), (), s32[]{:S(2)}) async-start(), calls=%async_computation.3 | async-start | bytes 4456448 | tf_op jit(solution)/shard_map/reduce_scatter | solution.py:104
  176.9 46.3 %collective-permute-start.1 = (f32[16,256,256]{2,1,0:T(8,128)}, f32[16,256,256]{2,1,0:T(8,128)}, u32[]{:S(2)}, u32[]{:S(2)}) collective-permute-start(f32[16,256,256]{2,1,0:T(8,128)} %all_to_all.11.refs_1_), channel_id=1, source_target_pairs={{16,0},{32,16},{48,32},{64,48},{80,64},{96,80},{112,96},{128,112},... | collective-permute-start | bytes 12582920 | tf_op jit(solution)/shard_map/ppermute | solution.py:88
  176.9 51.9 %collective-permute-start = (f32[16,256,256]{2,1,0:T(8,128)}, f32[16,256,256]{2,1,0:T(8,128)}, u32[]{:S(2)}, u32[]{:S(2)}) collective-permute-start(f32[16,256,256]{2,1,0:T(8,128)} %all_to_all.11.refs_1_), channel_id=1, source_target_pairs={{240,0},{0,16},{16,32},{32,48},{48,64},{64,80},{80,96},{96,112},{1... | collective-permute-start | bytes 12582920 | tf_op jit(solution)/shard_map/ppermute | solution.py:88
  228.7 2.2 copy-start.1
  245.3 1.9 copy-start
Sparse Core Ops, SparseCore 0:
  247.4 77.6 reduce-scatter.1

commit v2 on v0

v2 whole, which is shorter than its diff:
```python
import functools

import jax
import jax.numpy as jnp
import numpy as np
from jax import lax
from jax.experimental import pallas as pl
from jax.experimental.pallas import tpu as pltpu
from jax.sharding import Mesh
from jax.sharding import PartitionSpec as P

AXES = ("y_hi", "x", "core", "y_lo", "z")
ROW, COL = AXES[:3], AXES[3:]
WINDOW = 3
OFFSETS = (4, -3, 3, -2, 2, -1, 1, 0)
GROUPS = (2, 2, 4)
EARLY = 7
LARGE = 60 * 2**20
SMALL = 16 * 2**20


def order_body(along, index_ref, in_ref, *refs):
    out_refs, (held, in_sems, out_sems) = refs[:-3], refs[-3:]
    count, deep = held.shape[0], held.shape[1 + along]

    def bring(d):
        span = pl.ds(pl.multiple_of(index_ref[d] * deep, deep), deep)
        part = in_ref.at[span, :] if along == 0 else in_ref.at[:, span]
        return pltpu.make_async_copy(part, held.at[d], in_sems.at[d])

    places = [(out_ref, d) for out_ref in out_refs for d in range(out_ref.shape[0])]
    puts = [pltpu.make_async_copy(held.at[d], out.at[e], out_sems.at[d]) for d, (out, e) in enumerate(places)]
    for d in range(count):
        bring(d).start()
    for d in range(count):
        bring(d).wait()
        puts[d].start()
    for put in puts:
        put.wait()


def order_blocks(stored, index, deep, along, parts, name, room=LARGE):
    count = index.shape[0]
    shape = (deep, stored.shape[1]) if along == 0 else (stored.shape[0], deep)
    return pl.pallas_call(
        functools.partial(order_body, along),
        in_specs=[pl.BlockSpec(memory_space=pltpu.SMEM), pl.BlockSpec(memory_space=pl.ANY)],
        out_specs=[pl.BlockSpec(memory_space=pl.ANY)] * len(parts),
        out_shape=[jax.ShapeDtypeStruct((part, *shape), jnp.float32) for part in parts],
        scratch_shapes=[
            pltpu.VMEM((count, *shape), jnp.float32),
            pltpu.SemaphoreType.DMA((count,)),
            pltpu.SemaphoreType.DMA((count,)),
        ],
        name=name,
        compiler_params=pltpu.CompilerParams(vmem_limit_bytes=room),
        cost_estimate=pl.CostEstimate(flops=0, bytes_accessed=8 * count * shape[0] * shape[1], transcendentals=0),
    )(index, stored)


def split(value):
    high = value.astype(jnp.bfloat16)
    low = (value - high.astype(jnp.float32)).astype(jnp.bfloat16)
    return high, low


def split_stored_body(index_ref, in_ref, high_ref, low_ref):
    del index_ref
    high_ref[0], low_ref[0] = split(in_ref[...])


def split_stored(a_stored, index, deep):
    count, rows = index.shape[0], a_stored.shape[0]
    out = jax.ShapeDtypeStruct((count, rows, deep), jnp.bfloat16)
    out_spec = pl.BlockSpec((1, rows, deep), lambda g, index: (g, 0, 0))
    return pl.pallas_call(
        split_stored_body,
        grid_spec=pltpu.PrefetchScalarGridSpec(
            num_scalar_prefetch=1,
            grid=(count,),
            in_specs=[pl.BlockSpec((rows, deep), lambda g, index: (0, index[g]))],
            out_specs=[out_spec, out_spec],
        ),
        out_shape=[out, out],
        name="split_stored",
        compiler_params=pltpu.CompilerParams(vmem_limit_bytes=LARGE),
        cost_estimate=pl.CostEstimate(flops=0, bytes_accessed=8 * count * rows * deep, transcendentals=0),
    )(index, a_stored)


def split_blocks_body(cut, one_ref, two_ref, high_ref, low_ref):
    at = pl.program_id(0)

    @pl.when(at < cut)
    def _():
        high_ref[0], low_ref[0] = split(one_ref[0])

    @pl.when(at >= cut)
    def _():
        high_ref[0], low_ref[0] = split(two_ref[0])


def split_blocks(one, two):
    cut, rows, deep = one.shape
    count = cut + two.shape[0]
    out = jax.ShapeDtypeStruct((count, rows, deep), jnp.bfloat16)
    out_spec = pl.BlockSpec((1, rows, deep), lambda g: (g, 0, 0))
    return pl.pallas_call(
        functools.partial(split_blocks_body, cut),
        grid=(count,),
        in_specs=[
            pl.BlockSpec((1, rows, deep), lambda g: (jnp.minimum(g, cut - 1), 0, 0)),
            pl.BlockSpec((1, rows, deep), lambda g: (jnp.maximum(g - cut, 0), 0, 0)),
        ],
        out_specs=[out_spec, out_spec],
        out_shape=[out, out],
        name="split_blocks",
        compiler_params=pltpu.CompilerParams(vmem_limit_bytes=SMALL),
        cost_estimate=pl.CostEstimate(flops=0, bytes_accessed=8 * count * rows * deep, transcendentals=0),
    )(one, two)


def product_body(terms, has_start, around_ref, *refs):
    del around_ref
    out_ref = refs[-1]
    dot = functools.partial(jnp.dot, preferred_element_type=jnp.float32)
    total = refs[3 * terms][0] if has_start else None
    for t in range(terms):
        left_high, left_low, right_ref = refs[3 * t : 3 * t + 3]
        high, low = split(right_ref[0])
        part = dot(left_high[0], high) + (dot(left_high[0], low) + dot(left_low[0], high))
        total = part if total is None else total + part
    out_ref[0] = total


def products(around, a_high, a_low, panels, first, count, start=None):
    deep, cols = panels[0].shape[1:]
    rows = a_high.shape[1]
    ordered = panels[0].shape[0] == count < len(OFFSETS)

    def left_at(s):
        return lambda g, around: (around[first + g] + s, 0, 0)

    def right_at(g, around):
        return (g if ordered else around[first + g], 0, 0)

    in_specs, args = [], []
    for s, panel in enumerate(panels):
        in_specs += [pl.BlockSpec((1, rows, deep), left_at(s))] * 2
        in_specs += [pl.BlockSpec((1, deep, cols), right_at)]
        args += [a_high, a_low, panel]
    if start is not None:
        in_specs += [pl.BlockSpec((1, rows, cols), lambda g, around: (first + g, 0, 0))]
        args += [start]
    blocks = count * len(panels)
    return pl.pallas_call(
        functools.partial(product_body, len(panels), start is not None),
        grid_spec=pltpu.PrefetchScalarGridSpec(
            num_scalar_prefetch=1,
            grid=(count,),
            in_specs=in_specs,
            out_specs=pl.BlockSpec((1, rows, cols), lambda g, around: (g, 0, 0)),
        ),
        out_shape=jax.ShapeDtypeStruct((count, rows, cols), jnp.float32),
        name="products",
        compiler_params=pltpu.CompilerParams(vmem_limit_bytes=SMALL),
        cost_estimate=pl.CostEstimate(
            flops=6 * blocks * rows * deep * cols, bytes_accessed=8 * blocks * deep * cols, transcendentals=0
        ),
    )(around, *args)


def shifted(block, axes, distance):
    n = lax.axis_size(axes)
    return lax.ppermute(block, axes, [((i - distance) % n, i) for i in range(n)])


def exchange(block, axes):
    return lax.all_to_all(block, axes, split_axis=0, concat_axis=0, tiled=True)


def on_device(a_stored, b_stored):
    blocks = lax.axis_size(ROW)
    planes = lax.axis_size("z")
    deep = b_stored.shape[0] // blocks
    row_index = lax.axis_index(ROW).astype(jnp.int32)
    col_index = lax.axis_index(COL).astype(jnp.int32)
    plane = lax.axis_index("z").astype(jnp.int32)
    side = lax.axis_index("y_lo").astype(jnp.int32)
    kinds = jnp.arange(planes + WINDOW - 1, dtype=jnp.int32)
    mine = (row_index + side * planes + kinds) % blocks
    theirs = (row_index + (1 - side) * planes + kinds) % blocks
    around = (plane + jnp.array(OFFSETS, dtype=jnp.int32)) % planes
    order = (jnp.arange(blocks, dtype=jnp.int32) + col_index + 1) % blocks
    (panel,) = order_blocks(b_stored, order, deep, 0, (blocks,), "order_panel")
    panel = exchange(panel, ROW).reshape(2, planes, deep, panel.shape[2])

    one = lax.dynamic_index_in_dim(panel, side, 0, keepdims=False)
    theirs, one = lax.optimization_barrier((theirs, one))
    panel, _ = lax.optimization_barrier((panel, one))
    two = lax.dynamic_index_in_dim(panel, 1 - side, 0, keepdims=False)
    early, late = order_blocks(a_stored, theirs, deep, 1, (EARLY, planes + WINDOW - 1 - EARLY), "order_slab")
    early = shifted(early, "y_lo", 1)
    a_own = split_stored(a_stored, mine, deep)
    one = exchange(one, "z")
    two, one, early, late, *a_own = lax.optimization_barrier((two, one, early, late, *a_own))
    late = shifted(late, "y_lo", 1)
    one_before, one_after = shifted(one, ROW, 1), shifted(one, ROW, -1)
    two = exchange(two, "z")
    a_other = split_blocks(early, late)
    total = products(around, *a_own, [one_before, one, one_after], 0, planes)

    two, total, *a_other = lax.optimization_barrier((two, total, *a_other))
    groups = order_blocks(two.reshape(-1, two.shape[2]), around, deep, 0, GROUPS, "order_rest", SMALL)
    rest = [[shifted(group, ROW, 1), group, shifted(group, ROW, -1)] for group in groups]
    first, done = 0, []
    for group, count in zip(rest, GROUPS):
        done.append(products(around, *a_other, group, first, count, total))
        first += count
    far, mid, near = done
    ahead = shifted(far[0], "z", 1)
    behind = shifted(far[1], "z", -1)
    ahead = shifted(mid[0] + ahead, "z", 1)
    behind = shifted(mid[1] + behind, "z", -1)
    ahead = shifted(near[0] + ahead, "z", 1)
    behind = shifted(near[1] + behind, "z", -1)
    ahead = shifted(near[2] + ahead, "z", 1)
    return (near[3] + behind) + ahead


def solution(mesh):
    split_mesh = Mesh(np.array(mesh.devices).reshape(2, 4, 2, 2, 8), AXES)
    return jax.shard_map(
        on_device,
        mesh=split_mesh,
        in_specs=(P(ROW, COL), P(ROW, COL)),
        out_specs=P(ROW, COL),
        check_vma=False,
    )
```

time: 439 us -> 256 us (0.58)
  the two profiles are of different devices: /device:TPU:6 before, /device:TPU:8 now
where the time goes in v2:
time: 256 us; the launch traced here: 255 us
  waiting for transfers between devices  171 us (67%)
  starting transfers between devices  41.9 us (16%)
  Pallas kernels  30.8 us (12%)
  local copies, waits for them, and re-layouts  9.12 us (4%)
    ppermute x17, waiting for transfers between devices, shifted(): lax.ppermute(block, axes, [((i - distance) % n, i) for i in range(n)])  109 us
    all_to_all x3, waiting for transfers between devices, exchange(): return lax.all_to_all(block, axes, split_axis=0, concat_axis=0, tiled=True)  62 us
    ppermute x17, starting transfers between devices, shifted(): lax.ppermute(block, axes, [((i - distance) % n, i) for i in range(n)])  22.8 us
    all_to_all x3, starting transfers between devices, exchange(): return lax.all_to_all(block, axes, split_axis=0, concat_axis=0, tiled=True)  19.1 us
    pallas_call x4, Pallas kernels, products(): pl.pallas_call(functools.partial(product_body, len(panels), start is not...  12.6 us
    pallas_call x3, Pallas kernels, order_blocks(): pl.pallas_call(functools.partial(order_body, along), in_specs=[pl.BlockSp...  10.1 us
    pallas_call x1, Pallas kernels, split_stored(): pl.pallas_call(split_stored_body, grid_spec=pltpu.PrefetchScalarGridSpec(...  7.45 us
  transfers between devices with their start and end apart: 20, of which 11 were waited for; matrix products, arithmetic and copies ran while one was open for 1% of the time, Pallas kernels for 9%

profile of v2, /device:TPU:8, one launch (start us, length us, event | category | flops | bytes accessed | tf_op | source)
XLA Modules:
  0.0 255.4 jit_solution(11919036299328115493)
XLA Ops:
  0.0 0.5 and_select_fusion.2.index_ref
  0.5 4.5 %order_panel.1 = f32[16,256,256]{2,1,0:T(8,128)} custom-call(s32[16]{0:T(128)} %and_select_fusion.2.index_ref, f32[4096,256]{1,0:T(8,128)} %in_ref.3), custom_call_target="tpu_custom_call" | custom-call | bytes 8388608 | tf_op jit(solution)/shard_map/order_panel/pallas_call | solution.py:45
  5.1 6.2 %all-to-all-start = ((f32[16,256,256]{2,1,0:T(8,128)}), f32[16,256,256]{2,1,0:T(8,128)}, u32[]{:S(2)}, u32[]{:S(2)}) async-start(f32[16,256,256]{2,1,0:T(8,128)} %order_panel.1), calls=%async_computation | async-start | bytes 8388608 | tf_op jit(solution)/shard_map/all_to_all | solution.py:179
  11.3 0.6 and_select_fusion
  11.8 55.8 %all-to-all-done = f32[16,256,256]{2,1,0:T(8,128)} async-done(((f32[16,256,256]{2,1,0:T(8,128)}), f32[16,256,256]{2,1,0:T(8,128)}, u32[]{:S(2)}, u32[]{:S(2)}) %all-to-all-start) | async-done | bytes 4194336 | tf_op jit(solution)/shard_map/all_to_all | solution.py:179
  67.6 3.1 %dynamic-slice_bitcast_fusion.1 = f32[8,256,256]{2,1,0:T(8,128)} fusion(f32[2,8,256,256]{3,2,1,0:T(8,128)} %bitcast, s32[]{:T(128)S(6)} %select_n.33), kind=kLoop, calls=%fused_computation.1 | loop fusion | bytes 4194308 | tf_op jit(solution)/shard_map/jit(dynamic_index_in_dim)/squeeze | solution.py:198
  70.7 8.5 %all-to-all-start.1 = ((f32[8,256,256]{2,1,0:T(8,128)}), f32[8,256,256]{2,1,0:T(8,128)}, u32[]{:S(2)}, u32[]{:S(2)}) async-start(f32[8,256,256]{2,1,0:T(8,128)} %dynamic-slice_bitcast_fusion.1), calls=%async_computation.1 | async-start | bytes 4194304 | tf_op jit(solution)/shard_map/all_to_all | solution.py:179
  79.2 3.3 %order_slab.1 = (f32[7,256,256]{2,1,0:T(8,128)}, f32[3,256,256]{2,1,0:T(8,128)}) custom-call(s32[10]{0:T(128)} %get-tuple-element.29.index_ref, f32[256,4096]{1,0:T(8,128)} %in_ref.5), custom_call_target="tpu_custom_call" | custom-call | bytes 5242880 | tf_op jit(solution)/shard_map/order_slab/pallas_call | solution.py:45
  82.5 1.4 collective-permute-start
  83.9 7.5 %split_stored.1 = (bf16[10,256,256]{2,1,0:T(8,128)(2,1)}, bf16[10,256,256]{2,1,0:T(8,128)(2,1)}) custom-call(s32[10]{0:T(128)} %get-tuple-element.55.index_ref, f32[256,4096]{1,0:T(8,128)} %in_ref.5), custom_call_target="tpu_custom_call" | custom-call | bytes 5242880 | tf_op jit(solution)/shard_map/split_stored/pallas_call | solution.py:76
  91.4 3.1 %dynamic-slice_bitcast_fusion = f32[8,256,256]{2,1,0:T(8,128)} fusion(f32[2,8,256,256]{3,2,1,0:T(8,128)} %bitcast, s32[]{:T(128)S(6)} %select_n.34), kind=kLoop, calls=%fused_computation | loop fusion | bytes 4194308 | tf_op jit(solution)/shard_map/jit(dynamic_index_in_dim)/squeeze | solution.py:201
  94.5 29.9 %collective-permute-done.one_ref = f32[7,256,256]{2,1,0:T(8,128)S(1)} collective-permute-done((f32[7,256,256]{2,1,0:T(8,128)}, f32[7,256,256]{2,1,0:T(8,128)S(1)}, u32[]{:S(2)}, u32[]{:S(2)}) %collective-permute-start) | collective-permute-done | bytes 1835040 | tf_op jit(solution)/shard_map/ppermute | solution.py:175
  124.3 6.3 %all-to-all-done.1.refs_5_ = f32[8,256,256]{2,1,0:T(8,128)} async-done(((f32[8,256,256]{2,1,0:T(8,128)}), f32[8,256,256]{2,1,0:T(8,128)}, u32[]{:S(2)}, u32[]{:S(2)}) %all-to-all-start.1) | async-done | bytes 2097184 | tf_op jit(solution)/shard_map/all_to_all | solution.py:179
  130.6 4.5 %all-to-all-start.2 = ((f32[8,256,256]{2,1,0:T(8,128)}), f32[8,256,256]{2,1,0:T(8,128)}, u32[]{:S(2)}, u32[]{:S(2)}) async-start(f32[8,256,256]{2,1,0:T(8,128)} %dynamic-slice_bitcast_fusion), calls=%async_computation.2 | async-start | bytes 4194304 | tf_op jit(solution)/shard_map/all_to_all | solution.py:179
  135.1 0.1 collective-permute-start.2
  135.2 0.5 collective-permute-start.1
  135.7 1.3 collective-permute-start.3
  137.1 40.3 %collective-permute-done.3.two_ref = f32[3,256,256]{2,1,0:T(8,128)S(1)} collective-permute-done((f32[3,256,256]{2,1,0:T(8,128)S(1)}, f32[3,256,256]{2,1,0:T(8,128)S(1)}, u32[]{:S(2)}, u32[]{:S(2)}) %collective-permute-start.3) | collective-permute-done | bytes 786464 | tf_op jit(solution)/shard_map/ppermute | solution.py:175
  177.4 1.5 copy-done.5
  178.9 0.6 split_blocks.1
  179.5 0.0 collective-permute-done.2.refs_8_
  179.5 0.0 collective-permute-done.1.refs_2_
  179.5 6.9 %products.4.refs_9_ = f32[8,256,256]{2,1,0:T(8,128)S(1)} custom-call(s32[8]{0:T(128)S(1)} %and_select_fusion.3.around_ref.index_ref, bf16[10,256,256]{2,1,0:T(8,128)(2,1)S(1)} %copy-done.2, bf16[10,256,256]{2,1,0:T(8,128)(2,1)S(1)} %copy-done.3, f32[8,256,256]{2,1,0:T(8,128)S(1)} %collective-permute-done.1.refs_2_, bf16[10,256,256]{2,1,0:T(8,128)(2,1)S(1)} %copy-done.2, ...), custom_call_target="tpu_custom_call" | custom-call | flops 2415919104 | bytes 12582912 | tf_op jit(solution)/shard_map/products/pallas_call | solution.py:156
  186.5 1.3 copy-done
  187.8 2.3 order_rest.1
  190.1 3.8 %collective-permute-start.9 = (f32[2,256,256]{2,1,0:T(8,128)S(1)}, f32[2,256,256]{2,1,0:T(8,128)S(1)}, u32[]{:S(2)}, u32[]{:S(2)}) collective-permute-start(f32[2,256,256]{2,1,0:T(8,128)S(1)} %get-tuple-element.48.refs_5_), channel_id=1, source_target_pairs={{16,0},{32,16},{48,32},{64,48},{80,64},{96,80},{112,96},{128,112},... | collective-permute-start | bytes 1572872 | tf_op jit(solution)/shard_map/ppermute | solution.py:175
  193.9 5.4 %collective-permute-start.7 = (f32[2,256,256]{2,1,0:T(8,128)S(1)}, f32[2,256,256]{2,1,0:T(8,128)S(1)}, u32[]{:S(2)}, u32[]{:S(2)}) collective-permute-start(f32[2,256,256]{2,1,0:T(8,128)S(1)} %get-tuple-element.47.refs_5_), channel_id=1, source_target_pairs={{16,0},{32,16},{48,32},{64,48},{80,64},{96,80},{112,96},{128,112},... | collective-permute-start | bytes 1572872 | tf_op jit(solution)/shard_map/ppermute | solution.py:175
  199.2 0.0 collective-permute-start.5
  199.2 0.5 collective-permute-start.4
  199.7 0.8 collective-permute-done.9.refs_8_
  200.6 5.5 %collective-permute-done.8.refs_2_ = f32[2,256,256]{2,1,0:T(8,128)S(1)} collective-permute-done((f32[2,256,256]{2,1,0:T(8,128)S(1)}, f32[2,256,256]{2,1,0:T(8,128)S(1)}, u32[]{:S(2)}, u32[]{:S(2)}) %collective-permute-start.8) | collective-permute-done | bytes 524320 | tf_op jit(solution)/shard_map/ppermute | solution.py:175
  206.1 1.6 products.7
  207.7 3.1 %collective-permute-start.10 = (f32[256,256]{1,0:T(8,128)S(1)}, f32[256,256]{1,0:T(8,128)S(1)}, u32[]{:S(2)}, u32[]{:S(2)}) collective-permute-start(f32[256,256]{1,0:T(8,128)S(1)} %get-tuple-element.53), channel_id=1, source_target_pairs={{1,0},{2,1},{3,2},{4,3},{5,4},{6,5},{7,6},{0,7},{9,8},{10,9},{11,1... | collective-permute-start | bytes 786440 | tf_op jit(solution)/shard_map/ppermute | solution.py:175
  210.8 12.1 %collective-permute-done.6.refs_2_ = f32[2,256,256]{2,1,0:T(8,128)S(1)} collective-permute-done((f32[2,256,256]{2,1,0:T(8,128)S(1)}, f32[2,256,256]{2,1,0:T(8,128)S(1)}, u32[]{:S(2)}, u32[]{:S(2)}) %collective-permute-start.6) | collective-permute-done | bytes 524320 | tf_op jit(solution)/shard_map/ppermute | solution.py:175
  222.9 1.6 products.6
  224.5 0.0 collective-permute-done.13
  224.5 0.1 fusion.3
  224.6 3.3 %collective-permute-start.11 = (f32[256,256]{1,0:T(8,128)S(1)}, f32[256,256]{1,0:T(8,128)S(1)}, u32[]{:S(2)}, u32[]{:S(2)}) collective-permute-start(f32[256,256]{1,0:T(8,128)S(1)} %get-tuple-element.51), channel_id=1, source_target_pairs={{1,0},{2,1},{3,2},{4,3},{5,4},{6,5},{7,6},{0,7},{9,8},{10,9},{11,1... | collective-permute-start | bytes 786440 | tf_op jit(solution)/shard_map/ppermute | solution.py:175
  227.9 2.6 %products.5 = f32[4,256,256]{2,1,0:T(8,128)S(1)} custom-call(s32[8]{0:T(128)S(1)} %and_select_fusion.3.around_ref.index_ref, bf16[10,256,256]{2,1,0:T(8,128)(2,1)S(1)} %get-tuple-element.42.refs_0_.refs_3_.refs_6_, bf16[10,256,256]{2,1,0:T(8,128)(2,1)S(1)} %get-tuple-element.43.refs_1_.refs_4_.refs_7_, f32[4,256,256]{2,1,0:T(8,128)S(1)} %collective-permute-done.4.refs_2_, ...), custom_call_target="tpu_custom_call" | custom-call | flops 1207959552 | bytes 6291456 | tf_op jit(solution)/shard_map/products/pallas_call | solution.py:156
  230.5 1.6 collective-permute-done.11
  232.1 5.7 %collective-permute-done.14 = f32[256,256]{1,0:T(8,128)S(1)} collective-permute-done((f32[256,256]{1,0:T(8,128)S(1)}, f32[256,256]{1,0:T(8,128)S(1)}, u32[]{:S(2)}, u32[]{:S(2)}) %collective-permute-start.14) | collective-permute-done | bytes 262176 | tf_op jit(solution)/shard_map/ppermute | solution.py:175
  237.8 0.1 fusion.4
  237.8 0.1 collective-permute-start.15
  237.9 3.2 %collective-permute-start.12 = (f32[256,256]{1,0:T(8,128)S(1)}, f32[256,256]{1,0:T(8,128)S(1)}, u32[]{:S(2)}, u32[]{:S(2)}) collective-permute-start(f32[256,256]{1,0:T(8,128)S(1)} %get-tuple-element.49), channel_id=1, source_target_pairs={{1,0},{2,1},{3,2},{4,3},{5,4},{6,5},{7,6},{0,7},{9,8},{10,9},{11,1... | collective-permute-start | bytes 786440 | tf_op jit(solution)/shard_map/ppermute | solution.py:175
  241.2 5.8 %collective-permute-done.15 = f32[256,256]{1,0:T(8,128)S(1)} collective-permute-done((f32[256,256]{1,0:T(8,128)S(1)}, f32[256,256]{1,0:T(8,128)S(1)}, u32[]{:S(2)}, u32[]{:S(2)}) %collective-permute-start.15) | collective-permute-done | bytes 262176 | tf_op jit(solution)/shard_map/ppermute | solution.py:175
  247.0 0.1 collective-permute-start.16
  247.1 7.6 %collective-permute-done.16 = f32[256,256]{1,0:T(8,128)S(1)} collective-permute-done((f32[256,256]{1,0:T(8,128)S(1)}, f32[256,256]{1,0:T(8,128)S(1)}, u32[]{:S(2)}, u32[]{:S(2)}) %collective-permute-start.16) | collective-permute-done | bytes 262176 | tf_op jit(solution)/shard_map/ppermute | solution.py:175
  254.7 0.8 fusion.6
  (27 shorter events, 0.1 us)
Async XLA Ops:
  5.1 62.6 %all-to-all-start = ((f32[16,256,256]{2,1,0:T(8,128)}), f32[16,256,256]{2,1,0:T(8,128)}, u32[]{:S(2)}, u32[]{:S(2)}) async-start(f32[16,256,256]{2,1,0:T(8,128)} %order_panel.1), calls=%async_computation | async-start | bytes 8388608 | tf_op jit(solution)/shard_map/all_to_all | solution.py:179
  70.7 59.9 %all-to-all-start.1 = ((f32[8,256,256]{2,1,0:T(8,128)}), f32[8,256,256]{2,1,0:T(8,128)}, u32[]{:S(2)}, u32[]{:S(2)}) async-start(f32[8,256,256]{2,1,0:T(8,128)} %dynamic-slice_bitcast_fusion.1), calls=%async_computation.1 | async-start | bytes 4194304 | tf_op jit(solution)/shard_map/all_to_all | solution.py:179
  82.5 41.9 %collective-permute-start = (f32[7,256,256]{2,1,0:T(8,128)}, f32[7,256,256]{2,1,0:T(8,128)S(1)}, u32[]{:S(2)}, u32[]{:S(2)}) collective-permute-start(f32[7,256,256]{2,1,0:T(8,128)} %get-tuple-element.30), channel_id=1, source_target_pairs={{8,0},{0,8},{9,1},{1,9},{10,2},{2,10},{11,3},{3,11},{12,4},{4,12},... | collective-permute-start | bytes 5505032 | tf_op jit(solution)/shard_map/ppermute | solution.py:175
  124.3 6.3 %copy-start.4 = (f32[7,256,256]{2,1,0:T(8,128)}, f32[7,256,256]{2,1,0:T(8,128)S(1)}, u32[]{:S(2)}) copy-start(f32[7,256,256]{2,1,0:T(8,128)S(1)} %collective-permute-done.one_ref) | copy-start | bytes 5505028
  130.6 5.1 %copy-start.6 = (f32[3,256,256]{2,1,0:T(8,128)S(1)}, f32[3,256,256]{2,1,0:T(8,128)}, u32[]{:S(2)}) copy-start(f32[3,256,256]{2,1,0:T(8,128)} %get-tuple-element.39) | copy-start | bytes 2359300
  130.6 6.5 %copy-start.7 = (s32[8]{0:T(128)S(1)}, s32[8]{0:T(128)}, u32[]{:S(2)}) copy-start(s32[8]{0:T(128)} %constant.78.clone) | copy-start | bytes 100
  130.6 57.2 %all-to-all-start.2 = ((f32[8,256,256]{2,1,0:T(8,128)}), f32[8,256,256]{2,1,0:T(8,128)}, u32[]{:S(2)}, u32[]{:S(2)}) async-start(f32[8,256,256]{2,1,0:T(8,128)} %dynamic-slice_bitcast_fusion), calls=%async_computation.2 | async-start | bytes 4194304 | tf_op jit(solution)/shard_map/all_to_all | solution.py:179
  135.1 44.4 %copy-start.2 = (bf16[10,256,256]{2,1,0:T(8,128)(2,1)S(1)}, bf16[10,256,256]{2,1,0:T(8,128)(2,1)}, u32[]{:S(2)}) copy-start(bf16[10,256,256]{2,1,0:T(8,128)(2,1)} %get-tuple-element.35.refs_0_.refs_3_.refs_6_) | copy-start | bytes 3932164
  135.1 44.4 %copy-start.3 = (bf16[10,256,256]{2,1,0:T(8,128)(2,1)S(1)}, bf16[10,256,256]{2,1,0:T(8,128)(2,1)}, u32[]{:S(2)}) copy-start(bf16[10,256,256]{2,1,0:T(8,128)(2,1)} %get-tuple-element.36.refs_1_.refs_4_.refs_7_) | copy-start | bytes 3932164
  135.1 44.4 %collective-permute-start.2 = (f32[8,256,256]{2,1,0:T(8,128)}, f32[8,256,256]{2,1,0:T(8,128)S(1)}, u32[]{:S(2)}, u32[]{:S(2)}) collective-permute-start(f32[8,256,256]{2,1,0:T(8,128)} %all-to-all-done.1.refs_5_), channel_id=1, source_target_pairs={{16,0},{32,16},{48,32},{64,48},{80,64},{96,80},{112,96},{128,112},... | collective-permute-start | bytes 6291464 | tf_op jit(solution)/shard_map/ppermute | solution.py:175
  135.2 44.3 %collective-permute-start.1 = (f32[8,256,256]{2,1,0:T(8,128)}, f32[8,256,256]{2,1,0:T(8,128)S(1)}, u32[]{:S(2)}, u32[]{:S(2)}) collective-permute-start(f32[8,256,256]{2,1,0:T(8,128)} %all-to-all-done.1.refs_5_), channel_id=1, source_target_pairs={{240,0},{0,16},{16,32},{32,48},{48,64},{64,80},{80,96},{96,112},{1... | collective-permute-start | bytes 6291464 | tf_op jit(solution)/shard_map/ppermute | solution.py:175
  135.7 41.7 %collective-permute-start.3 = (f32[3,256,256]{2,1,0:T(8,128)S(1)}, f32[3,256,256]{2,1,0:T(8,128)S(1)}, u32[]{:S(2)}, u32[]{:S(2)}) collective-permute-start(f32[3,256,256]{2,1,0:T(8,128)S(1)} %copy-done.6), channel_id=1, source_target_pairs={{8,0},{0,8},{9,1},{1,9},{10,2},{2,10},{11,3},{3,11},{12,4},{4,12},... | collective-permute-start | bytes 2359304 | tf_op jit(solution)/shard_map/ppermute | solution.py:175
  177.4 1.5 copy-start.5
  186.4 1.3 copy-start
  187.8 18.3 %copy-start.1 = (f32[8,256,256]{2,1,0:T(8,128)S(1)}, f32[8,256,256]{2,1,0:T(8,128)}, u32[]{:S(2)}) copy-start(f32[8,256,256]{2,1,0:T(8,128)} %copy-done) | copy-start | bytes 6291460
  190.1 10.5 %collective-permute-start.9 = (f32[2,256,256]{2,1,0:T(8,128)S(1)}, f32[2,256,256]{2,1,0:T(8,128)S(1)}, u32[]{:S(2)}, u32[]{:S(2)}) collective-permute-start(f32[2,256,256]{2,1,0:T(8,128)S(1)} %get-tuple-element.48.refs_5_), channel_id=1, source_target_pairs={{16,0},{32,16},{48,32},{64,48},{80,64},{96,80},{112,96},{128,112},... | collective-permute-start | bytes 1572872 | tf_op jit(solution)/shard_map/ppermute | solution.py:175
  193.8 12.2 %collective-permute-start.8 = (f32[2,256,256]{2,1,0:T(8,128)S(1)}, f32[2,256,256]{2,1,0:T(8,128)S(1)}, u32[]{:S(2)}, u32[]{:S(2)}) collective-permute-start(f32[2,256,256]{2,1,0:T(8,128)S(1)} %get-tuple-element.48.refs_5_), channel_id=1, source_target_pairs={{240,0},{0,16},{16,32},{32,48},{48,64},{64,80},{80,96},{96,112},{1... | collective-permute-start | bytes 1572872 | tf_op jit(solution)/shard_map/ppermute | solution.py:175
  193.9 16.9 %collective-permute-start.7 = (f32[2,256,256]{2,1,0:T(8,128)S(1)}, f32[2,256,256]{2,1,0:T(8,128)S(1)}, u32[]{:S(2)}, u32[]{:S(2)}) collective-permute-start(f32[2,256,256]{2,1,0:T(8,128)S(1)} %get-tuple-element.47.refs_5_), channel_id=1, source_target_pairs={{16,0},{32,16},{48,32},{64,48},{80,64},{96,80},{112,96},{128,112},... | collective-permute-start | bytes 1572872 | tf_op jit(solution)/shard_map/ppermute | solution.py:175
  199.2 28.7 %collective-permute-start.5 = (f32[4,256,256]{2,1,0:T(8,128)S(1)}, f32[4,256,256]{2,1,0:T(8,128)S(1)}, u32[]{:S(2)}, u32[]{:S(2)}) collective-permute-start(f32[4,256,256]{2,1,0:T(8,128)S(1)} %get-tuple-element.45.refs_5_), channel_id=1, source_target_pairs={{16,0},{32,16},{48,32},{64,48},{80,64},{96,80},{112,96},{128,112},... | collective-permute-start | bytes 3145736 | tf_op jit(solution)/shard_map/ppermute | solution.py:175
  199.2 28.6 %collective-permute-start.4 = (f32[4,256,256]{2,1,0:T(8,128)S(1)}, f32[4,256,256]{2,1,0:T(8,128)S(1)}, u32[]{:S(2)}, u32[]{:S(2)}) collective-permute-start(f32[4,256,256]{2,1,0:T(8,128)S(1)} %get-tuple-element.45.refs_5_), channel_id=1, source_target_pairs={{240,0},{0,16},{16,32},{32,48},{48,64},{64,80},{80,96},{96,112},{1... | collective-permute-start | bytes 3145736 | tf_op jit(solution)/shard_map/ppermute | solution.py:175
  200.6 22.4 %collective-permute-start.6 = (f32[2,256,256]{2,1,0:T(8,128)S(1)}, f32[2,256,256]{2,1,0:T(8,128)S(1)}, u32[]{:S(2)}, u32[]{:S(2)}) collective-permute-start(f32[2,256,256]{2,1,0:T(8,128)S(1)} %get-tuple-element.47.refs_5_), channel_id=1, source_target_pairs={{240,0},{0,16},{16,32},{32,48},{48,64},{64,80},{80,96},{96,112},{1... | collective-permute-start | bytes 1572872 | tf_op jit(solution)/shard_map/ppermute | solution.py:175
  207.7 16.8 %collective-permute-start.10 = (f32[256,256]{1,0:T(8,128)S(1)}, f32[256,256]{1,0:T(8,128)S(1)}, u32[]{:S(2)}, u32[]{:S(2)}) collective-permute-start(f32[256,256]{1,0:T(8,128)S(1)} %get-tuple-element.53), channel_id=1, source_target_pairs={{1,0},{2,1},{3,2},{4,3},{5,4},{6,5},{7,6},{0,7},{9,8},{10,9},{11,1... | collective-permute-start | bytes 786440 | tf_op jit(solution)/shard_map/ppermute | solution.py:175
  210.8 13.7 %collective-permute-start.13 = (f32[256,256]{1,0:T(8,128)S(1)}, f32[256,256]{1,0:T(8,128)S(1)}, u32[]{:S(2)}, u32[]{:S(2)}) collective-permute-start(f32[256,256]{1,0:T(8,128)S(1)} %get-tuple-element.54), channel_id=1, source_target_pairs={{7,0},{0,1},{1,2},{2,3},{3,4},{4,5},{5,6},{6,7},{15,8},{8,9},{9,10... | collective-permute-start | bytes 786440 | tf_op jit(solution)/shard_map/ppermute | solution.py:175
  224.6 7.5 %collective-permute-start.11 = (f32[256,256]{1,0:T(8,128)S(1)}, f32[256,256]{1,0:T(8,128)S(1)}, u32[]{:S(2)}, u32[]{:S(2)}) collective-permute-start(f32[256,256]{1,0:T(8,128)S(1)} %get-tuple-element.51), channel_id=1, source_target_pairs={{1,0},{2,1},{3,2},{4,3},{5,4},{6,5},{7,6},{0,7},{9,8},{10,9},{11,1... | collective-permute-start | bytes 786440 | tf_op jit(solution)/shard_map/ppermute | solution.py:175
  227.9 9.9 %collective-permute-start.14 = (f32[256,256]{1,0:T(8,128)S(1)}, f32[256,256]{1,0:T(8,128)S(1)}, u32[]{:S(2)}, u32[]{:S(2)}) collective-permute-start(f32[256,256]{1,0:T(8,128)S(1)} %get-tuple-element.52), channel_id=1, source_target_pairs={{7,0},{0,1},{1,2},{2,3},{3,4},{4,5},{5,6},{6,7},{15,8},{8,9},{9,10... | collective-permute-start | bytes 786440 | tf_op jit(solution)/shard_map/ppermute | solution.py:175
  237.8 9.1 %collective-permute-start.15 = (f32[256,256]{1,0:T(8,128)S(1)}, f32[256,256]{1,0:T(8,128)S(1)}, u32[]{:S(2)}, u32[]{:S(2)}) collective-permute-start(f32[256,256]{1,0:T(8,128)S(1)} %get-tuple-element.50), channel_id=1, source_target_pairs={{7,0},{0,1},{1,2},{2,3},{3,4},{4,5},{5,6},{6,7},{15,8},{8,9},{9,10... | collective-permute-start | bytes 786440 | tf_op jit(solution)/shard_map/ppermute | solution.py:175
  237.9 9.2 %collective-permute-start.12 = (f32[256,256]{1,0:T(8,128)S(1)}, f32[256,256]{1,0:T(8,128)S(1)}, u32[]{:S(2)}, u32[]{:S(2)}) collective-permute-start(f32[256,256]{1,0:T(8,128)S(1)} %get-tuple-element.49), channel_id=1, source_target_pairs={{1,0},{2,1},{3,2},{4,3},{5,4},{6,5},{7,6},{0,7},{9,8},{10,9},{11,1... | collective-permute-start | bytes 786440 | tf_op jit(solution)/shard_map/ppermute | solution.py:175
  247.0 7.7 %collective-permute-start.16 = (f32[256,256]{1,0:T(8,128)S(1)}, f32[256,256]{1,0:T(8,128)S(1)}, u32[]{:S(2)}, u32[]{:S(2)}) collective-permute-start(f32[256,256]{1,0:T(8,128)S(1)} %fusion.2), channel_id=1, source_target_pairs={{7,0},{0,1},{1,2},{2,3},{3,4},{4,5},{5,6},{6,7},{15,8},{8,9},{9,10... | collective-permute-start | bytes 786440 | tf_op jit(solution)/shard_map/ppermute | solution.py:175

commit v3 on v2

--- a/solution.py
+++ b/solution.py
@@ -14,7 +14,7 @@
 WINDOW = 3
 OFFSETS = (4, -3, 3, -2, 2, -1, 1, 0)
 GROUPS = (2, 2, 4)
-EARLY = 7
+EARLY = 2
 LARGE = 60 * 2**20
 SMALL = 16 * 2**20
 
@@ -120,46 +120,59 @@
     )(one, two)
 
 
-def product_body(terms, has_start, around_ref, *refs):
-    del around_ref
+def product_body(cut, first, ordered, has_start, place_ref, *refs):
     out_ref = refs[-1]
+    at = pl.program_id(0)
+    at = at if ordered else place_ref[first + at]
     dot = functools.partial(jnp.dot, preferred_element_type=jnp.float32)
-    total = refs[3 * terms][0] if has_start else None
-    for t in range(terms):
-        left_high, left_low, right_ref = refs[3 * t : 3 * t + 3]
-        high, low = split(right_ref[0])
+    own_ref, other_ref, one_ref, two_ref = refs[:4]
+    rights = [own_ref[0], other_ref[0], jnp.where(at < cut, one_ref[0], two_ref[0])]
+    total = refs[10][0] if has_start else None
+    for t, right in enumerate(rights):
+        left_high, left_low = refs[4 + 2 * t : 6 + 2 * t]
+        high, low = split(right)
         part = dot(left_high[0], high) + (dot(left_high[0], low) + dot(left_low[0], high))
         total = part if total is None else total + part
     out_ref[0] = total
 
 
-def products(around, a_high, a_low, panels, first, count, start=None):
-    deep, cols = panels[0].shape[1:]
-    rows = a_high.shape[1]
-    ordered = panels[0].shape[0] == count < len(OFFSETS)
-
-    def left_at(s):
-        return lambda g, around: (around[first + g] + s, 0, 0)
-
-    def right_at(g, around):
-        return (g if ordered else around[first + g], 0, 0)
-
-    in_specs, args = [], []
-    for s, panel in enumerate(panels):
-        in_specs += [pl.BlockSpec((1, rows, deep), left_at(s))] * 2
-        in_specs += [pl.BlockSpec((1, deep, cols), right_at)]
-        args += [a_high, a_low, panel]
+def products(place, a_high, a_low, panels, first, count, base=None, start=None):
+    own, other, one, two = panels
+    deep, cols = own.shape[1:]
+    rows, cut = a_high.shape[1], one.shape[0]
+    ordered = base is not None
+
+    def left_at(term):
+        return lambda g, place: (place[first + g] + place[len(OFFSETS) + term], 0, 0)
+
+    def right_at(offset, low, high):
+        def at(g, place):
+            index = g + offset if ordered else place[first + g]
+            return (jnp.clip(index - low, 0, high - 1), 0, 0)
+
+        return at
+
+    block = (1, deep, cols)
+    in_specs = [
+        pl.BlockSpec(block, right_at(base or 0, 0, own.shape[0])),
+        pl.BlockSpec(block, right_at(base or 0, 0, other.shape[0])),
+        pl.BlockSpec(block, right_at(0, 0, cut)),
+        pl.BlockSpec(block, right_at(0, cut, two.shape[0])),
+    ]
+    for term in range(WINDOW):
+        in_specs += [pl.BlockSpec((1, rows, deep), left_at(term))] * 2
+    args = [own, other, one, two] + [a_high, a_low] * WINDOW
     if start is not None:
-        in_specs += [pl.BlockSpec((1, rows, cols), lambda g, around: (first + g, 0, 0))]
+        in_specs += [pl.BlockSpec((1, rows, cols), lambda g, place: (first + g, 0, 0))]
         args += [start]
-    blocks = count * len(panels)
-    return pl.pallas_call(
-        functools.partial(product_body, len(panels), start is not None),
+    blocks = count * WINDOW
+    return pl.pallas_call(
+        functools.partial(product_body, cut, first, ordered, start is not None),
         grid_spec=pltpu.PrefetchScalarGridSpec(
             num_scalar_prefetch=1,
             grid=(count,),
             in_specs=in_specs,
-            out_specs=pl.BlockSpec((1, rows, cols), lambda g, around: (g, 0, 0)),
+            out_specs=pl.BlockSpec((1, rows, cols), lambda g, place: (g, 0, 0)),
         ),
         out_shape=jax.ShapeDtypeStruct((count, rows, cols), jnp.float32),
         name="products",
@@ -167,12 +180,23 @@
         cost_estimate=pl.CostEstimate(
             flops=6 * blocks * rows * deep * cols, bytes_accessed=8 * blocks * deep * cols, transcendentals=0
         ),
-    )(around, *args)
+    )(place, *args)
 
 
 def shifted(block, axes, distance):
     n = lax.axis_size(axes)
     return lax.ppermute(block, axes, [((i - distance) % n, i) for i in range(n)])
+
+
+def to_other_core(block):
+    return lax.ppermute(block, ROW, [(i, i ^ 1) for i in range(lax.axis_size(ROW))])
+
+
+def to_next_chips(own, other):
+    n = lax.axis_size(ROW)
+    one = lax.ppermute(own, ROW, [(i, (i + (1 if i % 2 else -1)) % n) for i in range(n)])
+    two = lax.ppermute(other, ROW, [(i, (i + (-2 if i % 2 else 2)) % n) for i in range(n)])
+    return one, two
 
 
 def exchange(block, axes):
@@ -191,41 +215,46 @@
     mine = (row_index + side * planes + kinds) % blocks
     theirs = (row_index + (1 - side) * planes + kinds) % blocks
     around = (plane + jnp.array(OFFSETS, dtype=jnp.int32)) % planes
+    core = lax.axis_index("core").astype(jnp.int32)
+    place = jnp.concatenate([around, jnp.stack([jnp.ones_like(core), 2 - 2 * core, 2 * core])])
     order = (jnp.arange(blocks, dtype=jnp.int32) + col_index + 1) % blocks
     (panel,) = order_blocks(b_stored, order, deep, 0, (blocks,), "order_panel")
-    panel = exchange(panel, ROW).reshape(2, planes, deep, panel.shape[2])
+    theirs, panel = lax.optimization_barrier((theirs, panel))
+    early, late = order_blocks(a_stored, theirs, deep, 1, (EARLY, planes + WINDOW - 1 - EARLY), "order_slab")
+    early = shifted(early, "y_lo", 1)
+    panel = exchange(panel, ROW)
+    panel, early, late = lax.optimization_barrier((panel, early, late))
+    panel = panel.reshape(2, planes, deep, panel.shape[2])
 
     one = lax.dynamic_index_in_dim(panel, side, 0, keepdims=False)
-    theirs, one = lax.optimization_barrier((theirs, one))
+    late, mine, one = lax.optimization_barrier((late, mine, one))
     panel, _ = lax.optimization_barrier((panel, one))
     two = lax.dynamic_index_in_dim(panel, 1 - side, 0, keepdims=False)
-    early, late = order_blocks(a_stored, theirs, deep, 1, (EARLY, planes + WINDOW - 1 - EARLY), "order_slab")
-    early = shifted(early, "y_lo", 1)
+    late = shifted(late, "y_lo", 1)
     a_own = split_stored(a_stored, mine, deep)
     one = exchange(one, "z")
-    two, one, early, late, *a_own = lax.optimization_barrier((two, one, early, late, *a_own))
-    late = shifted(late, "y_lo", 1)
-    one_before, one_after = shifted(one, ROW, 1), shifted(one, ROW, -1)
+    two, one, late, *a_own = lax.optimization_barrier((two, one, late, *a_own))
+    one_other = to_other_core(one)
+    one_next = to_next_chips(one[: planes // 2], one_other[planes // 2 :])
     two = exchange(two, "z")
     a_other = split_blocks(early, late)
-    total = products(around, *a_own, [one_before, one, one_after], 0, planes)
+    total = products(place, *a_own, [one, one_other, *one_next], 0, planes)
 
     two, total, *a_other = lax.optimization_barrier((two, total, *a_other))
     groups = order_blocks(two.reshape(-1, two.shape[2]), around, deep, 0, GROUPS, "order_rest", SMALL)
-    rest = [[shifted(group, ROW, 1), group, shifted(group, ROW, -1)] for group in groups]
-    first, done = 0, []
-    for group, count in zip(rest, GROUPS):
-        done.append(products(around, *a_other, group, first, count, total))
+    others = [to_other_core(group) for group in groups]
+    done, first = [], 0
+    for own, other, count in zip(groups, others, GROUPS):
+        came = to_next_chips(own[: count // 2], other[count // 2 :])
+        part = products(place, *a_other, [own, other, *came], first, count, 0, total)
+        done += [part[g] for g in range(count)]
         first += count
-    far, mid, near = done
-    ahead = shifted(far[0], "z", 1)
-    behind = shifted(far[1], "z", -1)
-    ahead = shifted(mid[0] + ahead, "z", 1)
-    behind = shifted(mid[1] + behind, "z", -1)
-    ahead = shifted(near[0] + ahead, "z", 1)
-    behind = shifted(near[1] + behind, "z", -1)
-    ahead = shifted(near[2] + ahead, "z", 1)
-    return (near[3] + behind) + ahead
+    ahead, behind = shifted(done[0], "z", 1), shifted(done[1], "z", -1)
+    for far in (2, 4):
+        ahead = shifted(done[far] + ahead, "z", 1)
+        behind = shifted(done[far + 1] + behind, "z", -1)
+    ahead = shifted(done[6] + ahead, "z", 1)
+    return (done[7] + behind) + ahead
 
 
 def solution(mesh):

time: 256 us -> 250 us (0.977)
  waiting for transfers between devices: 171 us -> 154 us
  local copies, waits for them, and re-layouts: 9.12 us -> 15.4 us
  Pallas kernels: 30.8 us -> 35.8 us
    all_to_all x3, waiting for transfers between devices: 62 us -> 9.23 us  [exchange(): return lax.all_to_all(block, axes, split_axis=0, concat_axis=0, tiled=True)]
    ppermute x0 -> x12, waiting for transfers between devices: none -> 36.9 us  [the longest x4 24.4 us: to_next_chips(): lax.ppermute(own, ROW, [(i, (i + (1 if i % 2 else -1)) % n) for i in rang...]
    ppermute x17 -> x9, starting transfers between devices: 22.8 us -> 9.72 us  [shifted(): lax.ppermute(block, axes, [((i - distance) % n, i) for i in range(n)])]
    ppermute x0 -> x12, starting transfers between devices: none -> 13 us  [the longest x4 10.9 us: to_next_chips(): lax.ppermute(own, ROW, [(i, (i + (1 if i % 2 else -1)) % n) for i in rang...]
    pallas_call x1, Pallas kernels: 0.59 us -> 5.24 us  [split_blocks(): pl.pallas_call(functools.partial(split_blocks_body, cut), grid=(count,),...]
    unnamed x16 -> x18, local copies, waits for them, and re-layouts: 2.85 us -> 6.91 us
    ppermute x17 -> x9, waiting for transfers between devices: 109 us -> 107 us  [shifted(): lax.ppermute(block, axes, [((i - distance) % n, i) for i in range(n)])]
  transfers between devices with their start and end apart: 20 -> 24, of which waited for: 11 -> 14; matrix products, arithmetic and copies ran while one was open for 1% -> 2% of each run, Pallas kernels for 9% -> 12%
where the time goes in v3:
time: 250 us; the launch traced here: 249 us
  waiting for transfers between devices  154 us (62%)
  starting transfers between devices  41.8 us (17%)
  Pallas kernels  35.8 us (14%)
  local copies, waits for them, and re-layouts  15.4 us (6%)
    ppermute x9, waiting for transfers between devices, shifted(): lax.ppermute(block, axes, [((i - distance) % n, i) for i in range(n)])  107 us
    ppermute x4, waiting for transfers between devices, to_next_chips(): lax.ppermute(own, ROW, [(i, (i + (1 if i % 2 else -1)) % n) for i in rang...  24.4 us
    all_to_all x3, starting transfers between devices, exchange(): return lax.all_to_all(block, axes, split_axis=0, concat_axis=0, tiled=True)  19 us
    pallas_call x4, Pallas kernels, products(): pl.pallas_call(functools.partial(product_body, cut, first, ordered, start...  13 us
    ppermute x4, waiting for transfers between devices, to_next_chips(): lax.ppermute(other, ROW, [(i, (i + (-2 if i % 2 else 2)) % n) for i in ra...  12.5 us
    ppermute x4, starting transfers between devices, to_next_chips(): lax.ppermute(own, ROW, [(i, (i + (1 if i % 2 else -1)) % n) for i in rang...  10.9 us
    pallas_call x3, Pallas kernels, order_blocks(): pl.pallas_call(functools.partial(order_body, along), in_specs=[pl.BlockSp...  10.2 us
    ppermute x9, starting transfers between devices, shifted(): lax.ppermute(block, axes, [((i - distance) % n, i) for i in range(n)])  9.72 us
  transfers between devices with their start and end apart: 24, of which 14 were waited for; matrix products, arithmetic and copies ran while one was open for 2% of the time, Pallas kernels for 12%

profile of v3, /device:TPU:8, one launch (start us, length us, event | category | flops | bytes accessed | tf_op | source)
XLA Modules:
  0.0 249.1 jit_solution(7076952348177925882)
XLA Ops:
  0.0 0.5 and_select_fusion.1.index_ref
  0.5 0.6 and_select_fusion
  1.1 4.5 %order_panel.1 = f32[16,256,256]{2,1,0:T(8,128)} custom-call(s32[16]{0:T(128)} %and_select_fusion.1.index_ref, f32[4096,256]{1,0:T(8,128)} %in_ref.3), custom_call_target="tpu_custom_call" | custom-call | bytes 8388608 | tf_op jit(solution)/shard_map/order_panel/pallas_call | solution.py:45
  5.7 6.2 %all-to-all-start = ((f32[16,256,256]{2,1,0:T(8,128)}), f32[16,256,256]{2,1,0:T(8,128)}, u32[]{:S(2)}, u32[]{:S(2)}) async-start(f32[16,256,256]{2,1,0:T(8,128)} %order_panel.1), calls=%async_computation | async-start | bytes 8388608 | tf_op jit(solution)/shard_map/all_to_all | solution.py:203
  11.9 3.3 %order_slab.1 = (f32[2,256,256]{2,1,0:T(8,128)}, f32[8,256,256]{2,1,0:T(8,128)}) custom-call(s32[10]{0:T(128)} %get-tuple-element.33.index_ref, f32[256,4096]{1,0:T(8,128)} %in_ref.5), custom_call_target="tpu_custom_call" | custom-call | bytes 5242880 | tf_op jit(solution)/shard_map/order_slab/pallas_call | solution.py:45
  15.2 1.4 collective-permute-start
  16.7 54.2 %collective-permute-done.one_ref = f32[2,256,256]{2,1,0:T(8,128)S(1)} collective-permute-done((f32[2,256,256]{2,1,0:T(8,128)}, f32[2,256,256]{2,1,0:T(8,128)S(1)}, u32[]{:S(2)}, u32[]{:S(2)}) %collective-permute-start) | collective-permute-done | bytes 524320 | tf_op jit(solution)/shard_map/ppermute | solution.py:188
  70.8 3.1 %dynamic-slice_bitcast_fusion.1 = f32[8,256,256]{2,1,0:T(8,128)} fusion(f32[2,8,256,256]{3,2,1,0:T(8,128)} %bitcast.2, s32[]{:T(128)S(6)} %select_n.34), kind=kLoop, calls=%fused_computation.1 | loop fusion | bytes 4194308 | tf_op jit(solution)/shard_map/jit(dynamic_index_in_dim)/squeeze | solution.py:229
  73.9 8.5 %all-to-all-start.1 = ((f32[8,256,256]{2,1,0:T(8,128)}), f32[8,256,256]{2,1,0:T(8,128)S(1)}, u32[]{:S(2)}, u32[]{:S(2)}) async-start(f32[8,256,256]{2,1,0:T(8,128)} %dynamic-slice_bitcast_fusion.1), calls=%async_computation.1 | async-start | bytes 4194304 | tf_op jit(solution)/shard_map/all_to_all | solution.py:203
  82.4 0.7 collective-permute-start.1
  83.1 7.4 %split_stored.1 = (bf16[10,256,256]{2,1,0:T(8,128)(2,1)}, bf16[10,256,256]{2,1,0:T(8,128)(2,1)}) custom-call(s32[10]{0:T(128)} %get-tuple-element.41.index_ref, f32[256,4096]{1,0:T(8,128)} %in_ref.5), custom_call_target="tpu_custom_call" | custom-call | bytes 5242880 | tf_op jit(solution)/shard_map/split_stored/pallas_call | solution.py:76
  90.5 3.1 %dynamic-slice_bitcast_fusion = f32[8,256,256]{2,1,0:T(8,128)} fusion(f32[2,8,256,256]{3,2,1,0:T(8,128)} %bitcast.2, s32[]{:T(128)S(6)} %select_n.35), kind=kLoop, calls=%fused_computation | loop fusion | bytes 4194308 | tf_op jit(solution)/shard_map/jit(dynamic_index_in_dim)/squeeze | solution.py:232
  93.6 36.3 %collective-permute-done.1.two_ref = f32[8,256,256]{2,1,0:T(8,128)} collective-permute-done((f32[8,256,256]{2,1,0:T(8,128)}, f32[8,256,256]{2,1,0:T(8,128)}, u32[]{:S(2)}, u32[]{:S(2)}) %collective-permute-start.1) | collective-permute-done | bytes 2097184 | tf_op jit(solution)/shard_map/ppermute | solution.py:188
  129.9 3.8 %all-to-all-done.1.refs_0_ = f32[8,256,256]{2,1,0:T(8,128)S(1)} async-done(((f32[8,256,256]{2,1,0:T(8,128)}), f32[8,256,256]{2,1,0:T(8,128)S(1)}, u32[]{:S(2)}, u32[]{:S(2)}) %all-to-all-start.1) | async-done | bytes 2097184 | tf_op jit(solution)/shard_map/all_to_all | solution.py:203
  133.7 4.3 %all-to-all-start.2 = ((f32[8,256,256]{2,1,0:T(8,128)}), f32[8,256,256]{2,1,0:T(8,128)}, u32[]{:S(2)}, u32[]{:S(2)}) async-start(f32[8,256,256]{2,1,0:T(8,128)} %dynamic-slice_bitcast_fusion), calls=%async_computation.2 | async-start | bytes 4194304 | tf_op jit(solution)/shard_map/all_to_all | solution.py:203
  138.2 1.0 slice.48
  139.2 4.5 %collective-permute-start.3 = (f32[4,256,256]{2,1,0:T(8,128)}, f32[4,256,256]{2,1,0:T(8,128)}, u32[]{:S(2)}, u32[]{:S(2)}) collective-permute-start(f32[4,256,256]{2,1,0:T(8,128)} %slice.48), channel_id=1, source_target_pairs={{0,240},{16,32},{32,16},{48,64},{64,48},{80,96},{96,80},{112,128},... | collective-permute-start | bytes 3145736 | tf_op jit(solution)/shard_map/ppermute | solution.py:197
  143.7 1.0 slice.64
  144.8 1.4 copy-done.6
  146.2 5.2 %split_blocks.1 = (bf16[10,256,256]{2,1,0:T(8,128)(2,1)S(1)}, bf16[10,256,256]{2,1,0:T(8,128)(2,1)S(1)}) custom-call(f32[2,256,256]{2,1,0:T(8,128)S(1)} %collective-permute-done.one_ref, f32[8,256,256]{2,1,0:T(8,128)} %collective-permute-done.1.two_ref), custom_call_target="tpu_custom_call" | custom-call | bytes 5242880 | tf_op jit(solution)/shard_map/split_blocks/pallas_call | solution.py:108
  151.5 11.5 %collective-permute-done.3.refs_2_ = f32[4,256,256]{2,1,0:T(8,128)} collective-permute-done((f32[4,256,256]{2,1,0:T(8,128)}, f32[4,256,256]{2,1,0:T(8,128)}, u32[]{:S(2)}, u32[]{:S(2)}) %collective-permute-start.3) | collective-permute-done | bytes 1048608 | tf_op jit(solution)/shard_map/ppermute | solution.py:197
  162.9 5.7 %collective-permute-done.4.refs_3_ = f32[4,256,256]{2,1,0:T(8,128)} collective-permute-done((f32[4,256,256]{2,1,0:T(8,128)}, f32[4,256,256]{2,1,0:T(8,128)}, u32[]{:S(2)}, u32[]{:S(2)}) %collective-permute-start.4) | collective-permute-done | bytes 1048608 | tf_op jit(solution)/shard_map/ppermute | solution.py:198
  168.6 1.3 copy-done.4
  169.9 1.3 copy-done.5
  171.2 1.6 copy-done.7
  172.8 7.2 %products.4.refs_10_ = f32[8,256,256]{2,1,0:T(8,128)S(1)} custom-call(s32[11]{0:T(128)S(1)} %pad_add_fusion.place_ref, f32[8,256,256]{2,1,0:T(8,128)S(1)} %copy-done.3, f32[8,256,256]{2,1,0:T(8,128)S(1)} %copy-done.7, f32[4,256,256]{2,1,0:T(8,128)} %collective-permute-done.3.refs_2_, f32[4,256,256]{2,1,0:T(8,128)} %collective-permute-done.4.refs_3_, ...), custom_call_target="tpu_custom_call" | custom-call | flops 2415919104 | bytes 12582912 | tf_op jit(solution)/shard_map/products/pallas_call | solution.py:169
  180.1 1.3 copy-done
  181.4 5.4 %all-to-all-done.2 = f32[8,256,256]{2,1,0:T(8,128)} async-done(((f32[8,256,256]{2,1,0:T(8,128)}), f32[8,256,256]{2,1,0:T(8,128)}, u32[]{:S(2)}, u32[]{:S(2)}) %all-to-all-start.2) | async-done | bytes 2097184 | tf_op jit(solution)/shard_map/all_to_all | solution.py:203
  186.8 2.3 order_rest.1
  189.9 4.5 %collective-permute-start.12 = (f32[1,256,256]{2,1,0:T(8,128)S(1)}, f32[1,256,256]{2,1,0:T(8,128)S(1)}, u32[]{:S(2)}, u32[]{:S(2)}) collective-permute-start(f32[1,256,256]{2,1,0:T(8,128)S(1)} %slice.57), channel_id=1, source_target_pairs={{0,240},{16,32},{32,16},{48,64},{64,48},{80,96},{96,80},{112,128},... | collective-permute-start | bytes 786440 | tf_op jit(solution)/shard_map/ppermute | solution.py:197
  194.5 1.6 collective-permute-start.9
  196.1 1.2 collective-permute-start.10
  197.4 3.3 %collective-permute-done.12.refs_2_ = f32[1,256,256]{2,1,0:T(8,128)S(1)} collective-permute-done((f32[1,256,256]{2,1,0:T(8,128)S(1)}, f32[1,256,256]{2,1,0:T(8,128)S(1)}, u32[]{:S(2)}, u32[]{:S(2)}) %collective-permute-start.12) | collective-permute-done | bytes 262176 | tf_op jit(solution)/shard_map/ppermute | solution.py:197
  200.7 6.2 %collective-permute-done.13.refs_3_ = f32[1,256,256]{2,1,0:T(8,128)S(1)} collective-permute-done((f32[1,256,256]{2,1,0:T(8,128)S(1)}, f32[1,256,256]{2,1,0:T(8,128)S(1)}, u32[]{:S(2)}, u32[]{:S(2)}) %collective-permute-start.13) | collective-permute-done | bytes 262176 | tf_op jit(solution)/shard_map/ppermute | solution.py:198
  206.8 1.6 products.7
  208.5 2.0 collective-permute-start.17
  211.0 1.6 products.6
  212.6 2.3 collective-permute-done.14
  214.9 1.3 collective-permute-done.17
  216.3 2.0 collective-permute-start.18
  218.4 9.7 %collective-permute-done.6.refs_2_ = f32[2,256,256]{2,1,0:T(8,128)S(1)} collective-permute-done((f32[2,256,256]{2,1,0:T(8,128)S(1)}, f32[2,256,256]{2,1,0:T(8,128)S(1)}, u32[]{:S(2)}, u32[]{:S(2)}) %collective-permute-start.6) | collective-permute-done | bytes 524320 | tf_op jit(solution)/shard_map/ppermute | solution.py:197
  228.0 0.7 collective-permute-done.7.refs_3_
  228.7 2.6 %products.5 = f32[4,256,256]{2,1,0:T(8,128)S(1)} custom-call(s32[11]{0:T(128)S(1)} %pad_add_fusion.place_ref, f32[4,256,256]{2,1,0:T(8,128)S(1)} %get-tuple-element.53.refs_0_, f32[4,256,256]{2,1,0:T(8,128)S(1)} %collective-permute-done.5.refs_1_, f32[2,256,256]{2,1,0:T(8,128)S(1)} %collective-permute-done.6.refs_2_, ...), custom_call_target="tpu_custom_call" | custom-call | flops 1207959552 | bytes 6291456 | tf_op jit(solution)/shard_map/products/pallas_call | solution.py:169
  231.4 0.6 collective-permute-start.19
  232.0 2.7 %collective-permute-start.16 = (f32[256,256]{1,0:T(8,128)S(1)}, f32[256,256]{1,0:T(8,128)S(1)}, u32[]{:S(2)}, u32[]{:S(2)}) collective-permute-start(f32[256,256]{1,0:T(8,128)S(1)} %get-tuple-element.59), channel_id=1, source_target_pairs={{1,0},{2,1},{3,2},{4,3},{5,4},{6,5},{7,6},{0,7},{9,8},{10,9},{11,1... | collective-permute-start | bytes 786440 | tf_op jit(solution)/shard_map/ppermute | solution.py:188
  234.7 5.9 %collective-permute-done.19 = f32[256,256]{1,0:T(8,128)S(1)} collective-permute-done((f32[256,256]{1,0:T(8,128)S(1)}, f32[256,256]{1,0:T(8,128)S(1)}, u32[]{:S(2)}, u32[]{:S(2)}) %collective-permute-start.19) | collective-permute-done | bytes 262176 | tf_op jit(solution)/shard_map/ppermute | solution.py:188
  240.8 7.6 %collective-permute-done.20 = f32[256,256]{1,0:T(8,128)S(1)} collective-permute-done((f32[256,256]{1,0:T(8,128)S(1)}, f32[256,256]{1,0:T(8,128)S(1)}, u32[]{:S(2)}, u32[]{:S(2)}) %collective-permute-start.20) | collective-permute-done | bytes 262176 | tf_op jit(solution)/shard_map/ppermute | solution.py:188
  248.3 0.8 fusion.6
  (46 shorter events, 2.0 us)
Async XLA Ops:
  5.7 65.1 %all-to-all-start = ((f32[16,256,256]{2,1,0:T(8,128)}), f32[16,256,256]{2,1,0:T(8,128)}, u32[]{:S(2)}, u32[]{:S(2)}) async-start(f32[16,256,256]{2,1,0:T(8,128)} %order_panel.1), calls=%async_computation | async-start | bytes 8388608 | tf_op jit(solution)/shard_map/all_to_all | solution.py:203
  15.2 55.6 %collective-permute-start = (f32[2,256,256]{2,1,0:T(8,128)}, f32[2,256,256]{2,1,0:T(8,128)S(1)}, u32[]{:S(2)}, u32[]{:S(2)}) collective-permute-start(f32[2,256,256]{2,1,0:T(8,128)} %get-tuple-element.34), channel_id=1, source_target_pairs={{8,0},{0,8},{9,1},{1,9},{10,2},{2,10},{11,3},{3,11},{12,4},{4,12},... | collective-permute-start | bytes 1572872 | tf_op jit(solution)/shard_map/ppermute | solution.py:188
  73.9 59.8 %all-to-all-start.1 = ((f32[8,256,256]{2,1,0:T(8,128)}), f32[8,256,256]{2,1,0:T(8,128)S(1)}, u32[]{:S(2)}, u32[]{:S(2)}) async-start(f32[8,256,256]{2,1,0:T(8,128)} %dynamic-slice_bitcast_fusion.1), calls=%async_computation.1 | async-start | bytes 4194304 | tf_op jit(solution)/shard_map/all_to_all | solution.py:203
  82.4 47.5 %collective-permute-start.1 = (f32[8,256,256]{2,1,0:T(8,128)}, f32[8,256,256]{2,1,0:T(8,128)}, u32[]{:S(2)}, u32[]{:S(2)}) collective-permute-start(f32[8,256,256]{2,1,0:T(8,128)} %get-tuple-element.40), channel_id=1, source_target_pairs={{8,0},{0,8},{9,1},{1,9},{10,2},{2,10},{11,3},{3,11},{12,4},{4,12},... | collective-permute-start | bytes 6291464 | tf_op jit(solution)/shard_map/ppermute | solution.py:188
  133.7 4.5 %copy-start.2 = (f32[8,256,256]{2,1,0:T(8,128)}, f32[8,256,256]{2,1,0:T(8,128)S(1)}, u32[]{:S(2)}) copy-start(f32[8,256,256]{2,1,0:T(8,128)S(1)} %all-to-all-done.1.refs_0_) | copy-start | bytes 6291460
  133.7 53.1 %all-to-all-start.2 = ((f32[8,256,256]{2,1,0:T(8,128)}), f32[8,256,256]{2,1,0:T(8,128)}, u32[]{:S(2)}, u32[]{:S(2)}) async-start(f32[8,256,256]{2,1,0:T(8,128)} %dynamic-slice_bitcast_fusion), calls=%async_computation.2 | async-start | bytes 4194304 | tf_op jit(solution)/shard_map/all_to_all | solution.py:203
  138.0 8.1 %copy-start.8 = (s32[8]{0:T(128)S(1)}, s32[8]{0:T(128)}, u32[]{:S(2)}) copy-start(s32[8]{0:T(128)} %constant.80.clone) | copy-start | bytes 100
  138.1 5.6 %collective-permute-start.2 = (f32[8,256,256]{2,1,0:T(8,128)S(1)}, f32[8,256,256]{2,1,0:T(8,128)S(1)}, u32[]{:S(2)}, u32[]{:S(2)}) collective-permute-start(f32[8,256,256]{2,1,0:T(8,128)S(1)} %all-to-all-done.1.refs_0_), channel_id=1, source_target_pairs={{0,16},{16,0},{32,48},{48,32},{64,80},{80,64},{96,112},{112,96},{1... | collective-permute-start | bytes 6291464 | tf_op jit(solution)/shard_map/ppermute | solution.py:192
  139.2 23.7 %collective-permute-start.3 = (f32[4,256,256]{2,1,0:T(8,128)}, f32[4,256,256]{2,1,0:T(8,128)}, u32[]{:S(2)}, u32[]{:S(2)}) collective-permute-start(f32[4,256,256]{2,1,0:T(8,128)} %slice.48), channel_id=1, source_target_pairs={{0,240},{16,32},{32,16},{48,64},{64,48},{80,96},{96,80},{112,128},... | collective-permute-start | bytes 3145736 | tf_op jit(solution)/shard_map/ppermute | solution.py:197
  144.8 1.4 copy-start.6
  146.1 22.5 %collective-permute-start.4 = (f32[4,256,256]{2,1,0:T(8,128)}, f32[4,256,256]{2,1,0:T(8,128)}, u32[]{:S(2)}, u32[]{:S(2)}) collective-permute-start(f32[4,256,256]{2,1,0:T(8,128)} %slice.64), channel_id=1, source_target_pairs={{0,32},{16,240},{32,64},{48,16},{64,96},{80,48},{96,128},{112,80},... | collective-permute-start | bytes 3145736 | tf_op jit(solution)/shard_map/ppermute | solution.py:198
  146.1 22.5 %copy-start.3 = (f32[8,256,256]{2,1,0:T(8,128)S(1)}, f32[8,256,256]{2,1,0:T(8,128)}, u32[]{:S(2)}) copy-start(f32[8,256,256]{2,1,0:T(8,128)} %copy-done.2) | copy-start | bytes 6291460
  168.6 1.3 copy-start.4
  169.9 1.3 copy-start.5
  171.2 1.6 copy-start.7
  180.1 1.3 copy-start
  186.8 20.0 %copy-start.1 = (f32[8,256,256]{2,1,0:T(8,128)S(1)}, f32[8,256,256]{2,1,0:T(8,128)}, u32[]{:S(2)}) copy-start(f32[8,256,256]{2,1,0:T(8,128)} %copy-done) | copy-start | bytes 6291460
  189.1 5.2 %collective-permute-start.11 = (f32[2,256,256]{2,1,0:T(8,128)S(1)}, f32[2,256,256]{2,1,0:T(8,128)S(1)}, u32[]{:S(2)}, u32[]{:S(2)}) collective-permute-start(f32[2,256,256]{2,1,0:T(8,128)S(1)} %get-tuple-element.58.refs_0_), channel_id=1, source_target_pairs={{0,16},{16,0},{32,48},{48,32},{64,80},{80,64},{96,112},{112,96},{1... | collective-permute-start | bytes 1572872 | tf_op jit(solution)/shard_map/ppermute | solution.py:192
  189.2 21.3 %collective-permute-start.5 = (f32[4,256,256]{2,1,0:T(8,128)S(1)}, f32[4,256,256]{2,1,0:T(8,128)S(1)}, u32[]{:S(2)}, u32[]{:S(2)}) collective-permute-start(f32[4,256,256]{2,1,0:T(8,128)S(1)} %get-tuple-element.53.refs_0_), channel_id=1, source_target_pairs={{0,16},{16,0},{32,48},{48,32},{64,80},{80,64},{96,112},{112,96},{1... | collective-permute-start | bytes 3145736 | tf_op jit(solution)/shard_map/ppermute | solution.py:192
  189.7 6.4 %collective-permute-start.8 = (f32[2,256,256]{2,1,0:T(8,128)S(1)}, f32[2,256,256]{2,1,0:T(8,128)S(1)}, u32[]{:S(2)}, u32[]{:S(2)}) collective-permute-start(f32[2,256,256]{2,1,0:T(8,128)S(1)} %get-tuple-element.57.refs_0_), channel_id=1, source_target_pairs={{0,16},{16,0},{32,48},{48,32},{64,80},{80,64},{96,112},{112,96},{1... | collective-permute-start | bytes 1572872 | tf_op jit(solution)/shard_map/ppermute | solution.py:192
  189.9 10.8 %collective-permute-start.12 = (f32[1,256,256]{2,1,0:T(8,128)S(1)}, f32[1,256,256]{2,1,0:T(8,128)S(1)}, u32[]{:S(2)}, u32[]{:S(2)}) collective-permute-start(f32[1,256,256]{2,1,0:T(8,128)S(1)} %slice.57), channel_id=1, source_target_pairs={{0,240},{16,32},{32,16},{48,64},{64,48},{80,96},{96,80},{112,128},... | collective-permute-start | bytes 786440 | tf_op jit(solution)/shard_map/ppermute | solution.py:197
  194.4 12.4 %collective-permute-start.13 = (f32[1,256,256]{2,1,0:T(8,128)S(1)}, f32[1,256,256]{2,1,0:T(8,128)S(1)}, u32[]{:S(2)}, u32[]{:S(2)}) collective-permute-start(f32[1,256,256]{2,1,0:T(8,128)S(1)} %slice.70), channel_id=1, source_target_pairs={{0,32},{16,240},{32,64},{48,16},{64,96},{80,48},{96,128},{112,80},... | collective-permute-start | bytes 786440 | tf_op jit(solution)/shard_map/ppermute | solution.py:198
  194.5 16.4 %collective-permute-start.9 = (f32[1,256,256]{2,1,0:T(8,128)S(1)}, f32[1,256,256]{2,1,0:T(8,128)S(1)}, u32[]{:S(2)}, u32[]{:S(2)}) collective-permute-start(f32[1,256,256]{2,1,0:T(8,128)S(1)} %slice.54), channel_id=1, source_target_pairs={{0,240},{16,32},{32,16},{48,64},{64,48},{80,96},{96,80},{112,128},... | collective-permute-start | bytes 786440 | tf_op jit(solution)/shard_map/ppermute | solution.py:197
  196.1 14.9 %collective-permute-start.10 = (f32[1,256,256]{2,1,0:T(8,128)S(1)}, f32[1,256,256]{2,1,0:T(8,128)S(1)}, u32[]{:S(2)}, u32[]{:S(2)}) collective-permute-start(f32[1,256,256]{2,1,0:T(8,128)S(1)} %slice.68), channel_id=1, source_target_pairs={{0,32},{16,240},{32,64},{48,16},{64,96},{80,48},{96,128},{112,80},... | collective-permute-start | bytes 786440 | tf_op jit(solution)/shard_map/ppermute | solution.py:198
  208.4 6.5 %collective-permute-start.14 = (f32[256,256]{1,0:T(8,128)S(1)}, f32[256,256]{1,0:T(8,128)S(1)}, u32[]{:S(2)}, u32[]{:S(2)}) collective-permute-start(f32[256,256]{1,0:T(8,128)S(1)} %get-tuple-element.63), channel_id=1, source_target_pairs={{1,0},{2,1},{3,2},{4,3},{5,4},{6,5},{7,6},{0,7},{9,8},{10,9},{11,1... | collective-permute-start | bytes 786440 | tf_op jit(solution)/shard_map/ppermute | solution.py:188
  208.5 7.7 %collective-permute-start.17 = (f32[256,256]{1,0:T(8,128)S(1)}, f32[256,256]{1,0:T(8,128)S(1)}, u32[]{:S(2)}, u32[]{:S(2)}) collective-permute-start(f32[256,256]{1,0:T(8,128)S(1)} %get-tuple-element.64), channel_id=1, source_target_pairs={{7,0},{0,1},{1,2},{2,3},{3,4},{4,5},{5,6},{6,7},{15,8},{8,9},{9,10... | collective-permute-start | bytes 786440 | tf_op jit(solution)/shard_map/ppermute | solution.py:188
  210.6 17.4 %collective-permute-start.6 = (f32[2,256,256]{2,1,0:T(8,128)S(1)}, f32[2,256,256]{2,1,0:T(8,128)S(1)}, u32[]{:S(2)}, u32[]{:S(2)}) collective-permute-start(f32[2,256,256]{2,1,0:T(8,128)S(1)} %slice.50), channel_id=1, source_target_pairs={{0,240},{16,32},{32,16},{48,64},{64,48},{80,96},{96,80},{112,128},... | collective-permute-start | bytes 1572872 | tf_op jit(solution)/shard_map/ppermute | solution.py:197
  210.9 17.8 %collective-permute-start.7 = (f32[2,256,256]{2,1,0:T(8,128)S(1)}, f32[2,256,256]{2,1,0:T(8,128)S(1)}, u32[]{:S(2)}, u32[]{:S(2)}) collective-permute-start(f32[2,256,256]{2,1,0:T(8,128)S(1)} %slice.65), channel_id=1, source_target_pairs={{0,32},{16,240},{32,64},{48,16},{64,96},{80,48},{96,128},{112,80},... | collective-permute-start | bytes 1572872 | tf_op jit(solution)/shard_map/ppermute | solution.py:198
  216.3 15.0 %collective-permute-start.15 = (f32[256,256]{1,0:T(8,128)S(1)}, f32[256,256]{1,0:T(8,128)S(1)}, u32[]{:S(2)}, u32[]{:S(2)}) collective-permute-start(f32[256,256]{1,0:T(8,128)S(1)} %get-tuple-element.61), channel_id=1, source_target_pairs={{1,0},{2,1},{3,2},{4,3},{5,4},{6,5},{7,6},{0,7},{9,8},{10,9},{11,1... | collective-permute-start | bytes 786440 | tf_op jit(solution)/shard_map/ppermute | solution.py:188
  216.3 14.9 %collective-permute-start.18 = (f32[256,256]{1,0:T(8,128)S(1)}, f32[256,256]{1,0:T(8,128)S(1)}, u32[]{:S(2)}, u32[]{:S(2)}) collective-permute-start(f32[256,256]{1,0:T(8,128)S(1)} %get-tuple-element.62), channel_id=1, source_target_pairs={{7,0},{0,1},{1,2},{2,3},{3,4},{4,5},{5,6},{6,7},{15,8},{8,9},{9,10... | collective-permute-start | bytes 786440 | tf_op jit(solution)/shard_map/ppermute | solution.py:188
  231.4 9.2 %collective-permute-start.19 = (f32[256,256]{1,0:T(8,128)S(1)}, f32[256,256]{1,0:T(8,128)S(1)}, u32[]{:S(2)}, u32[]{:S(2)}) collective-permute-start(f32[256,256]{1,0:T(8,128)S(1)} %get-tuple-element.60), channel_id=1, source_target_pairs={{7,0},{0,1},{1,2},{2,3},{3,4},{4,5},{5,6},{6,7},{15,8},{8,9},{9,10... | collective-permute-start | bytes 786440 | tf_op jit(solution)/shard_map/ppermute | solution.py:188
  232.0 8.7 %collective-permute-start.16 = (f32[256,256]{1,0:T(8,128)S(1)}, f32[256,256]{1,0:T(8,128)S(1)}, u32[]{:S(2)}, u32[]{:S(2)}) collective-permute-start(f32[256,256]{1,0:T(8,128)S(1)} %get-tuple-element.59), channel_id=1, source_target_pairs={{1,0},{2,1},{3,2},{4,3},{5,4},{6,5},{7,6},{0,7},{9,8},{10,9},{11,1... | collective-permute-start | bytes 786440 | tf_op jit(solution)/shard_map/ppermute | solution.py:188
  240.7 7.7 %collective-permute-start.20 = (f32[256,256]{1,0:T(8,128)S(1)}, f32[256,256]{1,0:T(8,128)S(1)}, u32[]{:S(2)}, u32[]{:S(2)}) collective-permute-start(f32[256,256]{1,0:T(8,128)S(1)} %fusion.2), channel_id=1, source_target_pairs={{7,0},{0,1},{1,2},{2,3},{3,4},{4,5},{5,6},{6,7},{15,8},{8,9},{9,10... | collective-permute-start | bytes 786440 | tf_op jit(solution)/shard_map/ppermute | solution.py:188

commit v4 on v3

--- a/solution.py
+++ b/solution.py
@@ -14,7 +14,8 @@
 WINDOW = 3
 OFFSETS = (4, -3, 3, -2, 2, -1, 1, 0)
 GROUPS = (2, 2, 4)
-EARLY = 2
+EARLY = 3
+LATE = 5
 LARGE = 60 * 2**20
 SMALL = 16 * 2**20
 
@@ -64,60 +65,77 @@
     return high, low
 
 
-def split_stored_body(index_ref, in_ref, high_ref, low_ref):
+def move_body(sources, index_ref, *refs):
+    count = len(sources)
+    held, in_sems, out_sems = refs[-3:]
+    inputs = max(which for which, _ in sources) + 1
+    in_refs, out_refs = refs[:inputs], refs[inputs:-3]
+    if len(out_refs) == 1:
+        places = [(out_refs[0], index_ref[d]) for d in range(count)]
+    else:
+        places = [(out_ref, d) for out_ref in out_refs for d in range(out_ref.shape[0])]
+    brings = [
+        pltpu.make_async_copy(in_refs[which].at[e], held.at[d], in_sems.at[d])
+        for d, (which, e) in enumerate(sources)
+    ]
+    puts = [pltpu.make_async_copy(held.at[d], out.at[e], out_sems.at[d]) for d, (out, e) in enumerate(places)]
+    for bring in brings:
+        bring.start()
+    for bring, put in zip(brings, puts):
+        bring.wait()
+        put.start()
+    for put in puts:
+        put.wait()
+
+
+def move_blocks(inputs, sources, parts, index, name):
+    shape, count = inputs[0].shape[1:], len(sources)
+    return pl.pallas_call(
+        functools.partial(move_body, sources),
+        in_specs=[pl.BlockSpec(memory_space=pltpu.SMEM)] + [pl.BlockSpec(memory_space=pl.ANY)] * len(inputs),
+        out_specs=[pl.BlockSpec(memory_space=pl.ANY)] * len(parts),
+        out_shape=[jax.ShapeDtypeStruct((part, *shape), jnp.float32) for part in parts],
+        scratch_shapes=[
+            pltpu.VMEM((count, *shape), jnp.float32),
+            pltpu.SemaphoreType.DMA((count,)),
+            pltpu.SemaphoreType.DMA((count,)),
+        ],
+        name=name,
+        compiler_params=pltpu.CompilerParams(vmem_limit_bytes=LARGE),
+        cost_estimate=pl.CostEstimate(flops=0, bytes_accessed=8 * count * shape[0] * shape[1], transcendentals=0),
+    )(index, *inputs)
+
+
+def split_body(cut, index_ref, own_ref, one_ref, two_ref, high_ref, low_ref):
     del index_ref
-    high_ref[0], low_ref[0] = split(in_ref[...])
-
-
-def split_stored(a_stored, index, deep):
-    count, rows = index.shape[0], a_stored.shape[0]
-    out = jax.ShapeDtypeStruct((count, rows, deep), jnp.bfloat16)
-    out_spec = pl.BlockSpec((1, rows, deep), lambda g, index: (g, 0, 0))
+    deep = own_ref.shape[1]
+    high_ref[0, :, :deep], low_ref[0, :, :deep] = split(own_ref[...])
+    other = jnp.where(pl.program_id(0) < cut, one_ref[0], two_ref[0])
+    high_ref[0, :, deep:], low_ref[0, :, deep:] = split(other)
+
+
+def split_slab(a_stored, index, one, two):
+    cut, rows, deep = one.shape
+    count = cut + two.shape[0]
+    out = jax.ShapeDtypeStruct((count, rows, 2 * deep), jnp.bfloat16)
+    out_spec = pl.BlockSpec((1, rows, 2 * deep), lambda g, index: (g, 0, 0))
     return pl.pallas_call(
-        split_stored_body,
+        functools.partial(split_body, cut),
         grid_spec=pltpu.PrefetchScalarGridSpec(
             num_scalar_prefetch=1,
             grid=(count,),
-            in_specs=[pl.BlockSpec((rows, deep), lambda g, index: (0, index[g]))],
+            in_specs=[
+                pl.BlockSpec((rows, deep), lambda g, index: (0, index[g])),
+                pl.BlockSpec((1, rows, deep), lambda g, index: (jnp.minimum(g, cut - 1), 0, 0)),
+                pl.BlockSpec((1, rows, deep), lambda g, index: (jnp.maximum(g - cut, 0), 0, 0)),
+            ],
             out_specs=[out_spec, out_spec],
         ),
         out_shape=[out, out],
-        name="split_stored",
-        compiler_params=pltpu.CompilerParams(vmem_limit_bytes=LARGE),
-        cost_estimate=pl.CostEstimate(flops=0, bytes_accessed=8 * count * rows * deep, transcendentals=0),
-    )(index, a_stored)
-
-
-def split_blocks_body(cut, one_ref, two_ref, high_ref, low_ref):
-    at = pl.program_id(0)
-
-    @pl.when(at < cut)
-    def _():
-        high_ref[0], low_ref[0] = split(one_ref[0])
-
-    @pl.when(at >= cut)
-    def _():
-        high_ref[0], low_ref[0] = split(two_ref[0])
-
-
-def split_blocks(one, two):
-    cut, rows, deep = one.shape
-    count = cut + two.shape[0]
-    out = jax.ShapeDtypeStruct((count, rows, deep), jnp.bfloat16)
-    out_spec = pl.BlockSpec((1, rows, deep), lambda g: (g, 0, 0))
-    return pl.pallas_call(
-        functools.partial(split_blocks_body, cut),
-        grid=(count,),
-        in_specs=[
-            pl.BlockSpec((1, rows, deep), lambda g: (jnp.minimum(g, cut - 1), 0, 0)),
-            pl.BlockSpec((1, rows, deep), lambda g: (jnp.maximum(g - cut, 0), 0, 0)),
-        ],
-        out_specs=[out_spec, out_spec],
-        out_shape=[out, out],
-        name="split_blocks",
+        name="split_slab",
         compiler_params=pltpu.CompilerParams(vmem_limit_bytes=SMALL),
-        cost_estimate=pl.CostEstimate(flops=0, bytes_accessed=8 * count * rows * deep, transcendentals=0),
-    )(one, two)
+        cost_estimate=pl.CostEstimate(flops=0, bytes_accessed=16 * count * rows * deep, transcendentals=0),
+    )(index, a_stored, one, two)
 
 
 def product_body(cut, first, ordered, has_start, place_ref, *refs):
@@ -217,36 +235,62 @@
     around = (plane + jnp.array(OFFSETS, dtype=jnp.int32)) % planes
     core = lax.axis_index("core").astype(jnp.int32)
     place = jnp.concatenate([around, jnp.stack([jnp.ones_like(core), 2 - 2 * core, 2 * core])])
+    half = deep // 2
+    y_hi, x = lax.axis_index("y_hi").astype(jnp.int32), lax.axis_index("x").astype(jnp.int32)
+    x_count = lax.axis_size("x")
+
     order = (jnp.arange(blocks, dtype=jnp.int32) + col_index + 1) % blocks
-    (panel,) = order_blocks(b_stored, order, deep, 0, (blocks,), "order_panel")
-    theirs, panel = lax.optimization_barrier((theirs, panel))
-    early, late = order_blocks(a_stored, theirs, deep, 1, (EARLY, planes + WINDOW - 1 - EARLY), "order_slab")
-    early = shifted(early, "y_lo", 1)
+    (panel,) = order_blocks(b_stored, 2 * order, half, 0, (blocks,), "order_panel")
+
+    step = jnp.arange(blocks, dtype=jnp.int32)
+    to_core, to_y, to_x = step // (2 * x_count) ^ core, step // x_count % 2 ^ y_hi, (step % x_count + x) % x_count
+    far = (to_y * planes + to_x * 2 + to_core + col_index + 1) % blocks
+    far, panel = lax.optimization_barrier((far, panel))
+    here, there = order_blocks(b_stored, 2 * far + 1, half, 0, (planes, planes), "order_panel")
+    there = to_other_core(there)
+    slab = jnp.concatenate([2 * theirs, 2 * theirs + 1])
+    slab, panel = lax.optimization_barrier((slab, panel))
+    kinds = kinds.shape[0]
+    slabs = list(order_blocks(a_stored, slab, half, 1, (EARLY, kinds - EARLY, LATE, kinds - LATE), "order_slab"))
+    here_across = shifted(here[x_count:], "y_hi", 1)
     panel = exchange(panel, ROW)
-    panel, early, late = lax.optimization_barrier((panel, early, late))
-    panel = panel.reshape(2, planes, deep, panel.shape[2])
-
-    one = lax.dynamic_index_in_dim(panel, side, 0, keepdims=False)
-    late, mine, one = lax.optimization_barrier((late, mine, one))
-    panel, _ = lax.optimization_barrier((panel, one))
-    two = lax.dynamic_index_in_dim(panel, 1 - side, 0, keepdims=False)
-    late = shifted(late, "y_lo", 1)
-    a_own = split_stored(a_stored, mine, deep)
+    slabs[0] = shifted(slabs[0], "y_lo", 1)
+    panel, here_across, *slabs = lax.optimization_barrier((panel, here_across, *slabs))
+
+    pieces = (step % 2 ^ side) * planes + step // 2
+    (one,) = order_blocks(panel.reshape(-1, panel.shape[2]), pieces, half, 0, (blocks,), "order_planes")
+    there, one = lax.optimization_barrier((there, one))
+    there_across = shifted(there[x_count:], "y_hi", 1)
+    there_across, *slabs = lax.optimization_barrier((there_across, *slabs))
+    slabs[1:3] = [shifted(slab, "y_lo", 1) for slab in slabs[1:3]]
+    held = [here, here_across, there, there_across]
+    sources = tuple((which, distance) for distance in range(x_count) for which in range(4))
+    along = move_blocks(held, sources, (4,) * x_count, step, "order_distance")
+    along = [along[0]] + [shifted(along[d], "x", d) for d in range(1, x_count)]
+    from_x, from_core, from_y = (x - step // 4) % x_count, step // 2 % 2 ^ core, step % 2 ^ y_hi
+    goal = (from_x * 2 + from_core) * 2 + (from_y ^ side)
+    sources = tuple((distance, e) for distance in range(x_count) for e in range(4))
+    (two,) = move_blocks(along, sources, (blocks,), goal, "order_planes")
+    one, two = one.reshape(planes, deep, -1), two.reshape(planes, deep, -1)
+
     one = exchange(one, "z")
-    two, one, late, *a_own = lax.optimization_barrier((two, one, late, *a_own))
+    two, one, *slabs = lax.optimization_barrier((two, one, *slabs))
+    slabs[3] = shifted(slabs[3], "y_lo", 1)
     one_other = to_other_core(one)
     one_next = to_next_chips(one[: planes // 2], one_other[planes // 2 :])
     two = exchange(two, "z")
-    a_other = split_blocks(early, late)
-    total = products(place, *a_own, [one, one_other, *one_next], 0, planes)
-
-    two, total, *a_other = lax.optimization_barrier((two, total, *a_other))
+    a_first = split_slab(a_stored, 2 * mine, *slabs[:2])
+    total = products(place, *a_first, [one, one_other, *one_next], 0, planes)
+    total, *slabs = lax.optimization_barrier((total, *slabs))
+    a_second = split_slab(a_stored, 2 * mine + 1, *slabs[2:])
+
+    two, total, *a_second = lax.optimization_barrier((two, total, *a_second))
     groups = order_blocks(two.reshape(-1, two.shape[2]), around, deep, 0, GROUPS, "order_rest", SMALL)
     others = [to_other_core(group) for group in groups]
     done, first = [], 0
     for own, other, count in zip(groups, others, GROUPS):
         came = to_next_chips(own[: count // 2], other[count // 2 :])
-        part = products(place, *a_other, [own, other, *came], first, count, 0, total)
+        part = products(place, *a_second, [own, other, *came], first, count, 0, total)
         done += [part[g] for g in range(count)]
         first += count
     ahead, behind = shifted(done[0], "z", 1), shifted(done[1], "z", -1)

time: 250 us -> 240 us (0.960)
  waiting for transfers between devices: 154 us -> 123 us
  starting transfers between devices: 41.8 us -> 59.6 us
  Pallas kernels: 35.8 us -> 40.6 us
  local copies, waits for them, and re-layouts: 15.4 us -> 11.5 us
    ppermute x9 -> x16, waiting for transfers between devices: 107 us -> 85.8 us  [shifted(): lax.ppermute(block, axes, [((i - distance) % n, i) for i in range(n)])]
    ppermute x9 -> x16, starting transfers between devices: 9.72 us -> 24.5 us  [shifted(): lax.ppermute(block, axes, [((i - distance) % n, i) for i in range(n)])]
    all_to_all x3, waiting for transfers between devices: 9.23 us -> 1.76 us  [exchange(): return lax.all_to_all(block, axes, split_axis=0, concat_axis=0, tiled=True)]
    squeeze x2 -> x0, local copies, waits for them, and re-layouts: 6.22 us -> none  [the longest x1 3.11 us: on_device(): two = lax.dynamic_index_in_dim(panel, 1 - side, 0, keepdims=False)]
    pallas_call x3 -> x5, Pallas kernels: 10.2 us -> 15.6 us  [order_blocks(): pl.pallas_call(functools.partial(order_body, along), in_specs=[pl.BlockSp...]
    pallas_call x2 -> x4, Pallas kernels: 12.7 us -> 12 us  [the longest x2 6.54 us: move_blocks(): pl.pallas_call(functools.partial(move_body, sources), in_specs=[pl.BlockS...]
    unnamed x18 -> x26, local copies, waits for them, and re-layouts: 6.91 us -> 7.54 us
  transfers between devices with their start and end apart: 24 -> 32, of which waited for: 14 -> 19; matrix products, arithmetic and copies ran while one was open for 2% -> 2% of each run, Pallas kernels for 12% -> 15%
where the time goes in v4:
time: 240 us; the launch traced here: 239 us
  waiting for transfers between devices  123 us (51%)
  starting transfers between devices  59.6 us (25%)
  Pallas kernels  40.6 us (17%)
  local copies, waits for them, and re-layouts  11.5 us (5%)
  other arithmetic  3.78 us (2%)
    ppermute x16, waiting for transfers between devices, shifted(): lax.ppermute(block, axes, [((i - distance) % n, i) for i in range(n)])  85.8 us
    ppermute x16, starting transfers between devices, shifted(): lax.ppermute(block, axes, [((i - distance) % n, i) for i in range(n)])  24.5 us
    ppermute x4, waiting for transfers between devices, to_next_chips(): lax.ppermute(own, ROW, [(i, (i + (1 if i % 2 else -1)) % n) for i in rang...  22.7 us
    all_to_all x3, starting transfers between devices, exchange(): return lax.all_to_all(block, axes, split_axis=0, concat_axis=0, tiled=True)  21.2 us
    pallas_call x5, Pallas kernels, order_blocks(): pl.pallas_call(functools.partial(order_body, along), in_specs=[pl.BlockSp...  15.6 us
    pallas_call x4, Pallas kernels, products(): pl.pallas_call(functools.partial(product_body, cut, first, ordered, start...  13 us
    ppermute x4, waiting for transfers between devices, to_next_chips(): lax.ppermute(other, ROW, [(i, (i + (-2 if i % 2 else 2)) % n) for i in ra...  12.9 us
    ppermute x4, starting transfers between devices, to_next_chips(): lax.ppermute(own, ROW, [(i, (i + (1 if i % 2 else -1)) % n) for i in rang...  11.1 us
  transfers between devices with their start and end apart: 32, of which 19 were waited for; matrix products, arithmetic and copies ran while one was open for 2% of the time, Pallas kernels for 15%

profile of v4, /device:TPU:8, one launch (start us, length us, event | category | flops | bytes accessed | tf_op | source)
XLA Modules:
  0.0 239.0 jit_solution(8412762605171349079)
XLA Ops:
  0.5 3.3 %order_panel.2 = f32[16,128,256]{2,1,0:T(8,128)} custom-call(s32[16]{0:T(128)} %get-tuple-element.106.index_ref, f32[4096,256]{1,0:T(8,128)} %in_ref.4), custom_call_target="tpu_custom_call" | custom-call | bytes 4194304 | tf_op jit(solution)/shard_map/order_panel/pallas_call | solution.py:46
  4.5 6.1 %all-to-all-start = ((f32[16,128,256]{2,1,0:T(8,128)}), f32[16,128,256]{2,1,0:T(8,128)S(1)}, u32[]{:S(2)}, u32[]{:S(2)}) async-start(f32[16,128,256]{2,1,0:T(8,128)} %order_panel.2), calls=%async_computation | async-start | bytes 4194304 | tf_op jit(solution)/shard_map/all_to_all | solution.py:221
  11.1 3.3 %order_panel.3 = (f32[8,128,256]{2,1,0:T(8,128)}, f32[8,128,256]{2,1,0:T(8,128)}) custom-call(s32[16]{0:T(128)} %multiply_add_fusion.1.index_ref, f32[4096,256]{1,0:T(8,128)} %in_ref.4), custom_call_target="tpu_custom_call" | custom-call | bytes 4194304 | tf_op jit(solution)/shard_map/order_panel/pallas_call | solution.py:46
  16.0 3.3 %collective-permute-start = (f32[4,128,256]{2,1,0:T(8,128)S(1)}, f32[4,128,256]{2,1,0:T(8,128)}, u32[]{:S(2)}, u32[]{:S(2)}) collective-permute-start(f32[4,128,256]{2,1,0:T(8,128)S(1)} %slice.54), channel_id=1, source_target_pairs={{128,0},{0,128},{129,1},{1,129},{130,2},{2,130},{131,3},{3,131},{1... | collective-permute-start | bytes 1572872 | tf_op jit(solution)/shard_map/ppermute | solution.py:206
  19.3 3.5 %order_slab.1 = (f32[3,256,128]{2,1,0:T(8,128)}, f32[7,256,128]{2,1,0:T(8,128)}, f32[5,256,128]{2,1,0:T(8,128)}, f32[5,256,128]{2,1,0:T(8,128)}) custom-call(s32[20]{0:T(128)} %pad_add_fusion.1.index_ref, f32[256,4096]{1,0:T(8,128)} %own_ref.3), custom_call_target="tpu_custom_call" | custom-call | bytes 5242880 | tf_op jit(solution)/shard_map/order_slab/pallas_call | solution.py:46
  22.8 1.4 collective-permute-start.1
  24.7 30.8 %collective-permute-done.1.one_ref = f32[3,256,128]{2,1,0:T(8,128)S(1)} collective-permute-done((f32[3,256,128]{2,1,0:T(8,128)}, f32[3,256,128]{2,1,0:T(8,128)S(1)}, u32[]{:S(2)}, u32[]{:S(2)}) %collective-permute-start.1) | collective-permute-done | bytes 393248 | tf_op jit(solution)/shard_map/ppermute | solution.py:206
  55.6 1.4 copy-done.8
  56.9 3.3 %order_planes.2 = f32[16,128,256]{2,1,0:T(8,128)} custom-call(s32[16]{0:T(128)} %multiply_add_fusion.index_ref, f32[2048,256]{1,0:T(8,128)} %bitcast.38), custom_call_target="tpu_custom_call" | custom-call | bytes 4194304 | tf_op jit(solution)/shard_map/order_planes/pallas_call | solution.py:46
  60.2 8.5 %all-to-all-start.1 = ((f32[8,256,256]{2,1,0:T(8,128)}), f32[8,256,256]{2,1,0:T(8,128)S(1)}, u32[]{:S(2)}, u32[]{:S(2)}) async-start(f32[8,256,256]{2,1,0:T(8,128)} %bitcast.37), calls=%async_computation.1 | async-start | bytes 4194304 | tf_op jit(solution)/shard_map/all_to_all | solution.py:221
  68.7 2.7 %collective-permute-start.3 = (f32[4,128,256]{2,1,0:T(8,128)S(1)}, f32[4,128,256]{2,1,0:T(8,128)S(1)}, u32[]{:S(2)}, u32[]{:S(2)}) collective-permute-start(f32[4,128,256]{2,1,0:T(8,128)S(1)} %slice.55), channel_id=1, source_target_pairs={{128,0},{0,128},{129,1},{1,129},{130,2},{2,130},{131,3},{3,131},{1... | collective-permute-start | bytes 1572872 | tf_op jit(solution)/shard_map/ppermute | solution.py:206
  71.4 12.4 %collective-permute-done.3.refs_3_ = f32[4,128,256]{2,1,0:T(8,128)S(1)} collective-permute-done((f32[4,128,256]{2,1,0:T(8,128)S(1)}, f32[4,128,256]{2,1,0:T(8,128)S(1)}, u32[]{:S(2)}, u32[]{:S(2)}) %collective-permute-start.3) | collective-permute-done | bytes 524320 | tf_op jit(solution)/shard_map/ppermute | solution.py:206
  86.3 3.2 %order_distance.1 = (f32[4,128,256]{2,1,0:T(8,128)}, f32[4,128,256]{2,1,0:T(8,128)}, f32[4,128,256]{2,1,0:T(8,128)}, f32[4,128,256]{2,1,0:T(8,128)}) custom-call(s32[16]{0:T(128)} %iota.29.index_ref, f32[8,128,256]{2,1,0:T(8,128)} %get-tuple-element.53.refs_0_, f32[4,128,256]{2,1,0:T(8,128)} %collective-permute-done.refs_1_, f32[8,128,256]{2,1,0:T(8,128)} %copy-done.9, ...), custom_call_target="tpu_custom_call" | custom-call | bytes 4194304 | tf_op jit(solution)/shard_map/order_distance/pallas_call | solution.py:93
  89.6 1.5 collective-permute-start.4
  91.0 2.7 %collective-permute-start.5 = (f32[4,128,256]{2,1,0:T(8,128)}, f32[4,128,256]{2,1,0:T(8,128)}, u32[]{:S(2)}, u32[]{:S(2)}) collective-permute-start(f32[4,128,256]{2,1,0:T(8,128)} %get-tuple-element.72), channel_id=1, source_target_pairs={{64,0},{96,32},{0,64},{32,96},{65,1},{97,33},{1,65},{33,97},{66,2}... | collective-permute-start | bytes 1572872 | tf_op jit(solution)/shard_map/ppermute | solution.py:206
  93.7 1.5 collective-permute-start.6
  95.8 10.0 %collective-permute-done.4.refs_1_ = f32[4,128,256]{2,1,0:T(8,128)S(1)} collective-permute-done((f32[4,128,256]{2,1,0:T(8,128)}, f32[4,128,256]{2,1,0:T(8,128)S(1)}, u32[]{:S(2)}, u32[]{:S(2)}) %collective-permute-start.4) | collective-permute-done | bytes 524320 | tf_op jit(solution)/shard_map/ppermute | solution.py:206
  105.7 9.2 %collective-permute-done.5.refs_2_ = f32[4,128,256]{2,1,0:T(8,128)} collective-permute-done((f32[4,128,256]{2,1,0:T(8,128)}, f32[4,128,256]{2,1,0:T(8,128)}, u32[]{:S(2)}, u32[]{:S(2)}) %collective-permute-start.5) | collective-permute-done | bytes 524320 | tf_op jit(solution)/shard_map/ppermute | solution.py:206
  115.1 3.3 %order_planes.3 = f32[16,128,256]{2,1,0:T(8,128)} custom-call(s32[16]{0:T(128)} %xor_add_fusion.index_ref, f32[4,128,256]{2,1,0:T(8,128)} %get-tuple-element.70.refs_0_, f32[4,128,256]{2,1,0:T(8,128)} %copy-done.10, f32[4,128,256]{2,1,0:T(8,128)} %collective-permute-done.5.refs_2_, f32[4,128,256]{2,1,0:T(8,128)} %collective-permute-done.6.refs_3_), custom_call_target="tpu_custom_call" | custom-call | bytes 4194304 | tf_op jit(solution)/shard_map/order_planes/pallas_call | solution.py:93
  120.1 6.6 %all-to-all-start.2 = ((f32[8,256,256]{2,1,0:T(8,128)}), f32[8,256,256]{2,1,0:T(8,128)}, u32[]{:S(2)}, u32[]{:S(2)}) async-start(f32[8,256,256]{2,1,0:T(8,128)} %bitcast.36), calls=%async_computation.2 | async-start | bytes 4194304 | tf_op jit(solution)/shard_map/all_to_all | solution.py:221
  127.8 4.2 %collective-permute-start.10 = (f32[4,256,256]{2,1,0:T(8,128)}, f32[4,256,256]{2,1,0:T(8,128)S(1)}, u32[]{:S(2)}, u32[]{:S(2)}) collective-permute-start(f32[4,256,256]{2,1,0:T(8,128)} %slice.56), channel_id=1, source_target_pairs={{0,240},{16,32},{32,16},{48,64},{64,48},{80,96},{96,80},{112,128},... | collective-permute-start | bytes 3145736 | tf_op jit(solution)/shard_map/ppermute | solution.py:215
  133.2 1.3 copy-done.4
  134.5 1.9 collective-permute-start.12
  136.5 2.2 copy-done
  139.9 1.5 split_slab.2
  141.4 9.9 %collective-permute-done.10.refs_2_ = f32[4,256,256]{2,1,0:T(8,128)S(1)} collective-permute-done((f32[4,256,256]{2,1,0:T(8,128)}, f32[4,256,256]{2,1,0:T(8,128)S(1)}, u32[]{:S(2)}, u32[]{:S(2)}) %collective-permute-start.10) | collective-permute-done | bytes 1048608 | tf_op jit(solution)/shard_map/ppermute | solution.py:215
  151.2 6.1 %collective-permute-done.11.refs_3_ = f32[4,256,256]{2,1,0:T(8,128)} collective-permute-done((f32[4,256,256]{2,1,0:T(8,128)}, f32[4,256,256]{2,1,0:T(8,128)}, u32[]{:S(2)}, u32[]{:S(2)}) %collective-permute-start.11) | collective-permute-done | bytes 1048608 | tf_op jit(solution)/shard_map/ppermute | solution.py:216
  157.3 7.2 %products.4.refs_10_ = f32[8,256,256]{2,1,0:T(8,128)S(1)} custom-call(s32[11]{0:T(128)S(1)} %pad_add_fusion.place_ref, f32[8,256,256]{2,1,0:T(8,128)S(1)} %all-to-all-done.1.refs_0_, f32[8,256,256]{2,1,0:T(8,128)S(1)} %copy-done.5, f32[4,256,256]{2,1,0:T(8,128)S(1)} %collective-permute-done.10.refs_2_, f32[4,256,256]{2,1,0:T(8,128)} %collective-permute-done.11.refs_3_, ...), custom_call_target="tpu_custom_call" | custom-call | flops 2415919104 | bytes 12582912 | tf_op jit(solution)/shard_map/products/pallas_call | solution.py:187
  164.6 1.3 copy-done.2
  165.9 5.5 %collective-permute-done.12.two_ref = f32[5,256,128]{2,1,0:T(8,128)S(1)} collective-permute-done((f32[5,256,128]{2,1,0:T(8,128)}, f32[5,256,128]{2,1,0:T(8,128)S(1)}, u32[]{:S(2)}, u32[]{:S(2)}) %collective-permute-start.12) | collective-permute-done | bytes 655392 | tf_op jit(solution)/shard_map/ppermute | solution.py:206
  171.4 4.0 %split_slab.3 = (bf16[10,256,256]{2,1,0:T(8,128)(2,1)S(1)}, bf16[10,256,256]{2,1,0:T(8,128)(2,1)S(1)}) custom-call(s32[10]{0:T(128)S(1)} %get-tuple-element.110.index_ref, f32[256,4096]{1,0:T(8,128)S(1)} %copy-done.1, f32[5,256,128]{2,1,0:T(8,128)} %collective-permute-done.8.one_ref, f32[5,256,128]{2,1,0:T(8,128)S(1)} %collective-permute-done.12.two_ref), custom_call_target="tpu_custom_call" | custom-call | bytes 5242880 | tf_op jit(solution)/shard_map/split_slab/pallas_call | solution.py:122
  176.4 2.3 order_rest.1
  179.4 5.3 %collective-permute-start.20 = (f32[1,256,256]{2,1,0:T(8,128)S(1)}, f32[1,256,256]{2,1,0:T(8,128)S(1)}, u32[]{:S(2)}, u32[]{:S(2)}) collective-permute-start(f32[1,256,256]{2,1,0:T(8,128)S(1)} %slice.65), channel_id=1, source_target_pairs={{0,240},{16,32},{32,16},{48,64},{64,48},{80,96},{96,80},{112,128},... | collective-permute-start | bytes 786440 | tf_op jit(solution)/shard_map/ppermute | solution.py:215
  184.8 1.5 collective-permute-start.17
  186.4 1.3 collective-permute-start.18
  187.7 3.4 %collective-permute-done.20.refs_2_ = f32[1,256,256]{2,1,0:T(8,128)S(1)} collective-permute-done((f32[1,256,256]{2,1,0:T(8,128)S(1)}, f32[1,256,256]{2,1,0:T(8,128)S(1)}, u32[]{:S(2)}, u32[]{:S(2)}) %collective-permute-start.20) | collective-permute-done | bytes 262176 | tf_op jit(solution)/shard_map/ppermute | solution.py:215
  191.0 6.1 %collective-permute-done.21.refs_3_ = f32[1,256,256]{2,1,0:T(8,128)S(1)} collective-permute-done((f32[1,256,256]{2,1,0:T(8,128)S(1)}, f32[1,256,256]{2,1,0:T(8,128)S(1)}, u32[]{:S(2)}, u32[]{:S(2)}) %collective-permute-start.21) | collective-permute-done | bytes 262176 | tf_op jit(solution)/shard_map/ppermute | solution.py:216
  197.1 1.6 products.7
  198.9 2.0 collective-permute-start.25
  201.2 1.6 products.6
  202.8 2.4 %collective-permute-done.22 = f32[256,256]{1,0:T(8,128)S(1)} collective-permute-done((f32[256,256]{1,0:T(8,128)S(1)}, f32[256,256]{1,0:T(8,128)S(1)}, u32[]{:S(2)}, u32[]{:S(2)}) %collective-permute-start.22) | collective-permute-done | bytes 262176 | tf_op jit(solution)/shard_map/ppermute | solution.py:206
  205.2 1.3 collective-permute-done.25
  206.7 2.0 collective-permute-start.26
  208.7 9.5 %collective-permute-done.14.refs_2_ = f32[2,256,256]{2,1,0:T(8,128)S(1)} collective-permute-done((f32[2,256,256]{2,1,0:T(8,128)S(1)}, f32[2,256,256]{2,1,0:T(8,128)S(1)}, u32[]{:S(2)}, u32[]{:S(2)}) %collective-permute-start.14) | collective-permute-done | bytes 524320 | tf_op jit(solution)/shard_map/ppermute | solution.py:215
  218.8 2.6 %products.5 = f32[4,256,256]{2,1,0:T(8,128)S(1)} custom-call(s32[11]{0:T(128)S(1)} %pad_add_fusion.place_ref, f32[4,256,256]{2,1,0:T(8,128)S(1)} %get-tuple-element.93.refs_0_, f32[4,256,256]{2,1,0:T(8,128)S(1)} %collective-permute-done.13.refs_1_, f32[2,256,256]{2,1,0:T(8,128)S(1)} %collective-permute-done.14.refs_2_, ...), custom_call_target="tpu_custom_call" | custom-call | flops 1207959552 | bytes 6291456 | tf_op jit(solution)/shard_map/products/pallas_call | solution.py:187
  222.1 2.8 %collective-permute-start.24 = (f32[256,256]{1,0:T(8,128)S(1)}, f32[256,256]{1,0:T(8,128)S(1)}, u32[]{:S(2)}, u32[]{:S(2)}) collective-permute-start(f32[256,256]{1,0:T(8,128)S(1)} %get-tuple-element.99), channel_id=1, source_target_pairs={{1,0},{2,1},{3,2},{4,3},{5,4},{6,5},{7,6},{0,7},{9,8},{10,9},{11,1... | collective-permute-start | bytes 786440 | tf_op jit(solution)/shard_map/ppermute | solution.py:206
  224.8 5.7 %collective-permute-done.27 = f32[256,256]{1,0:T(8,128)S(1)} collective-permute-done((f32[256,256]{1,0:T(8,128)S(1)}, f32[256,256]{1,0:T(8,128)S(1)}, u32[]{:S(2)}, u32[]{:S(2)}) %collective-permute-start.27) | collective-permute-done | bytes 262176 | tf_op jit(solution)/shard_map/ppermute | solution.py:206
  230.7 7.6 %collective-permute-done.28 = f32[256,256]{1,0:T(8,128)S(1)} collective-permute-done((f32[256,256]{1,0:T(8,128)S(1)}, f32[256,256]{1,0:T(8,128)S(1)}, u32[]{:S(2)}, u32[]{:S(2)}) %collective-permute-start.28) | collective-permute-done | bytes 262176 | tf_op jit(solution)/shard_map/ppermute | solution.py:206
  (80 shorter events, 16.8 us)
Async XLA Ops:
  4.5 51.1 %all-to-all-start = ((f32[16,128,256]{2,1,0:T(8,128)}), f32[16,128,256]{2,1,0:T(8,128)S(1)}, u32[]{:S(2)}, u32[]{:S(2)}) async-start(f32[16,128,256]{2,1,0:T(8,128)} %order_panel.2), calls=%async_computation | async-start | bytes 4194304 | tf_op jit(solution)/shard_map/all_to_all | solution.py:221
  14.4 45.8 %collective-permute-start.2 = (f32[8,128,256]{2,1,0:T(8,128)}, f32[8,128,256]{2,1,0:T(8,128)S(1)}, u32[]{:S(2)}, u32[]{:S(2)}) collective-permute-start(f32[8,128,256]{2,1,0:T(8,128)} %get-tuple-element.62), channel_id=1, source_target_pairs={{0,16},{16,0},{32,48},{48,32},{64,80},{80,64},{96,112},{112,96},{1... | collective-permute-start | bytes 3145736 | tf_op jit(solution)/shard_map/ppermute | solution.py:210
  16.0 39.6 %collective-permute-start = (f32[4,128,256]{2,1,0:T(8,128)S(1)}, f32[4,128,256]{2,1,0:T(8,128)}, u32[]{:S(2)}, u32[]{:S(2)}) collective-permute-start(f32[4,128,256]{2,1,0:T(8,128)S(1)} %slice.54), channel_id=1, source_target_pairs={{128,0},{0,128},{129,1},{1,129},{130,2},{2,130},{131,3},{3,131},{1... | collective-permute-start | bytes 1572872 | tf_op jit(solution)/shard_map/ppermute | solution.py:206
  22.8 32.8 %collective-permute-start.1 = (f32[3,256,128]{2,1,0:T(8,128)}, f32[3,256,128]{2,1,0:T(8,128)S(1)}, u32[]{:S(2)}, u32[]{:S(2)}) collective-permute-start(f32[3,256,128]{2,1,0:T(8,128)} %get-tuple-element.57), channel_id=1, source_target_pairs={{8,0},{0,8},{9,1},{1,9},{10,2},{2,10},{11,3},{3,11},{12,4},{4,12},... | collective-permute-start | bytes 1179656 | tf_op jit(solution)/shard_map/ppermute | solution.py:206
  55.6 1.4 copy-start.8
  60.2 8.5 %copy-start.9 = (f32[8,128,256]{2,1,0:T(8,128)}, f32[8,128,256]{2,1,0:T(8,128)S(1)}, u32[]{:S(2)}) copy-start(f32[8,128,256]{2,1,0:T(8,128)S(1)} %collective-permute-done.2.refs_2_) | copy-start | bytes 3145732
  60.2 59.8 %all-to-all-start.1 = ((f32[8,256,256]{2,1,0:T(8,128)}), f32[8,256,256]{2,1,0:T(8,128)S(1)}, u32[]{:S(2)}, u32[]{:S(2)}) async-start(f32[8,256,256]{2,1,0:T(8,128)} %bitcast.37), calls=%async_computation.1 | async-start | bytes 4194304 | tf_op jit(solution)/shard_map/all_to_all | solution.py:221
  68.7 15.1 %collective-permute-start.3 = (f32[4,128,256]{2,1,0:T(8,128)S(1)}, f32[4,128,256]{2,1,0:T(8,128)S(1)}, u32[]{:S(2)}, u32[]{:S(2)}) collective-permute-start(f32[4,128,256]{2,1,0:T(8,128)S(1)} %slice.55), channel_id=1, source_target_pairs={{128,0},{0,128},{129,1},{1,129},{130,2},{2,130},{131,3},{3,131},{1... | collective-permute-start | bytes 1572872 | tf_op jit(solution)/shard_map/ppermute | solution.py:206
  83.8 2.5 %copy-start.11 = (f32[4,128,256]{2,1,0:T(8,128)}, f32[4,128,256]{2,1,0:T(8,128)S(1)}, u32[]{:S(2)}) copy-start(f32[4,128,256]{2,1,0:T(8,128)S(1)} %collective-permute-done.3.refs_3_) | copy-start | bytes 1572868
  83.8 35.4 %collective-permute-start.7 = (f32[7,256,128]{2,1,0:T(8,128)}, f32[7,256,128]{2,1,0:T(8,128)S(1)}, u32[]{:S(2)}, u32[]{:S(2)}) collective-permute-start(f32[7,256,128]{2,1,0:T(8,128)} %get-tuple-element.76), channel_id=1, source_target_pairs={{8,0},{0,8},{9,1},{1,9},{10,2},{2,10},{11,3},{3,11},{12,4},{4,12},... | collective-permute-start | bytes 2752520 | tf_op jit(solution)/shard_map/ppermute | solution.py:206
  84.7 34.4 %collective-permute-start.8 = (f32[5,256,128]{2,1,0:T(8,128)}, f32[5,256,128]{2,1,0:T(8,128)}, u32[]{:S(2)}, u32[]{:S(2)}) collective-permute-start(f32[5,256,128]{2,1,0:T(8,128)} %get-tuple-element.77), channel_id=1, source_target_pairs={{8,0},{0,8},{9,1},{1,9},{10,2},{2,10},{11,3},{3,11},{12,4},{4,12},... | collective-permute-start | bytes 1966088 | tf_op jit(solution)/shard_map/ppermute | solution.py:206
  89.6 16.1 %collective-permute-start.4 = (f32[4,128,256]{2,1,0:T(8,128)}, f32[4,128,256]{2,1,0:T(8,128)S(1)}, u32[]{:S(2)}, u32[]{:S(2)}) collective-permute-start(f32[4,128,256]{2,1,0:T(8,128)} %get-tuple-element.71), channel_id=1, source_target_pairs={{96,0},{0,32},{32,64},{64,96},{97,1},{1,33},{33,65},{65,97},{98,2}... | collective-permute-start | bytes 1572872 | tf_op jit(solution)/shard_map/ppermute | solution.py:206
  91.0 23.9 %collective-permute-start.5 = (f32[4,128,256]{2,1,0:T(8,128)}, f32[4,128,256]{2,1,0:T(8,128)}, u32[]{:S(2)}, u32[]{:S(2)}) collective-permute-start(f32[4,128,256]{2,1,0:T(8,128)} %get-tuple-element.72), channel_id=1, source_target_pairs={{64,0},{96,32},{0,64},{32,96},{65,1},{97,33},{1,65},{33,97},{66,2}... | collective-permute-start | bytes 1572872 | tf_op jit(solution)/shard_map/ppermute | solution.py:206
  93.7 21.3 %collective-permute-start.6 = (f32[4,128,256]{2,1,0:T(8,128)}, f32[4,128,256]{2,1,0:T(8,128)}, u32[]{:S(2)}, u32[]{:S(2)}) collective-permute-start(f32[4,128,256]{2,1,0:T(8,128)} %get-tuple-element.73), channel_id=1, source_target_pairs={{32,0},{64,32},{96,64},{0,96},{33,1},{65,33},{97,65},{1,97},{34,2}... | collective-permute-start | bytes 1572872 | tf_op jit(solution)/shard_map/ppermute | solution.py:206
  105.7 9.3 %copy-start.10 = (f32[4,128,256]{2,1,0:T(8,128)}, f32[4,128,256]{2,1,0:T(8,128)S(1)}, u32[]{:S(2)}) copy-start(f32[4,128,256]{2,1,0:T(8,128)S(1)} %collective-permute-done.4.refs_1_) | copy-start | bytes 1572868
  119.2 0.9 copy-start.6
  120.1 56.3 %all-to-all-start.2 = ((f32[8,256,256]{2,1,0:T(8,128)}), f32[8,256,256]{2,1,0:T(8,128)}, u32[]{:S(2)}, u32[]{:S(2)}) async-start(f32[8,256,256]{2,1,0:T(8,128)} %bitcast.36), calls=%async_computation.2 | async-start | bytes 4194304 | tf_op jit(solution)/shard_map/all_to_all | solution.py:221
  126.7 9.7 %copy-start.12 = (s32[8]{0:T(128)S(1)}, s32[8]{0:T(128)}, u32[]{:S(2)}) copy-start(s32[8]{0:T(128)} %constant.162.clone) | copy-start | bytes 100
  126.7 5.4 %collective-permute-start.9 = (f32[8,256,256]{2,1,0:T(8,128)S(1)}, f32[8,256,256]{2,1,0:T(8,128)S(1)}, u32[]{:S(2)}, u32[]{:S(2)}) collective-permute-start(f32[8,256,256]{2,1,0:T(8,128)S(1)} %all-to-all-done.1.refs_0_), channel_id=1, source_target_pairs={{0,16},{16,0},{32,48},{48,32},{64,80},{80,64},{96,112},{112,96},{1... | collective-permute-start | bytes 6291464 | tf_op jit(solution)/shard_map/ppermute | solution.py:210
  127.8 23.4 %collective-permute-start.10 = (f32[4,256,256]{2,1,0:T(8,128)}, f32[4,256,256]{2,1,0:T(8,128)S(1)}, u32[]{:S(2)}, u32[]{:S(2)}) collective-permute-start(f32[4,256,256]{2,1,0:T(8,128)} %slice.56), channel_id=1, source_target_pairs={{0,240},{16,32},{32,16},{48,64},{64,48},{80,96},{96,80},{112,128},... | collective-permute-start | bytes 3145736 | tf_op jit(solution)/shard_map/ppermute | solution.py:215
  133.2 1.3 copy-start.4
  134.5 22.8 %collective-permute-start.11 = (f32[4,256,256]{2,1,0:T(8,128)}, f32[4,256,256]{2,1,0:T(8,128)}, u32[]{:S(2)}, u32[]{:S(2)}) collective-permute-start(f32[4,256,256]{2,1,0:T(8,128)} %slice.72), channel_id=1, source_target_pairs={{0,32},{16,240},{32,64},{48,16},{64,96},{80,48},{96,128},{112,80},... | collective-permute-start | bytes 3145736 | tf_op jit(solution)/shard_map/ppermute | solution.py:216
  134.5 36.9 %collective-permute-start.12 = (f32[5,256,128]{2,1,0:T(8,128)}, f32[5,256,128]{2,1,0:T(8,128)S(1)}, u32[]{:S(2)}, u32[]{:S(2)}) collective-permute-start(f32[5,256,128]{2,1,0:T(8,128)} %get-tuple-element.86), channel_id=1, source_target_pairs={{8,0},{0,8},{9,1},{1,9},{10,2},{2,10},{11,3},{3,11},{12,4},{4,12},... | collective-permute-start | bytes 1966088 | tf_op jit(solution)/shard_map/ppermute | solution.py:206
  136.5 2.2 copy-start
  138.7 1.2 copy-start.7
  139.9 17.4 %copy-start.5 = (f32[8,256,256]{2,1,0:T(8,128)S(1)}, f32[8,256,256]{2,1,0:T(8,128)}, u32[]{:S(2)}) copy-start(f32[8,256,256]{2,1,0:T(8,128)} %copy-done.4) | copy-start | bytes 6291460
  157.3 14.1 %copy-start.1 = (f32[256,4096]{1,0:T(8,128)S(1)}, f32[256,4096]{1,0:T(8,128)}, u32[]{:S(2)}) copy-start(f32[256,4096]{1,0:T(8,128)} %own_ref.3) | copy-start | bytes 12582916
  164.6 1.3 copy-start.2
  176.4 20.8 %copy-start.3 = (f32[8,256,256]{2,1,0:T(8,128)S(1)}, f32[8,256,256]{2,1,0:T(8,128)}, u32[]{:S(2)}) copy-start(f32[8,256,256]{2,1,0:T(8,128)} %copy-done.2) | copy-start | bytes 6291460
  178.7 6.0 %collective-permute-start.19 = (f32[2,256,256]{2,1,0:T(8,128)S(1)}, f32[2,256,256]{2,1,0:T(8,128)S(1)}, u32[]{:S(2)}, u32[]{:S(2)}) collective-permute-start(f32[2,256,256]{2,1,0:T(8,128)S(1)} %get-tuple-element.98.refs_0_), channel_id=1, source_target_pairs={{0,16},{16,0},{32,48},{48,32},{64,80},{80,64},{96,112},{112,96},{1... | collective-permute-start | bytes 1572872 | tf_op jit(solution)/shard_map/ppermute | solution.py:210
  178.8 22.1 %collective-permute-start.13 = (f32[4,256,256]{2,1,0:T(8,128)S(1)}, f32[4,256,256]{2,1,0:T(8,128)S(1)}, u32[]{:S(2)}, u32[]{:S(2)}) collective-permute-start(f32[4,256,256]{2,1,0:T(8,128)S(1)} %get-tuple-element.93.refs_0_), channel_id=1, source_target_pairs={{0,16},{16,0},{32,48},{48,32},{64,80},{80,64},{96,112},{112,96},{1... | collective-permute-start | bytes 3145736 | tf_op jit(solution)/shard_map/ppermute | solution.py:210
  179.3 7.1 %collective-permute-start.16 = (f32[2,256,256]{2,1,0:T(8,128)S(1)}, f32[2,256,256]{2,1,0:T(8,128)S(1)}, u32[]{:S(2)}, u32[]{:S(2)}) collective-permute-start(f32[2,256,256]{2,1,0:T(8,128)S(1)} %get-tuple-element.97.refs_0_), channel_id=1, source_target_pairs={{0,16},{16,0},{32,48},{48,32},{64,80},{80,64},{96,112},{112,96},{1... | collective-permute-start | bytes 1572872 | tf_op jit(solution)/shard_map/ppermute | solution.py:210
  179.4 11.6 %collective-permute-start.20 = (f32[1,256,256]{2,1,0:T(8,128)S(1)}, f32[1,256,256]{2,1,0:T(8,128)S(1)}, u32[]{:S(2)}, u32[]{:S(2)}) collective-permute-start(f32[1,256,256]{2,1,0:T(8,128)S(1)} %slice.65), channel_id=1, source_target_pairs={{0,240},{16,32},{32,16},{48,64},{64,48},{80,96},{96,80},{112,128},... | collective-permute-start | bytes 786440 | tf_op jit(solution)/shard_map/ppermute | solution.py:215
  184.7 12.4 %collective-permute-start.21 = (f32[1,256,256]{2,1,0:T(8,128)S(1)}, f32[1,256,256]{2,1,0:T(8,128)S(1)}, u32[]{:S(2)}, u32[]{:S(2)}) collective-permute-start(f32[1,256,256]{2,1,0:T(8,128)S(1)} %slice.78), channel_id=1, source_target_pairs={{0,32},{16,240},{32,64},{48,16},{64,96},{80,48},{96,128},{112,80},... | collective-permute-start | bytes 786440 | tf_op jit(solution)/shard_map/ppermute | solution.py:216
  184.8 16.2 %collective-permute-start.17 = (f32[1,256,256]{2,1,0:T(8,128)S(1)}, f32[1,256,256]{2,1,0:T(8,128)S(1)}, u32[]{:S(2)}, u32[]{:S(2)}) collective-permute-start(f32[1,256,256]{2,1,0:T(8,128)S(1)} %slice.62), channel_id=1, source_target_pairs={{0,240},{16,32},{32,16},{48,64},{64,48},{80,96},{96,80},{112,128},... | collective-permute-start | bytes 786440 | tf_op jit(solution)/shard_map/ppermute | solution.py:215
  186.4 14.8 %collective-permute-start.18 = (f32[1,256,256]{2,1,0:T(8,128)S(1)}, f32[1,256,256]{2,1,0:T(8,128)S(1)}, u32[]{:S(2)}, u32[]{:S(2)}) collective-permute-start(f32[1,256,256]{2,1,0:T(8,128)S(1)} %slice.76), channel_id=1, source_target_pairs={{0,32},{16,240},{32,64},{48,16},{64,96},{80,48},{96,128},{112,80},... | collective-permute-start | bytes 786440 | tf_op jit(solution)/shard_map/ppermute | solution.py:216
  198.8 6.5 %collective-permute-start.22 = (f32[256,256]{1,0:T(8,128)S(1)}, f32[256,256]{1,0:T(8,128)S(1)}, u32[]{:S(2)}, u32[]{:S(2)}) collective-permute-start(f32[256,256]{1,0:T(8,128)S(1)} %get-tuple-element.103), channel_id=1, source_target_pairs={{1,0},{2,1},{3,2},{4,3},{5,4},{6,5},{7,6},{0,7},{9,8},{10,9},{11,1... | collective-permute-start | bytes 786440 | tf_op jit(solution)/shard_map/ppermute | solution.py:206
  198.9 7.7 %collective-permute-start.25 = (f32[256,256]{1,0:T(8,128)S(1)}, f32[256,256]{1,0:T(8,128)S(1)}, u32[]{:S(2)}, u32[]{:S(2)}) collective-permute-start(f32[256,256]{1,0:T(8,128)S(1)} %get-tuple-element.104), channel_id=1, source_target_pairs={{7,0},{0,1},{1,2},{2,3},{3,4},{4,5},{5,6},{6,7},{15,8},{8,9},{9,10... | collective-permute-start | bytes 786440 | tf_op jit(solution)/shard_map/ppermute | solution.py:206
  200.9 17.2 %collective-permute-start.14 = (f32[2,256,256]{2,1,0:T(8,128)S(1)}, f32[2,256,256]{2,1,0:T(8,128)S(1)}, u32[]{:S(2)}, u32[]{:S(2)}) collective-permute-start(f32[2,256,256]{2,1,0:T(8,128)S(1)} %slice.58), channel_id=1, source_target_pairs={{0,240},{16,32},{32,16},{48,64},{64,48},{80,96},{96,80},{112,128},... | collective-permute-start | bytes 1572872 | tf_op jit(solution)/shard_map/ppermute | solution.py:215
  201.1 17.8 %collective-permute-start.15 = (f32[2,256,256]{2,1,0:T(8,128)S(1)}, f32[2,256,256]{2,1,0:T(8,128)S(1)}, u32[]{:S(2)}, u32[]{:S(2)}) collective-permute-start(f32[2,256,256]{2,1,0:T(8,128)S(1)} %slice.73), channel_id=1, source_target_pairs={{0,32},{16,240},{32,64},{48,16},{64,96},{80,48},{96,128},{112,80},... | collective-permute-start | bytes 1572872 | tf_op jit(solution)/shard_map/ppermute | solution.py:216
  206.6 14.8 %collective-permute-start.23 = (f32[256,256]{1,0:T(8,128)S(1)}, f32[256,256]{1,0:T(8,128)S(1)}, u32[]{:S(2)}, u32[]{:S(2)}) collective-permute-start(f32[256,256]{1,0:T(8,128)S(1)} %get-tuple-element.101), channel_id=1, source_target_pairs={{1,0},{2,1},{3,2},{4,3},{5,4},{6,5},{7,6},{0,7},{9,8},{10,9},{11,1... | collective-permute-start | bytes 786440 | tf_op jit(solution)/shard_map/ppermute | solution.py:206
  206.7 14.8 %collective-permute-start.26 = (f32[256,256]{1,0:T(8,128)S(1)}, f32[256,256]{1,0:T(8,128)S(1)}, u32[]{:S(2)}, u32[]{:S(2)}) collective-permute-start(f32[256,256]{1,0:T(8,128)S(1)} %get-tuple-element.102), channel_id=1, source_target_pairs={{7,0},{0,1},{1,2},{2,3},{3,4},{4,5},{5,6},{6,7},{15,8},{8,9},{9,10... | collective-permute-start | bytes 786440 | tf_op jit(solution)/shard_map/ppermute | solution.py:206
  221.5 9.0 %collective-permute-start.27 = (f32[256,256]{1,0:T(8,128)S(1)}, f32[256,256]{1,0:T(8,128)S(1)}, u32[]{:S(2)}, u32[]{:S(2)}) collective-permute-start(f32[256,256]{1,0:T(8,128)S(1)} %get-tuple-element.100), channel_id=1, source_target_pairs={{7,0},{0,1},{1,2},{2,3},{3,4},{4,5},{5,6},{6,7},{15,8},{8,9},{9,10... | collective-permute-start | bytes 786440 | tf_op jit(solution)/shard_map/ppermute | solution.py:206
  222.1 8.6 %collective-permute-start.24 = (f32[256,256]{1,0:T(8,128)S(1)}, f32[256,256]{1,0:T(8,128)S(1)}, u32[]{:S(2)}, u32[]{:S(2)}) collective-permute-start(f32[256,256]{1,0:T(8,128)S(1)} %get-tuple-element.99), channel_id=1, source_target_pairs={{1,0},{2,1},{3,2},{4,3},{5,4},{6,5},{7,6},{0,7},{9,8},{10,9},{11,1... | collective-permute-start | bytes 786440 | tf_op jit(solution)/shard_map/ppermute | solution.py:206
  230.6 7.7 %collective-permute-start.28 = (f32[256,256]{1,0:T(8,128)S(1)}, f32[256,256]{1,0:T(8,128)S(1)}, u32[]{:S(2)}, u32[]{:S(2)}) collective-permute-start(f32[256,256]{1,0:T(8,128)S(1)} %fusion.2), channel_id=1, source_target_pairs={{7,0},{0,1},{1,2},{2,3},{3,4},{4,5},{5,6},{6,7},{15,8},{8,9},{9,10... | collective-permute-start | bytes 786440 | tf_op jit(solution)/shard_map/ppermute | solution.py:206

commit v5 on v4

--- a/solution.py
+++ b/solution.py
@@ -13,7 +13,7 @@
 ROW, COL = AXES[:3], AXES[3:]
 WINDOW = 3
 OFFSETS = (4, -3, 3, -2, 2, -1, 1, 0)
-GROUPS = (2, 2, 4)
+GROUPS = (2, 2, 2, 2)
 EARLY = 3
 LATE = 5
 LARGE = 60 * 2**20

time: 240 us -> 239 us (level); the launches traced: 239 us -> 236 us
  waiting for transfers between devices: 123 us -> 109 us
  starting transfers between devices: 59.6 us -> 69.5 us
    ppermute x4 -> x5, waiting for transfers between devices: 22.7 us -> 11 us  [to_next_chips(): lax.ppermute(own, ROW, [(i, (i + (1 if i % 2 else -1)) % n) for i in rang...]
    ppermute x4 -> x5, starting transfers between devices: 11.1 us -> 17.4 us  [to_next_chips(): lax.ppermute(own, ROW, [(i, (i + (1 if i % 2 else -1)) % n) for i in rang...]
    ppermute x16, waiting for transfers between devices: 85.8 us -> 80.1 us  [shifted(): lax.ppermute(block, axes, [((i - distance) % n, i) for i in range(n)])]
    ppermute x4 -> x5, waiting for transfers between devices: 12.9 us -> 16.4 us  [to_next_chips(): lax.ppermute(other, ROW, [(i, (i + (-2 if i % 2 else 2)) % n) for i in ra...]
    ppermute x16, starting transfers between devices: 24.5 us -> 27.1 us  [shifted(): lax.ppermute(block, axes, [((i - distance) % n, i) for i in range(n)])]
    pallas_call x4 -> x5, Pallas kernels: 13 us -> 13.6 us  [products(): pl.pallas_call(functools.partial(product_body, cut, first, ordered, start...]
  transfers between devices with their start and end apart: 32 -> 35, of which waited for: 19 -> 22; matrix products, arithmetic and copies ran while one was open for 2% -> 2% of each run, Pallas kernels for 15% -> 15%
where the time goes in v5:
time: 239 us; the launch traced here: 236 us
  waiting for transfers between devices  109 us (46%)
  starting transfers between devices  69.5 us (29%)
  Pallas kernels  41.2 us (17%)
  local copies, waits for them, and re-layouts  11.6 us (5%)
  other arithmetic  3.71 us (2%)
    ppermute x16, waiting for transfers between devices, shifted(): lax.ppermute(block, axes, [((i - distance) % n, i) for i in range(n)])  80.1 us
    ppermute x16, starting transfers between devices, shifted(): lax.ppermute(block, axes, [((i - distance) % n, i) for i in range(n)])  27.1 us
    all_to_all x3, starting transfers between devices, exchange(): return lax.all_to_all(block, axes, split_axis=0, concat_axis=0, tiled=True)  21.2 us
    ppermute x5, starting transfers between devices, to_next_chips(): lax.ppermute(own, ROW, [(i, (i + (1 if i % 2 else -1)) % n) for i in rang...  17.4 us
    ppermute x5, waiting for transfers between devices, to_next_chips(): lax.ppermute(other, ROW, [(i, (i + (-2 if i % 2 else 2)) % n) for i in ra...  16.4 us
    pallas_call x5, Pallas kernels, order_blocks(): pl.pallas_call(functools.partial(order_body, along), in_specs=[pl.BlockSp...  15.7 us
    pallas_call x5, Pallas kernels, products(): pl.pallas_call(functools.partial(product_body, cut, first, ordered, start...  13.6 us
    ppermute x5, waiting for transfers between devices, to_next_chips(): lax.ppermute(own, ROW, [(i, (i + (1 if i % 2 else -1)) % n) for i in rang...  11 us
  transfers between devices with their start and end apart: 35, of which 22 were waited for; matrix products, arithmetic and copies ran while one was open for 2% of the time, Pallas kernels for 15%

profile of v5, /device:TPU:8, one launch (start us, length us, event | category | flops | bytes accessed | tf_op | source)
XLA Modules:
  0.0 235.6 jit_solution(7278394381956359755)
XLA Ops:
  0.5 3.3 %order_panel.2 = f32[16,128,256]{2,1,0:T(8,128)} custom-call(s32[16]{0:T(128)} %get-tuple-element.108.index_ref, f32[4096,256]{1,0:T(8,128)} %in_ref.4), custom_call_target="tpu_custom_call" | custom-call | bytes 4194304 | tf_op jit(solution)/shard_map/order_panel/pallas_call | solution.py:46
  4.4 6.1 %all-to-all-start = ((f32[16,128,256]{2,1,0:T(8,128)}), f32[16,128,256]{2,1,0:T(8,128)S(1)}, u32[]{:S(2)}, u32[]{:S(2)}) async-start(f32[16,128,256]{2,1,0:T(8,128)} %order_panel.2), calls=%async_computation | async-start | bytes 4194304 | tf_op jit(solution)/shard_map/all_to_all | solution.py:221
  11.1 3.3 %order_panel.3 = (f32[8,128,256]{2,1,0:T(8,128)}, f32[8,128,256]{2,1,0:T(8,128)}) custom-call(s32[16]{0:T(128)} %multiply_add_fusion.1.index_ref, f32[4096,256]{1,0:T(8,128)} %in_ref.4), custom_call_target="tpu_custom_call" | custom-call | bytes 4194304 | tf_op jit(solution)/shard_map/order_panel/pallas_call | solution.py:46
  15.9 3.3 %collective-permute-start = (f32[4,128,256]{2,1,0:T(8,128)S(1)}, f32[4,128,256]{2,1,0:T(8,128)}, u32[]{:S(2)}, u32[]{:S(2)}) collective-permute-start(f32[4,128,256]{2,1,0:T(8,128)S(1)} %slice.60), channel_id=1, source_target_pairs={{128,0},{0,128},{129,1},{1,129},{130,2},{2,130},{131,3},{3,131},{1... | collective-permute-start | bytes 1572872 | tf_op jit(solution)/shard_map/ppermute | solution.py:206
  19.2 3.5 %order_slab.1 = (f32[3,256,128]{2,1,0:T(8,128)}, f32[7,256,128]{2,1,0:T(8,128)}, f32[5,256,128]{2,1,0:T(8,128)}, f32[5,256,128]{2,1,0:T(8,128)}) custom-call(s32[20]{0:T(128)} %pad_add_fusion.1.index_ref, f32[256,4096]{1,0:T(8,128)} %own_ref.3), custom_call_target="tpu_custom_call" | custom-call | bytes 5242880 | tf_op jit(solution)/shard_map/order_slab/pallas_call | solution.py:46
  22.7 1.4 collective-permute-start.1
  24.7 30.8 %collective-permute-done.1.one_ref = f32[3,256,128]{2,1,0:T(8,128)S(1)} collective-permute-done((f32[3,256,128]{2,1,0:T(8,128)}, f32[3,256,128]{2,1,0:T(8,128)S(1)}, u32[]{:S(2)}, u32[]{:S(2)}) %collective-permute-start.1) | collective-permute-done | bytes 393248 | tf_op jit(solution)/shard_map/ppermute | solution.py:206
  55.5 1.4 copy-done.8
  56.9 3.3 %order_planes.2 = f32[16,128,256]{2,1,0:T(8,128)} custom-call(s32[16]{0:T(128)} %multiply_add_fusion.index_ref, f32[2048,256]{1,0:T(8,128)} %bitcast.38), custom_call_target="tpu_custom_call" | custom-call | bytes 4194304 | tf_op jit(solution)/shard_map/order_planes/pallas_call | solution.py:46
  60.2 8.5 %all-to-all-start.1 = ((f32[8,256,256]{2,1,0:T(8,128)}), f32[8,256,256]{2,1,0:T(8,128)S(1)}, u32[]{:S(2)}, u32[]{:S(2)}) async-start(f32[8,256,256]{2,1,0:T(8,128)} %bitcast.37), calls=%async_computation.1 | async-start | bytes 4194304 | tf_op jit(solution)/shard_map/all_to_all | solution.py:221
  68.7 2.7 %collective-permute-start.3 = (f32[4,128,256]{2,1,0:T(8,128)S(1)}, f32[4,128,256]{2,1,0:T(8,128)S(1)}, u32[]{:S(2)}, u32[]{:S(2)}) collective-permute-start(f32[4,128,256]{2,1,0:T(8,128)S(1)} %slice.61), channel_id=1, source_target_pairs={{128,0},{0,128},{129,1},{1,129},{130,2},{2,130},{131,3},{3,131},{1... | collective-permute-start | bytes 1572872 | tf_op jit(solution)/shard_map/ppermute | solution.py:206
  71.3 12.4 %collective-permute-done.3.refs_3_ = f32[4,128,256]{2,1,0:T(8,128)S(1)} collective-permute-done((f32[4,128,256]{2,1,0:T(8,128)S(1)}, f32[4,128,256]{2,1,0:T(8,128)S(1)}, u32[]{:S(2)}, u32[]{:S(2)}) %collective-permute-start.3) | collective-permute-done | bytes 524320 | tf_op jit(solution)/shard_map/ppermute | solution.py:206
  86.3 3.3 %order_distance.1 = (f32[4,128,256]{2,1,0:T(8,128)}, f32[4,128,256]{2,1,0:T(8,128)}, f32[4,128,256]{2,1,0:T(8,128)}, f32[4,128,256]{2,1,0:T(8,128)}) custom-call(s32[16]{0:T(128)} %iota.29.index_ref, f32[8,128,256]{2,1,0:T(8,128)} %get-tuple-element.54.refs_0_, f32[4,128,256]{2,1,0:T(8,128)} %collective-permute-done.refs_1_, f32[8,128,256]{2,1,0:T(8,128)} %copy-done.9, ...), custom_call_target="tpu_custom_call" | custom-call | bytes 4194304 | tf_op jit(solution)/shard_map/order_distance/pallas_call | solution.py:93
  89.6 1.5 collective-permute-start.4
  91.0 2.7 %collective-permute-start.5 = (f32[4,128,256]{2,1,0:T(8,128)}, f32[4,128,256]{2,1,0:T(8,128)}, u32[]{:S(2)}, u32[]{:S(2)}) collective-permute-start(f32[4,128,256]{2,1,0:T(8,128)} %get-tuple-element.73), channel_id=1, source_target_pairs={{64,0},{96,32},{0,64},{32,96},{65,1},{97,33},{1,65},{33,97},{66,2}... | collective-permute-start | bytes 1572872 | tf_op jit(solution)/shard_map/ppermute | solution.py:206
  93.7 1.5 collective-permute-start.6
  95.7 10.0 %collective-permute-done.4.refs_1_ = f32[4,128,256]{2,1,0:T(8,128)S(1)} collective-permute-done((f32[4,128,256]{2,1,0:T(8,128)}, f32[4,128,256]{2,1,0:T(8,128)S(1)}, u32[]{:S(2)}, u32[]{:S(2)}) %collective-permute-start.4) | collective-permute-done | bytes 524320 | tf_op jit(solution)/shard_map/ppermute | solution.py:206
  105.7 9.2 %collective-permute-done.5.refs_2_ = f32[4,128,256]{2,1,0:T(8,128)} collective-permute-done((f32[4,128,256]{2,1,0:T(8,128)}, f32[4,128,256]{2,1,0:T(8,128)}, u32[]{:S(2)}, u32[]{:S(2)}) %collective-permute-start.5) | collective-permute-done | bytes 524320 | tf_op jit(solution)/shard_map/ppermute | solution.py:206
  115.0 3.3 %order_planes.3 = f32[16,128,256]{2,1,0:T(8,128)} custom-call(s32[16]{0:T(128)} %xor_add_fusion.index_ref, f32[4,128,256]{2,1,0:T(8,128)} %get-tuple-element.71.refs_0_, f32[4,128,256]{2,1,0:T(8,128)} %copy-done.10, f32[4,128,256]{2,1,0:T(8,128)} %collective-permute-done.5.refs_2_, f32[4,128,256]{2,1,0:T(8,128)} %collective-permute-done.6.refs_3_), custom_call_target="tpu_custom_call" | custom-call | bytes 4194304 | tf_op jit(solution)/shard_map/order_planes/pallas_call | solution.py:93
  120.0 6.6 %all-to-all-start.2 = ((f32[8,256,256]{2,1,0:T(8,128)}), f32[8,256,256]{2,1,0:T(8,128)}, u32[]{:S(2)}, u32[]{:S(2)}) async-start(f32[8,256,256]{2,1,0:T(8,128)} %bitcast.36), calls=%async_computation.2 | async-start | bytes 4194304 | tf_op jit(solution)/shard_map/all_to_all | solution.py:221
  127.8 4.2 %collective-permute-start.10 = (f32[4,256,256]{2,1,0:T(8,128)}, f32[4,256,256]{2,1,0:T(8,128)S(1)}, u32[]{:S(2)}, u32[]{:S(2)}) collective-permute-start(f32[4,256,256]{2,1,0:T(8,128)} %slice.62), channel_id=1, source_target_pairs={{0,240},{16,32},{32,16},{48,64},{64,48},{80,96},{96,80},{112,128},... | collective-permute-start | bytes 3145736 | tf_op jit(solution)/shard_map/ppermute | solution.py:215
  133.2 1.4 copy-done.4
  134.5 1.9 collective-permute-start.12
  136.5 2.2 copy-done.2
  139.9 1.5 split_slab.2
  141.4 9.8 %collective-permute-done.10.refs_2_ = f32[4,256,256]{2,1,0:T(8,128)S(1)} collective-permute-done((f32[4,256,256]{2,1,0:T(8,128)}, f32[4,256,256]{2,1,0:T(8,128)S(1)}, u32[]{:S(2)}, u32[]{:S(2)}) %collective-permute-start.10) | collective-permute-done | bytes 1048608 | tf_op jit(solution)/shard_map/ppermute | solution.py:215
  151.2 6.1 %collective-permute-done.11.refs_3_ = f32[4,256,256]{2,1,0:T(8,128)} collective-permute-done((f32[4,256,256]{2,1,0:T(8,128)}, f32[4,256,256]{2,1,0:T(8,128)}, u32[]{:S(2)}, u32[]{:S(2)}) %collective-permute-start.11) | collective-permute-done | bytes 1048608 | tf_op jit(solution)/shard_map/ppermute | solution.py:216
  157.3 7.2 %products.5.refs_10_ = f32[8,256,256]{2,1,0:T(8,128)S(1)} custom-call(s32[11]{0:T(128)S(1)} %pad_add_fusion.place_ref, f32[8,256,256]{2,1,0:T(8,128)S(1)} %all-to-all-done.1.refs_0_, f32[8,256,256]{2,1,0:T(8,128)S(1)} %copy-done.5, f32[4,256,256]{2,1,0:T(8,128)S(1)} %collective-permute-done.10.refs_2_, f32[4,256,256]{2,1,0:T(8,128)} %collective-permute-done.11.refs_3_, ...), custom_call_target="tpu_custom_call" | custom-call | flops 2415919104 | bytes 12582912 | tf_op jit(solution)/shard_map/products/pallas_call | solution.py:187
  165.9 5.5 %collective-permute-done.12.two_ref = f32[5,256,128]{2,1,0:T(8,128)S(1)} collective-permute-done((f32[5,256,128]{2,1,0:T(8,128)}, f32[5,256,128]{2,1,0:T(8,128)S(1)}, u32[]{:S(2)}, u32[]{:S(2)}) %collective-permute-start.12) | collective-permute-done | bytes 655392 | tf_op jit(solution)/shard_map/ppermute | solution.py:206
  171.4 4.0 %split_slab.3 = (bf16[10,256,256]{2,1,0:T(8,128)(2,1)S(1)}, bf16[10,256,256]{2,1,0:T(8,128)(2,1)S(1)}) custom-call(s32[10]{0:T(128)S(1)} %get-tuple-element.112.index_ref, f32[256,4096]{1,0:T(8,128)S(1)} %copy-done.3, f32[5,256,128]{2,1,0:T(8,128)} %collective-permute-done.8.one_ref, f32[5,256,128]{2,1,0:T(8,128)S(1)} %collective-permute-done.12.two_ref), custom_call_target="tpu_custom_call" | custom-call | bytes 5242880 | tf_op jit(solution)/shard_map/split_slab/pallas_call | solution.py:122
  176.3 2.3 order_rest.1
  179.3 5.2 %collective-permute-start.23 = (f32[1,256,256]{2,1,0:T(8,128)S(1)}, f32[1,256,256]{2,1,0:T(8,128)S(1)}, u32[]{:S(2)}, u32[]{:S(2)}) collective-permute-start(f32[1,256,256]{2,1,0:T(8,128)S(1)} %slice.73), channel_id=1, source_target_pairs={{0,240},{16,32},{32,16},{48,64},{64,48},{80,96},{96,80},{112,128},... | collective-permute-start | bytes 786440 | tf_op jit(solution)/shard_map/ppermute | solution.py:215
  185.8 4.6 %collective-permute-start.20 = (f32[1,256,256]{2,1,0:T(8,128)S(1)}, f32[1,256,256]{2,1,0:T(8,128)S(1)}, u32[]{:S(2)}, u32[]{:S(2)}) collective-permute-start(f32[1,256,256]{2,1,0:T(8,128)S(1)} %slice.70), channel_id=1, source_target_pairs={{0,240},{16,32},{32,16},{48,64},{64,48},{80,96},{96,80},{112,128},... | collective-permute-start | bytes 786440 | tf_op jit(solution)/shard_map/ppermute | solution.py:215
  190.5 6.0 %collective-permute-done.24.refs_3_ = f32[1,256,256]{2,1,0:T(8,128)S(1)} collective-permute-done((f32[1,256,256]{2,1,0:T(8,128)S(1)}, f32[1,256,256]{2,1,0:T(8,128)S(1)}, u32[]{:S(2)}, u32[]{:S(2)}) %collective-permute-start.24) | collective-permute-done | bytes 262176 | tf_op jit(solution)/shard_map/ppermute | solution.py:216
  196.6 1.6 products.9
  198.3 2.0 collective-permute-start.28
  200.4 2.0 collective-permute-start.17
  202.6 1.6 products.8
  206.1 2.0 collective-permute-start.29
  208.2 1.5 collective-permute-start.14
  211.0 1.6 collective-permute-done.18.refs_3_
  212.7 1.6 products.7
  215.0 2.2 collective-permute-start.30
  217.9 2.6 %collective-permute-done.15.refs_3_ = f32[1,256,256]{2,1,0:T(8,128)S(1)} collective-permute-done((f32[1,256,256]{2,1,0:T(8,128)S(1)}, f32[1,256,256]{2,1,0:T(8,128)S(1)}, u32[]{:S(2)}, u32[]{:S(2)}) %collective-permute-start.15) | collective-permute-done | bytes 262176 | tf_op jit(solution)/shard_map/ppermute | solution.py:216
  220.5 1.6 products.6
  222.1 2.9 %collective-permute-start.27 = (f32[256,256]{1,0:T(8,128)S(1)}, f32[256,256]{1,0:T(8,128)S(1)}, u32[]{:S(2)}, u32[]{:S(2)}) collective-permute-start(f32[256,256]{1,0:T(8,128)S(1)} %get-tuple-element.101), channel_id=1, source_target_pairs={{1,0},{2,1},{3,2},{4,3},{5,4},{6,5},{7,6},{0,7},{9,8},{10,9},{11,1... | collective-permute-start | bytes 786440 | tf_op jit(solution)/shard_map/ppermute | solution.py:206
  225.9 3.0 %collective-permute-done.27 = f32[256,256]{1,0:T(8,128)S(1)} collective-permute-done((f32[256,256]{1,0:T(8,128)S(1)}, f32[256,256]{1,0:T(8,128)S(1)}, u32[]{:S(2)}, u32[]{:S(2)}) %collective-permute-start.27) | collective-permute-done | bytes 262176 | tf_op jit(solution)/shard_map/ppermute | solution.py:206
  228.9 5.9 %collective-permute-done.31 = f32[256,256]{1,0:T(8,128)S(1)} collective-permute-done((f32[256,256]{1,0:T(8,128)S(1)}, f32[256,256]{1,0:T(8,128)S(1)}, u32[]{:S(2)}, u32[]{:S(2)}) %collective-permute-start.31) | collective-permute-done | bytes 262176 | tf_op jit(solution)/shard_map/ppermute | solution.py:206
  (89 shorter events, 23.5 us)
Async XLA Ops:
  4.4 51.1 %all-to-all-start = ((f32[16,128,256]{2,1,0:T(8,128)}), f32[16,128,256]{2,1,0:T(8,128)S(1)}, u32[]{:S(2)}, u32[]{:S(2)}) async-start(f32[16,128,256]{2,1,0:T(8,128)} %order_panel.2), calls=%async_computation | async-start | bytes 4194304 | tf_op jit(solution)/shard_map/all_to_all | solution.py:221
  14.4 45.8 %collective-permute-start.2 = (f32[8,128,256]{2,1,0:T(8,128)}, f32[8,128,256]{2,1,0:T(8,128)S(1)}, u32[]{:S(2)}, u32[]{:S(2)}) collective-permute-start(f32[8,128,256]{2,1,0:T(8,128)} %get-tuple-element.63), channel_id=1, source_target_pairs={{0,16},{16,0},{32,48},{48,32},{64,80},{80,64},{96,112},{112,96},{1... | collective-permute-start | bytes 3145736 | tf_op jit(solution)/shard_map/ppermute | solution.py:210
  15.9 39.6 %collective-permute-start = (f32[4,128,256]{2,1,0:T(8,128)S(1)}, f32[4,128,256]{2,1,0:T(8,128)}, u32[]{:S(2)}, u32[]{:S(2)}) collective-permute-start(f32[4,128,256]{2,1,0:T(8,128)S(1)} %slice.60), channel_id=1, source_target_pairs={{128,0},{0,128},{129,1},{1,129},{130,2},{2,130},{131,3},{3,131},{1... | collective-permute-start | bytes 1572872 | tf_op jit(solution)/shard_map/ppermute | solution.py:206
  22.7 32.7 %collective-permute-start.1 = (f32[3,256,128]{2,1,0:T(8,128)}, f32[3,256,128]{2,1,0:T(8,128)S(1)}, u32[]{:S(2)}, u32[]{:S(2)}) collective-permute-start(f32[3,256,128]{2,1,0:T(8,128)} %get-tuple-element.58), channel_id=1, source_target_pairs={{8,0},{0,8},{9,1},{1,9},{10,2},{2,10},{11,3},{3,11},{12,4},{4,12},... | collective-permute-start | bytes 1179656 | tf_op jit(solution)/shard_map/ppermute | solution.py:206
  55.5 1.4 copy-start.8
  60.2 8.5 %copy-start.9 = (f32[8,128,256]{2,1,0:T(8,128)}, f32[8,128,256]{2,1,0:T(8,128)S(1)}, u32[]{:S(2)}) copy-start(f32[8,128,256]{2,1,0:T(8,128)S(1)} %collective-permute-done.2.refs_2_) | copy-start | bytes 3145732
  60.2 59.8 %all-to-all-start.1 = ((f32[8,256,256]{2,1,0:T(8,128)}), f32[8,256,256]{2,1,0:T(8,128)S(1)}, u32[]{:S(2)}, u32[]{:S(2)}) async-start(f32[8,256,256]{2,1,0:T(8,128)} %bitcast.37), calls=%async_computation.1 | async-start | bytes 4194304 | tf_op jit(solution)/shard_map/all_to_all | solution.py:221
  68.7 15.1 %collective-permute-start.3 = (f32[4,128,256]{2,1,0:T(8,128)S(1)}, f32[4,128,256]{2,1,0:T(8,128)S(1)}, u32[]{:S(2)}, u32[]{:S(2)}) collective-permute-start(f32[4,128,256]{2,1,0:T(8,128)S(1)} %slice.61), channel_id=1, source_target_pairs={{128,0},{0,128},{129,1},{1,129},{130,2},{2,130},{131,3},{3,131},{1... | collective-permute-start | bytes 1572872 | tf_op jit(solution)/shard_map/ppermute | solution.py:206
  83.8 2.5 %copy-start.11 = (f32[4,128,256]{2,1,0:T(8,128)}, f32[4,128,256]{2,1,0:T(8,128)S(1)}, u32[]{:S(2)}) copy-start(f32[4,128,256]{2,1,0:T(8,128)S(1)} %collective-permute-done.3.refs_3_) | copy-start | bytes 1572868
  83.8 35.4 %collective-permute-start.7 = (f32[7,256,128]{2,1,0:T(8,128)}, f32[7,256,128]{2,1,0:T(8,128)S(1)}, u32[]{:S(2)}, u32[]{:S(2)}) collective-permute-start(f32[7,256,128]{2,1,0:T(8,128)} %get-tuple-element.77), channel_id=1, source_target_pairs={{8,0},{0,8},{9,1},{1,9},{10,2},{2,10},{11,3},{3,11},{12,4},{4,12},... | collective-permute-start | bytes 2752520 | tf_op jit(solution)/shard_map/ppermute | solution.py:206
  84.7 34.4 %collective-permute-start.8 = (f32[5,256,128]{2,1,0:T(8,128)}, f32[5,256,128]{2,1,0:T(8,128)}, u32[]{:S(2)}, u32[]{:S(2)}) collective-permute-start(f32[5,256,128]{2,1,0:T(8,128)} %get-tuple-element.78), channel_id=1, source_target_pairs={{8,0},{0,8},{9,1},{1,9},{10,2},{2,10},{11,3},{3,11},{12,4},{4,12},... | collective-permute-start | bytes 1966088 | tf_op jit(solution)/shard_map/ppermute | solution.py:206
  89.6 16.1 %collective-permute-start.4 = (f32[4,128,256]{2,1,0:T(8,128)}, f32[4,128,256]{2,1,0:T(8,128)S(1)}, u32[]{:S(2)}, u32[]{:S(2)}) collective-permute-start(f32[4,128,256]{2,1,0:T(8,128)} %get-tuple-element.72), channel_id=1, source_target_pairs={{96,0},{0,32},{32,64},{64,96},{97,1},{1,33},{33,65},{65,97},{98,2}... | collective-permute-start | bytes 1572872 | tf_op jit(solution)/shard_map/ppermute | solution.py:206
  91.0 23.9 %collective-permute-start.5 = (f32[4,128,256]{2,1,0:T(8,128)}, f32[4,128,256]{2,1,0:T(8,128)}, u32[]{:S(2)}, u32[]{:S(2)}) collective-permute-start(f32[4,128,256]{2,1,0:T(8,128)} %get-tuple-element.73), channel_id=1, source_target_pairs={{64,0},{96,32},{0,64},{32,96},{65,1},{97,33},{1,65},{33,97},{66,2}... | collective-permute-start | bytes 1572872 | tf_op jit(solution)/shard_map/ppermute | solution.py:206
  93.7 21.3 %collective-permute-start.6 = (f32[4,128,256]{2,1,0:T(8,128)}, f32[4,128,256]{2,1,0:T(8,128)}, u32[]{:S(2)}, u32[]{:S(2)}) collective-permute-start(f32[4,128,256]{2,1,0:T(8,128)} %get-tuple-element.74), channel_id=1, source_target_pairs={{32,0},{64,32},{96,64},{0,96},{33,1},{65,33},{97,65},{1,97},{34,2}... | collective-permute-start | bytes 1572872 | tf_op jit(solution)/shard_map/ppermute | solution.py:206
  105.7 9.3 %copy-start.10 = (f32[4,128,256]{2,1,0:T(8,128)}, f32[4,128,256]{2,1,0:T(8,128)S(1)}, u32[]{:S(2)}) copy-start(f32[4,128,256]{2,1,0:T(8,128)S(1)} %collective-permute-done.4.refs_1_) | copy-start | bytes 1572868
  119.1 0.9 copy-start.6
  120.0 56.3 %all-to-all-start.2 = ((f32[8,256,256]{2,1,0:T(8,128)}), f32[8,256,256]{2,1,0:T(8,128)}, u32[]{:S(2)}, u32[]{:S(2)}) async-start(f32[8,256,256]{2,1,0:T(8,128)} %bitcast.36), calls=%async_computation.2 | async-start | bytes 4194304 | tf_op jit(solution)/shard_map/all_to_all | solution.py:221
  126.7 9.8 %copy-start.12 = (s32[8]{0:T(128)S(1)}, s32[8]{0:T(128)}, u32[]{:S(2)}) copy-start(s32[8]{0:T(128)} %constant.162.clone) | copy-start | bytes 100
  126.7 5.4 %collective-permute-start.9 = (f32[8,256,256]{2,1,0:T(8,128)S(1)}, f32[8,256,256]{2,1,0:T(8,128)S(1)}, u32[]{:S(2)}, u32[]{:S(2)}) collective-permute-start(f32[8,256,256]{2,1,0:T(8,128)S(1)} %all-to-all-done.1.refs_0_), channel_id=1, source_target_pairs={{0,16},{16,0},{32,48},{48,32},{64,80},{80,64},{96,112},{112,96},{1... | collective-permute-start | bytes 6291464 | tf_op jit(solution)/shard_map/ppermute | solution.py:210
  127.8 23.4 %collective-permute-start.10 = (f32[4,256,256]{2,1,0:T(8,128)}, f32[4,256,256]{2,1,0:T(8,128)S(1)}, u32[]{:S(2)}, u32[]{:S(2)}) collective-permute-start(f32[4,256,256]{2,1,0:T(8,128)} %slice.62), channel_id=1, source_target_pairs={{0,240},{16,32},{32,16},{48,64},{64,48},{80,96},{96,80},{112,128},... | collective-permute-start | bytes 3145736 | tf_op jit(solution)/shard_map/ppermute | solution.py:215
  133.2 1.4 copy-start.4
  134.5 22.8 %collective-permute-start.11 = (f32[4,256,256]{2,1,0:T(8,128)}, f32[4,256,256]{2,1,0:T(8,128)}, u32[]{:S(2)}, u32[]{:S(2)}) collective-permute-start(f32[4,256,256]{2,1,0:T(8,128)} %slice.80), channel_id=1, source_target_pairs={{0,32},{16,240},{32,64},{48,16},{64,96},{80,48},{96,128},{112,80},... | collective-permute-start | bytes 3145736 | tf_op jit(solution)/shard_map/ppermute | solution.py:216
  134.5 36.9 %collective-permute-start.12 = (f32[5,256,128]{2,1,0:T(8,128)}, f32[5,256,128]{2,1,0:T(8,128)S(1)}, u32[]{:S(2)}, u32[]{:S(2)}) collective-permute-start(f32[5,256,128]{2,1,0:T(8,128)} %get-tuple-element.87), channel_id=1, source_target_pairs={{8,0},{0,8},{9,1},{1,9},{10,2},{2,10},{11,3},{3,11},{12,4},{4,12},... | collective-permute-start | bytes 1966088 | tf_op jit(solution)/shard_map/ppermute | solution.py:206
  136.5 2.2 copy-start.2
  138.7 1.2 copy-start.7
  139.9 17.4 %copy-start.5 = (f32[8,256,256]{2,1,0:T(8,128)S(1)}, f32[8,256,256]{2,1,0:T(8,128)}, u32[]{:S(2)}) copy-start(f32[8,256,256]{2,1,0:T(8,128)} %copy-done.4) | copy-start | bytes 6291460
  157.3 14.1 %copy-start.3 = (f32[256,4096]{1,0:T(8,128)S(1)}, f32[256,4096]{1,0:T(8,128)}, u32[]{:S(2)}) copy-start(f32[256,4096]{1,0:T(8,128)} %own_ref.3) | copy-start | bytes 12582916
  164.6 1.4 copy-start
  176.3 20.3 %copy-start.1 = (f32[8,256,256]{2,1,0:T(8,128)S(1)}, f32[8,256,256]{2,1,0:T(8,128)}, u32[]{:S(2)}) copy-start(f32[8,256,256]{2,1,0:T(8,128)} %copy-done) | copy-start | bytes 6291460
  178.6 5.8 %collective-permute-start.22 = (f32[2,256,256]{2,1,0:T(8,128)S(1)}, f32[2,256,256]{2,1,0:T(8,128)S(1)}, u32[]{:S(2)}, u32[]{:S(2)}) collective-permute-start(f32[2,256,256]{2,1,0:T(8,128)S(1)} %get-tuple-element.100.refs_0_), channel_id=1, source_target_pairs={{0,16},{16,0},{32,48},{48,32},{64,80},{80,64},{96,112},{112,96},{1... | collective-permute-start | bytes 1572872 | tf_op jit(solution)/shard_map/ppermute | solution.py:210
  178.7 11.7 %collective-permute-start.19 = (f32[2,256,256]{2,1,0:T(8,128)S(1)}, f32[2,256,256]{2,1,0:T(8,128)S(1)}, u32[]{:S(2)}, u32[]{:S(2)}) collective-permute-start(f32[2,256,256]{2,1,0:T(8,128)S(1)} %get-tuple-element.99.refs_0_), channel_id=1, source_target_pairs={{0,16},{16,0},{32,48},{48,32},{64,80},{80,64},{96,112},{112,96},{1... | collective-permute-start | bytes 1572872 | tf_op jit(solution)/shard_map/ppermute | solution.py:210
  179.3 11.3 %collective-permute-start.23 = (f32[1,256,256]{2,1,0:T(8,128)S(1)}, f32[1,256,256]{2,1,0:T(8,128)S(1)}, u32[]{:S(2)}, u32[]{:S(2)}) collective-permute-start(f32[1,256,256]{2,1,0:T(8,128)S(1)} %slice.73), channel_id=1, source_target_pairs={{0,240},{16,32},{32,16},{48,64},{64,48},{80,96},{96,80},{112,128},... | collective-permute-start | bytes 786440 | tf_op jit(solution)/shard_map/ppermute | solution.py:215
  184.5 12.1 %collective-permute-start.24 = (f32[1,256,256]{2,1,0:T(8,128)S(1)}, f32[1,256,256]{2,1,0:T(8,128)S(1)}, u32[]{:S(2)}, u32[]{:S(2)}) collective-permute-start(f32[1,256,256]{2,1,0:T(8,128)S(1)} %slice.87), channel_id=1, source_target_pairs={{0,32},{16,240},{32,64},{48,16},{64,96},{80,48},{96,128},{112,80},... | collective-permute-start | bytes 786440 | tf_op jit(solution)/shard_map/ppermute | solution.py:216
  184.6 15.7 %collective-permute-start.16 = (f32[2,256,256]{2,1,0:T(8,128)S(1)}, f32[2,256,256]{2,1,0:T(8,128)S(1)}, u32[]{:S(2)}, u32[]{:S(2)}) collective-permute-start(f32[2,256,256]{2,1,0:T(8,128)S(1)} %get-tuple-element.98.refs_0_), channel_id=1, source_target_pairs={{0,16},{16,0},{32,48},{48,32},{64,80},{80,64},{96,112},{112,96},{1... | collective-permute-start | bytes 1572872 | tf_op jit(solution)/shard_map/ppermute | solution.py:210
  185.8 14.5 %collective-permute-start.20 = (f32[1,256,256]{2,1,0:T(8,128)S(1)}, f32[1,256,256]{2,1,0:T(8,128)S(1)}, u32[]{:S(2)}, u32[]{:S(2)}) collective-permute-start(f32[1,256,256]{2,1,0:T(8,128)S(1)} %slice.70), channel_id=1, source_target_pairs={{0,240},{16,32},{32,16},{48,64},{64,48},{80,96},{96,80},{112,128},... | collective-permute-start | bytes 786440 | tf_op jit(solution)/shard_map/ppermute | solution.py:215
  190.4 11.9 %collective-permute-start.21 = (f32[1,256,256]{2,1,0:T(8,128)S(1)}, f32[1,256,256]{2,1,0:T(8,128)S(1)}, u32[]{:S(2)}, u32[]{:S(2)}) collective-permute-start(f32[1,256,256]{2,1,0:T(8,128)S(1)} %slice.85), channel_id=1, source_target_pairs={{0,32},{16,240},{32,64},{48,16},{64,96},{80,48},{96,128},{112,80},... | collective-permute-start | bytes 786440 | tf_op jit(solution)/shard_map/ppermute | solution.py:216
  198.2 6.5 %collective-permute-start.25 = (f32[256,256]{1,0:T(8,128)S(1)}, f32[256,256]{1,0:T(8,128)S(1)}, u32[]{:S(2)}, u32[]{:S(2)}) collective-permute-start(f32[256,256]{1,0:T(8,128)S(1)} %get-tuple-element.105), channel_id=1, source_target_pairs={{1,0},{2,1},{3,2},{4,3},{5,4},{6,5},{7,6},{0,7},{9,8},{10,9},{11,1... | collective-permute-start | bytes 786440 | tf_op jit(solution)/shard_map/ppermute | solution.py:206
  198.3 7.7 %collective-permute-start.28 = (f32[256,256]{1,0:T(8,128)S(1)}, f32[256,256]{1,0:T(8,128)S(1)}, u32[]{:S(2)}, u32[]{:S(2)}) collective-permute-start(f32[256,256]{1,0:T(8,128)S(1)} %get-tuple-element.106), channel_id=1, source_target_pairs={{7,0},{0,1},{1,2},{2,3},{3,4},{4,5},{5,6},{6,7},{15,8},{8,9},{9,10... | collective-permute-start | bytes 786440 | tf_op jit(solution)/shard_map/ppermute | solution.py:206
  200.3 7.8 %collective-permute-start.13 = (f32[2,256,256]{2,1,0:T(8,128)S(1)}, f32[2,256,256]{2,1,0:T(8,128)S(1)}, u32[]{:S(2)}, u32[]{:S(2)}) collective-permute-start(f32[2,256,256]{2,1,0:T(8,128)S(1)} %get-tuple-element.94.refs_0_), channel_id=1, source_target_pairs={{0,16},{16,0},{32,48},{48,32},{64,80},{80,64},{96,112},{112,96},{1... | collective-permute-start | bytes 1572872 | tf_op jit(solution)/shard_map/ppermute | solution.py:210
  200.4 9.8 %collective-permute-start.17 = (f32[1,256,256]{2,1,0:T(8,128)S(1)}, f32[1,256,256]{2,1,0:T(8,128)S(1)}, u32[]{:S(2)}, u32[]{:S(2)}) collective-permute-start(f32[1,256,256]{2,1,0:T(8,128)S(1)} %slice.67), channel_id=1, source_target_pairs={{0,240},{16,32},{32,16},{48,64},{64,48},{80,96},{96,80},{112,128},... | collective-permute-start | bytes 786440 | tf_op jit(solution)/shard_map/ppermute | solution.py:215
  202.3 10.4 %collective-permute-start.18 = (f32[1,256,256]{2,1,0:T(8,128)S(1)}, f32[1,256,256]{2,1,0:T(8,128)S(1)}, u32[]{:S(2)}, u32[]{:S(2)}) collective-permute-start(f32[1,256,256]{2,1,0:T(8,128)S(1)} %slice.83), channel_id=1, source_target_pairs={{0,32},{16,240},{32,64},{48,16},{64,96},{80,48},{96,128},{112,80},... | collective-permute-start | bytes 786440 | tf_op jit(solution)/shard_map/ppermute | solution.py:216
  206.0 8.7 %collective-permute-start.26 = (f32[256,256]{1,0:T(8,128)S(1)}, f32[256,256]{1,0:T(8,128)S(1)}, u32[]{:S(2)}, u32[]{:S(2)}) collective-permute-start(f32[256,256]{1,0:T(8,128)S(1)} %get-tuple-element.103), channel_id=1, source_target_pairs={{1,0},{2,1},{3,2},{4,3},{5,4},{6,5},{7,6},{0,7},{9,8},{10,9},{11,1... | collective-permute-start | bytes 786440 | tf_op jit(solution)/shard_map/ppermute | solution.py:206
  206.1 8.8 %collective-permute-start.29 = (f32[256,256]{1,0:T(8,128)S(1)}, f32[256,256]{1,0:T(8,128)S(1)}, u32[]{:S(2)}, u32[]{:S(2)}) collective-permute-start(f32[256,256]{1,0:T(8,128)S(1)} %get-tuple-element.104), channel_id=1, source_target_pairs={{7,0},{0,1},{1,2},{2,3},{3,4},{4,5},{5,6},{6,7},{15,8},{8,9},{9,10... | collective-permute-start | bytes 786440 | tf_op jit(solution)/shard_map/ppermute | solution.py:206
  208.2 9.7 %collective-permute-start.14 = (f32[1,256,256]{2,1,0:T(8,128)S(1)}, f32[1,256,256]{2,1,0:T(8,128)S(1)}, u32[]{:S(2)}, u32[]{:S(2)}) collective-permute-start(f32[1,256,256]{2,1,0:T(8,128)S(1)} %slice.64), channel_id=1, source_target_pairs={{0,240},{16,32},{32,16},{48,64},{64,48},{80,96},{96,80},{112,128},... | collective-permute-start | bytes 786440 | tf_op jit(solution)/shard_map/ppermute | solution.py:215
  210.2 10.3 %collective-permute-start.15 = (f32[1,256,256]{2,1,0:T(8,128)S(1)}, f32[1,256,256]{2,1,0:T(8,128)S(1)}, u32[]{:S(2)}, u32[]{:S(2)}) collective-permute-start(f32[1,256,256]{2,1,0:T(8,128)S(1)} %slice.81), channel_id=1, source_target_pairs={{0,32},{16,240},{32,64},{48,16},{64,96},{80,48},{96,128},{112,80},... | collective-permute-start | bytes 786440 | tf_op jit(solution)/shard_map/ppermute | solution.py:216
  215.0 10.0 %collective-permute-start.30 = (f32[256,256]{1,0:T(8,128)S(1)}, f32[256,256]{1,0:T(8,128)S(1)}, u32[]{:S(2)}, u32[]{:S(2)}) collective-permute-start(f32[256,256]{1,0:T(8,128)S(1)} %get-tuple-element.102), channel_id=1, source_target_pairs={{7,0},{0,1},{1,2},{2,3},{3,4},{4,5},{5,6},{6,7},{15,8},{8,9},{9,10... | collective-permute-start | bytes 786440 | tf_op jit(solution)/shard_map/ppermute | solution.py:206
  222.1 6.8 %collective-permute-start.27 = (f32[256,256]{1,0:T(8,128)S(1)}, f32[256,256]{1,0:T(8,128)S(1)}, u32[]{:S(2)}, u32[]{:S(2)}) collective-permute-start(f32[256,256]{1,0:T(8,128)S(1)} %get-tuple-element.101), channel_id=1, source_target_pairs={{1,0},{2,1},{3,2},{4,3},{5,4},{6,5},{7,6},{0,7},{9,8},{10,9},{11,1... | collective-permute-start | bytes 786440 | tf_op jit(solution)/shard_map/ppermute | solution.py:206
  225.0 9.8 %collective-permute-start.31 = (f32[256,256]{1,0:T(8,128)S(1)}, f32[256,256]{1,0:T(8,128)S(1)}, u32[]{:S(2)}, u32[]{:S(2)}) collective-permute-start(f32[256,256]{1,0:T(8,128)S(1)} %fusion.2), channel_id=1, source_target_pairs={{7,0},{0,1},{1,2},{2,3},{3,4},{4,5},{5,6},{6,7},{15,8},{8,9},{9,10... | collective-permute-start | bytes 786440 | tf_op jit(solution)/shard_map/ppermute | solution.py:206

commit v6 on v5

--- a/solution.py
+++ b/solution.py
@@ -14,7 +14,7 @@
 WINDOW = 3
 OFFSETS = (4, -3, 3, -2, 2, -1, 1, 0)
 GROUPS = (2, 2, 2, 2)
-EARLY = 3
+EARLY = 2
 LATE = 5
 LARGE = 60 * 2**20
 SMALL = 16 * 2**20

time: 239 us -> 239 us (level)
  starting transfers between devices: 69.5 us -> 66.6 us
    ppermute x16, waiting for transfers between devices: 80.1 us -> 84 us  [shifted(): lax.ppermute(block, axes, [((i - distance) % n, i) for i in range(n)])]
  transfers between devices with their start and end apart: 35 -> 35, of which waited for: 22 -> 21; matrix products, arithmetic and copies ran while one was open for 2% -> 3% of each run, Pallas kernels for 15% -> 15%
where the time goes in v6:
time: 239 us; the launch traced here: 234 us
  waiting for transfers between devices  110 us (46%)
  starting transfers between devices  66.6 us (28%)
  Pallas kernels  41.2 us (17%)
  local copies, waits for them, and re-layouts  12.5 us (5%)
  other arithmetic  3.85 us (2%)
    ppermute x16, waiting for transfers between devices, shifted(): lax.ppermute(block, axes, [((i - distance) % n, i) for i in range(n)])  84 us
    ppermute x16, starting transfers between devices, shifted(): lax.ppermute(block, axes, [((i - distance) % n, i) for i in range(n)])  25.1 us
    all_to_all x3, starting transfers between devices, exchange(): return lax.all_to_all(block, axes, split_axis=0, concat_axis=0, tiled=True)  21.2 us
    ppermute x5, starting transfers between devices, to_next_chips(): lax.ppermute(own, ROW, [(i, (i + (1 if i % 2 else -1)) % n) for i in rang...  16.6 us
    pallas_call x5, Pallas kernels, order_blocks(): pl.pallas_call(functools.partial(order_body, along), in_specs=[pl.BlockSp...  15.6 us
    ppermute x5, waiting for transfers between devices, to_next_chips(): lax.ppermute(other, ROW, [(i, (i + (-2 if i % 2 else 2)) % n) for i in ra...  15.2 us
    pallas_call x5, Pallas kernels, products(): pl.pallas_call(functools.partial(product_body, cut, first, ordered, start...  13.6 us
    ppermute x5, waiting for transfers between devices, to_next_chips(): lax.ppermute(own, ROW, [(i, (i + (1 if i % 2 else -1)) % n) for i in rang...  10.3 us
  transfers between devices with their start and end apart: 35, of which 21 were waited for; matrix products, arithmetic and copies ran while one was open for 3% of the time, Pallas kernels for 15%

profile of v6, /device:TPU:8, one launch (start us, length us, event | category | flops | bytes accessed | tf_op | source)
XLA Modules:
  0.0 234.2 jit_solution(9294306284896044414)
XLA Ops:
  0.5 3.3 %order_panel.2 = f32[16,128,256]{2,1,0:T(8,128)} custom-call(s32[16]{0:T(128)} %get-tuple-element.108.index_ref, f32[4096,256]{1,0:T(8,128)} %in_ref.4), custom_call_target="tpu_custom_call" | custom-call | bytes 4194304 | tf_op jit(solution)/shard_map/order_panel/pallas_call | solution.py:46
  4.5 6.1 %all-to-all-start = ((f32[16,128,256]{2,1,0:T(8,128)}), f32[16,128,256]{2,1,0:T(8,128)S(1)}, u32[]{:S(2)}, u32[]{:S(2)}) async-start(f32[16,128,256]{2,1,0:T(8,128)} %order_panel.2), calls=%async_computation | async-start | bytes 4194304 | tf_op jit(solution)/shard_map/all_to_all | solution.py:221
  11.1 3.3 %order_panel.3 = (f32[8,128,256]{2,1,0:T(8,128)}, f32[8,128,256]{2,1,0:T(8,128)}) custom-call(s32[16]{0:T(128)} %multiply_add_fusion.1.index_ref, f32[4096,256]{1,0:T(8,128)} %in_ref.4), custom_call_target="tpu_custom_call" | custom-call | bytes 4194304 | tf_op jit(solution)/shard_map/order_panel/pallas_call | solution.py:46
  16.0 3.3 %collective-permute-start = (f32[4,128,256]{2,1,0:T(8,128)S(1)}, f32[4,128,256]{2,1,0:T(8,128)}, u32[]{:S(2)}, u32[]{:S(2)}) collective-permute-start(f32[4,128,256]{2,1,0:T(8,128)S(1)} %slice.60), channel_id=1, source_target_pairs={{128,0},{0,128},{129,1},{1,129},{130,2},{2,130},{131,3},{3,131},{1... | collective-permute-start | bytes 1572872 | tf_op jit(solution)/shard_map/ppermute | solution.py:206
  19.2 3.5 %order_slab.1 = (f32[2,256,128]{2,1,0:T(8,128)}, f32[8,256,128]{2,1,0:T(8,128)}, f32[5,256,128]{2,1,0:T(8,128)}, f32[5,256,128]{2,1,0:T(8,128)}) custom-call(s32[20]{0:T(128)} %pad_add_fusion.1.index_ref, f32[256,4096]{1,0:T(8,128)} %own_ref.3), custom_call_target="tpu_custom_call" | custom-call | bytes 5242880 | tf_op jit(solution)/shard_map/order_slab/pallas_call | solution.py:46
  22.7 1.4 collective-permute-start.1
  24.8 28.0 %collective-permute-done.1.one_ref = f32[2,256,128]{2,1,0:T(8,128)S(1)} collective-permute-done((f32[2,256,128]{2,1,0:T(8,128)}, f32[2,256,128]{2,1,0:T(8,128)S(1)}, u32[]{:S(2)}, u32[]{:S(2)}) %collective-permute-start.1) | collective-permute-done | bytes 262176 | tf_op jit(solution)/shard_map/ppermute | solution.py:206
  54.1 3.3 %order_planes.2 = f32[16,128,256]{2,1,0:T(8,128)} custom-call(s32[16]{0:T(128)} %multiply_add_fusion.index_ref, f32[2048,256]{1,0:T(8,128)} %bitcast.38), custom_call_target="tpu_custom_call" | custom-call | bytes 4194304 | tf_op jit(solution)/shard_map/order_planes/pallas_call | solution.py:46
  57.4 8.5 %all-to-all-start.1 = ((f32[8,256,256]{2,1,0:T(8,128)}), f32[8,256,256]{2,1,0:T(8,128)S(1)}, u32[]{:S(2)}, u32[]{:S(2)}) async-start(f32[8,256,256]{2,1,0:T(8,128)} %bitcast.37), calls=%async_computation.1 | async-start | bytes 4194304 | tf_op jit(solution)/shard_map/all_to_all | solution.py:221
  65.9 2.7 %collective-permute-start.3 = (f32[4,128,256]{2,1,0:T(8,128)S(1)}, f32[4,128,256]{2,1,0:T(8,128)S(1)}, u32[]{:S(2)}, u32[]{:S(2)}) collective-permute-start(f32[4,128,256]{2,1,0:T(8,128)S(1)} %slice.61), channel_id=1, source_target_pairs={{128,0},{0,128},{129,1},{1,129},{130,2},{2,130},{131,3},{3,131},{1... | collective-permute-start | bytes 1572872 | tf_op jit(solution)/shard_map/ppermute | solution.py:206
  68.6 12.4 %collective-permute-done.3.refs_3_ = f32[4,128,256]{2,1,0:T(8,128)S(1)} collective-permute-done((f32[4,128,256]{2,1,0:T(8,128)S(1)}, f32[4,128,256]{2,1,0:T(8,128)S(1)}, u32[]{:S(2)}, u32[]{:S(2)}) %collective-permute-start.3) | collective-permute-done | bytes 524320 | tf_op jit(solution)/shard_map/ppermute | solution.py:206
  83.6 3.3 %order_distance.1 = (f32[4,128,256]{2,1,0:T(8,128)}, f32[4,128,256]{2,1,0:T(8,128)}, f32[4,128,256]{2,1,0:T(8,128)}, f32[4,128,256]{2,1,0:T(8,128)}) custom-call(s32[16]{0:T(128)} %iota.29.index_ref, f32[8,128,256]{2,1,0:T(8,128)} %get-tuple-element.54.refs_0_, f32[4,128,256]{2,1,0:T(8,128)} %collective-permute-done.refs_1_, f32[8,128,256]{2,1,0:T(8,128)} %copy-done.9, ...), custom_call_target="tpu_custom_call" | custom-call | bytes 4194304 | tf_op jit(solution)/shard_map/order_distance/pallas_call | solution.py:93
  86.9 1.5 collective-permute-start.4
  88.3 2.7 %collective-permute-start.5 = (f32[4,128,256]{2,1,0:T(8,128)}, f32[4,128,256]{2,1,0:T(8,128)}, u32[]{:S(2)}, u32[]{:S(2)}) collective-permute-start(f32[4,128,256]{2,1,0:T(8,128)} %get-tuple-element.73), channel_id=1, source_target_pairs={{64,0},{96,32},{0,64},{32,96},{65,1},{97,33},{1,65},{33,97},{66,2}... | collective-permute-start | bytes 1572872 | tf_op jit(solution)/shard_map/ppermute | solution.py:206
  91.0 1.5 collective-permute-start.6
  93.0 10.0 %collective-permute-done.4.refs_1_ = f32[4,128,256]{2,1,0:T(8,128)S(1)} collective-permute-done((f32[4,128,256]{2,1,0:T(8,128)}, f32[4,128,256]{2,1,0:T(8,128)S(1)}, u32[]{:S(2)}, u32[]{:S(2)}) %collective-permute-start.4) | collective-permute-done | bytes 524320 | tf_op jit(solution)/shard_map/ppermute | solution.py:206
  103.0 9.2 %collective-permute-done.5.refs_2_ = f32[4,128,256]{2,1,0:T(8,128)} collective-permute-done((f32[4,128,256]{2,1,0:T(8,128)}, f32[4,128,256]{2,1,0:T(8,128)}, u32[]{:S(2)}, u32[]{:S(2)}) %collective-permute-start.5) | collective-permute-done | bytes 524320 | tf_op jit(solution)/shard_map/ppermute | solution.py:206
  112.3 3.3 %order_planes.3 = f32[16,128,256]{2,1,0:T(8,128)} custom-call(s32[16]{0:T(128)} %xor_add_fusion.index_ref, f32[4,128,256]{2,1,0:T(8,128)} %get-tuple-element.71.refs_0_, f32[4,128,256]{2,1,0:T(8,128)} %copy-done.10, f32[4,128,256]{2,1,0:T(8,128)} %collective-permute-done.5.refs_2_, f32[4,128,256]{2,1,0:T(8,128)} %collective-permute-done.6.refs_3_), custom_call_target="tpu_custom_call" | custom-call | bytes 4194304 | tf_op jit(solution)/shard_map/order_planes/pallas_call | solution.py:93
  115.7 3.5 %collective-permute-done.8.one_ref = f32[5,256,128]{2,1,0:T(8,128)} collective-permute-done((f32[5,256,128]{2,1,0:T(8,128)}, f32[5,256,128]{2,1,0:T(8,128)}, u32[]{:S(2)}, u32[]{:S(2)}) %collective-permute-start.8) | collective-permute-done | bytes 655392 | tf_op jit(solution)/shard_map/ppermute | solution.py:206
  120.2 6.6 %all-to-all-start.2 = ((f32[8,256,256]{2,1,0:T(8,128)}), f32[8,256,256]{2,1,0:T(8,128)}, u32[]{:S(2)}, u32[]{:S(2)}) async-start(f32[8,256,256]{2,1,0:T(8,128)} %bitcast.36), calls=%async_computation.2 | async-start | bytes 4194304 | tf_op jit(solution)/shard_map/all_to_all | solution.py:221
  128.0 4.2 %collective-permute-start.10 = (f32[4,256,256]{2,1,0:T(8,128)}, f32[4,256,256]{2,1,0:T(8,128)S(1)}, u32[]{:S(2)}, u32[]{:S(2)}) collective-permute-start(f32[4,256,256]{2,1,0:T(8,128)} %slice.62), channel_id=1, source_target_pairs={{0,240},{16,32},{32,16},{48,64},{64,48},{80,96},{96,80},{112,128},... | collective-permute-start | bytes 3145736 | tf_op jit(solution)/shard_map/ppermute | solution.py:215
  134.7 1.9 collective-permute-start.12
  136.7 2.2 copy-done.2
  140.1 1.5 split_slab.2
  141.6 10.0 %collective-permute-done.10.refs_2_ = f32[4,256,256]{2,1,0:T(8,128)S(1)} collective-permute-done((f32[4,256,256]{2,1,0:T(8,128)}, f32[4,256,256]{2,1,0:T(8,128)S(1)}, u32[]{:S(2)}, u32[]{:S(2)}) %collective-permute-start.10) | collective-permute-done | bytes 1048608 | tf_op jit(solution)/shard_map/ppermute | solution.py:215
  151.6 5.9 %collective-permute-done.11.refs_3_ = f32[4,256,256]{2,1,0:T(8,128)} collective-permute-done((f32[4,256,256]{2,1,0:T(8,128)}, f32[4,256,256]{2,1,0:T(8,128)}, u32[]{:S(2)}, u32[]{:S(2)}) %collective-permute-start.11) | collective-permute-done | bytes 1048608 | tf_op jit(solution)/shard_map/ppermute | solution.py:216
  157.5 7.2 %products.5.refs_10_ = f32[8,256,256]{2,1,0:T(8,128)S(1)} custom-call(s32[11]{0:T(128)S(1)} %pad_add_fusion.place_ref, f32[8,256,256]{2,1,0:T(8,128)S(1)} %all-to-all-done.1.refs_0_, f32[8,256,256]{2,1,0:T(8,128)S(1)} %copy-done.5, f32[4,256,256]{2,1,0:T(8,128)S(1)} %collective-permute-done.10.refs_2_, f32[4,256,256]{2,1,0:T(8,128)} %collective-permute-done.11.refs_3_, ...), custom_call_target="tpu_custom_call" | custom-call | flops 2415919104 | bytes 12582912 | tf_op jit(solution)/shard_map/products/pallas_call | solution.py:187
  166.1 5.5 %collective-permute-done.12.two_ref = f32[5,256,128]{2,1,0:T(8,128)S(1)} collective-permute-done((f32[5,256,128]{2,1,0:T(8,128)}, f32[5,256,128]{2,1,0:T(8,128)S(1)}, u32[]{:S(2)}, u32[]{:S(2)}) %collective-permute-start.12) | collective-permute-done | bytes 655392 | tf_op jit(solution)/shard_map/ppermute | solution.py:206
  171.6 4.0 %split_slab.3 = (bf16[10,256,256]{2,1,0:T(8,128)(2,1)S(1)}, bf16[10,256,256]{2,1,0:T(8,128)(2,1)S(1)}) custom-call(s32[10]{0:T(128)S(1)} %get-tuple-element.112.index_ref, f32[256,4096]{1,0:T(8,128)S(1)} %copy-done.3, f32[5,256,128]{2,1,0:T(8,128)} %collective-permute-done.8.one_ref, f32[5,256,128]{2,1,0:T(8,128)S(1)} %collective-permute-done.12.two_ref), custom_call_target="tpu_custom_call" | custom-call | bytes 5242880 | tf_op jit(solution)/shard_map/split_slab/pallas_call | solution.py:122
  175.8 2.3 order_rest.1
  178.7 3.8 %collective-permute-start.23 = (f32[1,256,256]{2,1,0:T(8,128)S(1)}, f32[1,256,256]{2,1,0:T(8,128)S(1)}, u32[]{:S(2)}, u32[]{:S(2)}) collective-permute-start(f32[1,256,256]{2,1,0:T(8,128)S(1)} %slice.73), channel_id=1, source_target_pairs={{0,240},{16,32},{32,16},{48,64},{64,48},{80,96},{96,80},{112,128},... | collective-permute-start | bytes 786440 | tf_op jit(solution)/shard_map/ppermute | solution.py:215
  182.6 1.9 collective-permute-start.16
  184.6 3.9 %collective-permute-start.20 = (f32[1,256,256]{2,1,0:T(8,128)S(1)}, f32[1,256,256]{2,1,0:T(8,128)S(1)}, u32[]{:S(2)}, u32[]{:S(2)}) collective-permute-start(f32[1,256,256]{2,1,0:T(8,128)S(1)} %slice.70), channel_id=1, source_target_pairs={{0,240},{16,32},{32,16},{48,64},{64,48},{80,96},{96,80},{112,128},... | collective-permute-start | bytes 786440 | tf_op jit(solution)/shard_map/ppermute | solution.py:215
  188.6 5.3 %collective-permute-done.24.refs_3_ = f32[1,256,256]{2,1,0:T(8,128)S(1)} collective-permute-done((f32[1,256,256]{2,1,0:T(8,128)S(1)}, f32[1,256,256]{2,1,0:T(8,128)S(1)}, u32[]{:S(2)}, u32[]{:S(2)}) %collective-permute-start.24) | collective-permute-done | bytes 262176 | tf_op jit(solution)/shard_map/ppermute | solution.py:216
  193.9 1.6 products.9
  197.6 1.9 collective-permute-start.17
  199.9 1.6 products.8
  201.9 2.2 collective-permute-done.28
  204.6 1.7 collective-permute-start.29
  206.4 2.8 %collective-permute-start.14 = (f32[1,256,256]{2,1,0:T(8,128)S(1)}, f32[1,256,256]{2,1,0:T(8,128)S(1)}, u32[]{:S(2)}, u32[]{:S(2)}) collective-permute-start(f32[1,256,256]{2,1,0:T(8,128)S(1)} %slice.64), channel_id=1, source_target_pairs={{0,240},{16,32},{32,16},{48,64},{64,48},{80,96},{96,80},{112,128},... | collective-permute-start | bytes 786440 | tf_op jit(solution)/shard_map/ppermute | solution.py:215
  210.0 1.6 products.7
  211.5 1.6 collective-permute-done.26
  213.7 1.9 collective-permute-start.30
  215.9 3.4 %collective-permute-done.15.refs_3_ = f32[1,256,256]{2,1,0:T(8,128)S(1)} collective-permute-done((f32[1,256,256]{2,1,0:T(8,128)S(1)}, f32[1,256,256]{2,1,0:T(8,128)S(1)}, u32[]{:S(2)}, u32[]{:S(2)}) %collective-permute-start.15) | collective-permute-done | bytes 262176 | tf_op jit(solution)/shard_map/ppermute | solution.py:216
  219.2 1.6 products.6
  220.8 1.8 collective-permute-start.27
  223.9 3.4 %collective-permute-done.27 = f32[256,256]{1,0:T(8,128)S(1)} collective-permute-done((f32[256,256]{1,0:T(8,128)S(1)}, f32[256,256]{1,0:T(8,128)S(1)}, u32[]{:S(2)}, u32[]{:S(2)}) %collective-permute-start.27) | collective-permute-done | bytes 262176 | tf_op jit(solution)/shard_map/ppermute | solution.py:206
  227.3 6.2 %collective-permute-done.31 = f32[256,256]{1,0:T(8,128)S(1)} collective-permute-done((f32[256,256]{1,0:T(8,128)S(1)}, f32[256,256]{1,0:T(8,128)S(1)}, u32[]{:S(2)}, u32[]{:S(2)}) %collective-permute-start.31) | collective-permute-done | bytes 262176 | tf_op jit(solution)/shard_map/ppermute | solution.py:206
  (89 shorter events, 23.8 us)
Async XLA Ops:
  4.5 48.3 %all-to-all-start = ((f32[16,128,256]{2,1,0:T(8,128)}), f32[16,128,256]{2,1,0:T(8,128)S(1)}, u32[]{:S(2)}, u32[]{:S(2)}) async-start(f32[16,128,256]{2,1,0:T(8,128)} %order_panel.2), calls=%async_computation | async-start | bytes 4194304 | tf_op jit(solution)/shard_map/all_to_all | solution.py:221
  14.4 43.0 %collective-permute-start.2 = (f32[8,128,256]{2,1,0:T(8,128)}, f32[8,128,256]{2,1,0:T(8,128)S(1)}, u32[]{:S(2)}, u32[]{:S(2)}) collective-permute-start(f32[8,128,256]{2,1,0:T(8,128)} %get-tuple-element.63), channel_id=1, source_target_pairs={{0,16},{16,0},{32,48},{48,32},{64,80},{80,64},{96,112},{112,96},{1... | collective-permute-start | bytes 3145736 | tf_op jit(solution)/shard_map/ppermute | solution.py:210
  16.0 36.8 %collective-permute-start = (f32[4,128,256]{2,1,0:T(8,128)S(1)}, f32[4,128,256]{2,1,0:T(8,128)}, u32[]{:S(2)}, u32[]{:S(2)}) collective-permute-start(f32[4,128,256]{2,1,0:T(8,128)S(1)} %slice.60), channel_id=1, source_target_pairs={{128,0},{0,128},{129,1},{1,129},{130,2},{2,130},{131,3},{3,131},{1... | collective-permute-start | bytes 1572872 | tf_op jit(solution)/shard_map/ppermute | solution.py:206
  22.7 30.0 %collective-permute-start.1 = (f32[2,256,128]{2,1,0:T(8,128)}, f32[2,256,128]{2,1,0:T(8,128)S(1)}, u32[]{:S(2)}, u32[]{:S(2)}) collective-permute-start(f32[2,256,128]{2,1,0:T(8,128)} %get-tuple-element.58), channel_id=1, source_target_pairs={{8,0},{0,8},{9,1},{1,9},{10,2},{2,10},{11,3},{3,11},{12,4},{4,12},... | collective-permute-start | bytes 786440 | tf_op jit(solution)/shard_map/ppermute | solution.py:206
  52.8 1.4 copy-start.8
  57.4 8.5 %copy-start.9 = (f32[8,128,256]{2,1,0:T(8,128)}, f32[8,128,256]{2,1,0:T(8,128)S(1)}, u32[]{:S(2)}) copy-start(f32[8,128,256]{2,1,0:T(8,128)S(1)} %collective-permute-done.2.refs_2_) | copy-start | bytes 3145732
  57.4 61.8 %all-to-all-start.1 = ((f32[8,256,256]{2,1,0:T(8,128)}), f32[8,256,256]{2,1,0:T(8,128)S(1)}, u32[]{:S(2)}, u32[]{:S(2)}) async-start(f32[8,256,256]{2,1,0:T(8,128)} %bitcast.37), calls=%async_computation.1 | async-start | bytes 4194304 | tf_op jit(solution)/shard_map/all_to_all | solution.py:221
  65.9 15.1 %collective-permute-start.3 = (f32[4,128,256]{2,1,0:T(8,128)S(1)}, f32[4,128,256]{2,1,0:T(8,128)S(1)}, u32[]{:S(2)}, u32[]{:S(2)}) collective-permute-start(f32[4,128,256]{2,1,0:T(8,128)S(1)} %slice.61), channel_id=1, source_target_pairs={{128,0},{0,128},{129,1},{1,129},{130,2},{2,130},{131,3},{3,131},{1... | collective-permute-start | bytes 1572872 | tf_op jit(solution)/shard_map/ppermute | solution.py:206
  81.0 2.5 %copy-start.11 = (f32[4,128,256]{2,1,0:T(8,128)}, f32[4,128,256]{2,1,0:T(8,128)S(1)}, u32[]{:S(2)}) copy-start(f32[4,128,256]{2,1,0:T(8,128)S(1)} %collective-permute-done.3.refs_3_) | copy-start | bytes 1572868
  81.0 38.2 %collective-permute-start.7 = (f32[8,256,128]{2,1,0:T(8,128)}, f32[8,256,128]{2,1,0:T(8,128)S(1)}, u32[]{:S(2)}, u32[]{:S(2)}) collective-permute-start(f32[8,256,128]{2,1,0:T(8,128)} %get-tuple-element.77), channel_id=1, source_target_pairs={{8,0},{0,8},{9,1},{1,9},{10,2},{2,10},{11,3},{3,11},{12,4},{4,12},... | collective-permute-start | bytes 3145736 | tf_op jit(solution)/shard_map/ppermute | solution.py:206
  81.9 37.2 %collective-permute-start.8 = (f32[5,256,128]{2,1,0:T(8,128)}, f32[5,256,128]{2,1,0:T(8,128)}, u32[]{:S(2)}, u32[]{:S(2)}) collective-permute-start(f32[5,256,128]{2,1,0:T(8,128)} %get-tuple-element.78), channel_id=1, source_target_pairs={{8,0},{0,8},{9,1},{1,9},{10,2},{2,10},{11,3},{3,11},{12,4},{4,12},... | collective-permute-start | bytes 1966088 | tf_op jit(solution)/shard_map/ppermute | solution.py:206
  86.9 16.1 %collective-permute-start.4 = (f32[4,128,256]{2,1,0:T(8,128)}, f32[4,128,256]{2,1,0:T(8,128)S(1)}, u32[]{:S(2)}, u32[]{:S(2)}) collective-permute-start(f32[4,128,256]{2,1,0:T(8,128)} %get-tuple-element.72), channel_id=1, source_target_pairs={{96,0},{0,32},{32,64},{64,96},{97,1},{1,33},{33,65},{65,97},{98,2}... | collective-permute-start | bytes 1572872 | tf_op jit(solution)/shard_map/ppermute | solution.py:206
  88.3 23.9 %collective-permute-start.5 = (f32[4,128,256]{2,1,0:T(8,128)}, f32[4,128,256]{2,1,0:T(8,128)}, u32[]{:S(2)}, u32[]{:S(2)}) collective-permute-start(f32[4,128,256]{2,1,0:T(8,128)} %get-tuple-element.73), channel_id=1, source_target_pairs={{64,0},{96,32},{0,64},{32,96},{65,1},{97,33},{1,65},{33,97},{66,2}... | collective-permute-start | bytes 1572872 | tf_op jit(solution)/shard_map/ppermute | solution.py:206
  91.0 21.3 %collective-permute-start.6 = (f32[4,128,256]{2,1,0:T(8,128)}, f32[4,128,256]{2,1,0:T(8,128)}, u32[]{:S(2)}, u32[]{:S(2)}) collective-permute-start(f32[4,128,256]{2,1,0:T(8,128)} %get-tuple-element.74), channel_id=1, source_target_pairs={{32,0},{64,32},{96,64},{0,96},{33,1},{65,33},{97,65},{1,97},{34,2}... | collective-permute-start | bytes 1572872 | tf_op jit(solution)/shard_map/ppermute | solution.py:206
  103.0 9.3 %copy-start.10 = (f32[4,128,256]{2,1,0:T(8,128)}, f32[4,128,256]{2,1,0:T(8,128)S(1)}, u32[]{:S(2)}) copy-start(f32[4,128,256]{2,1,0:T(8,128)S(1)} %collective-permute-done.4.refs_1_) | copy-start | bytes 1572868
  119.2 1.0 copy-start.6
  120.2 55.6 %all-to-all-start.2 = ((f32[8,256,256]{2,1,0:T(8,128)}), f32[8,256,256]{2,1,0:T(8,128)}, u32[]{:S(2)}, u32[]{:S(2)}) async-start(f32[8,256,256]{2,1,0:T(8,128)} %bitcast.36), calls=%async_computation.2 | async-start | bytes 4194304 | tf_op jit(solution)/shard_map/all_to_all | solution.py:221
  126.8 9.8 %copy-start.12 = (s32[8]{0:T(128)S(1)}, s32[8]{0:T(128)}, u32[]{:S(2)}) copy-start(s32[8]{0:T(128)} %constant.162.clone) | copy-start | bytes 100
  126.8 5.5 %collective-permute-start.9 = (f32[8,256,256]{2,1,0:T(8,128)S(1)}, f32[8,256,256]{2,1,0:T(8,128)S(1)}, u32[]{:S(2)}, u32[]{:S(2)}) collective-permute-start(f32[8,256,256]{2,1,0:T(8,128)S(1)} %all-to-all-done.1.refs_0_), channel_id=1, source_target_pairs={{0,16},{16,0},{32,48},{48,32},{64,80},{80,64},{96,112},{112,96},{1... | collective-permute-start | bytes 6291464 | tf_op jit(solution)/shard_map/ppermute | solution.py:210
  128.0 23.6 %collective-permute-start.10 = (f32[4,256,256]{2,1,0:T(8,128)}, f32[4,256,256]{2,1,0:T(8,128)S(1)}, u32[]{:S(2)}, u32[]{:S(2)}) collective-permute-start(f32[4,256,256]{2,1,0:T(8,128)} %slice.62), channel_id=1, source_target_pairs={{0,240},{16,32},{32,16},{48,64},{64,48},{80,96},{96,80},{112,128},... | collective-permute-start | bytes 3145736 | tf_op jit(solution)/shard_map/ppermute | solution.py:215
  133.3 1.4 copy-start.4
  134.7 22.9 %collective-permute-start.11 = (f32[4,256,256]{2,1,0:T(8,128)}, f32[4,256,256]{2,1,0:T(8,128)}, u32[]{:S(2)}, u32[]{:S(2)}) collective-permute-start(f32[4,256,256]{2,1,0:T(8,128)} %slice.80), channel_id=1, source_target_pairs={{0,32},{16,240},{32,64},{48,16},{64,96},{80,48},{96,128},{112,80},... | collective-permute-start | bytes 3145736 | tf_op jit(solution)/shard_map/ppermute | solution.py:216
  134.7 37.0 %collective-permute-start.12 = (f32[5,256,128]{2,1,0:T(8,128)}, f32[5,256,128]{2,1,0:T(8,128)S(1)}, u32[]{:S(2)}, u32[]{:S(2)}) collective-permute-start(f32[5,256,128]{2,1,0:T(8,128)} %get-tuple-element.87), channel_id=1, source_target_pairs={{8,0},{0,8},{9,1},{1,9},{10,2},{2,10},{11,3},{3,11},{12,4},{4,12},... | collective-permute-start | bytes 1966088 | tf_op jit(solution)/shard_map/ppermute | solution.py:206
  136.7 2.2 copy-start.2
  138.8 1.2 copy-start.7
  140.1 17.5 %copy-start.5 = (f32[8,256,256]{2,1,0:T(8,128)S(1)}, f32[8,256,256]{2,1,0:T(8,128)}, u32[]{:S(2)}) copy-start(f32[8,256,256]{2,1,0:T(8,128)} %copy-done.4) | copy-start | bytes 6291460
  157.5 14.1 %copy-start.3 = (f32[256,4096]{1,0:T(8,128)S(1)}, f32[256,4096]{1,0:T(8,128)}, u32[]{:S(2)}) copy-start(f32[256,4096]{1,0:T(8,128)} %own_ref.3) | copy-start | bytes 12582916
  164.8 1.4 copy-start
  175.8 18.1 %copy-start.1 = (f32[8,256,256]{2,1,0:T(8,128)S(1)}, f32[8,256,256]{2,1,0:T(8,128)}, u32[]{:S(2)}) copy-start(f32[8,256,256]{2,1,0:T(8,128)} %copy-done) | copy-start | bytes 6291460
  178.1 4.4 %collective-permute-start.22 = (f32[2,256,256]{2,1,0:T(8,128)S(1)}, f32[2,256,256]{2,1,0:T(8,128)S(1)}, u32[]{:S(2)}, u32[]{:S(2)}) collective-permute-start(f32[2,256,256]{2,1,0:T(8,128)S(1)} %get-tuple-element.100.refs_0_), channel_id=1, source_target_pairs={{0,16},{16,0},{32,48},{48,32},{64,80},{80,64},{96,112},{112,96},{1... | collective-permute-start | bytes 1572872 | tf_op jit(solution)/shard_map/ppermute | solution.py:210
  178.3 10.1 %collective-permute-start.19 = (f32[2,256,256]{2,1,0:T(8,128)S(1)}, f32[2,256,256]{2,1,0:T(8,128)S(1)}, u32[]{:S(2)}, u32[]{:S(2)}) collective-permute-start(f32[2,256,256]{2,1,0:T(8,128)S(1)} %get-tuple-element.99.refs_0_), channel_id=1, source_target_pairs={{0,16},{16,0},{32,48},{48,32},{64,80},{80,64},{96,112},{112,96},{1... | collective-permute-start | bytes 1572872 | tf_op jit(solution)/shard_map/ppermute | solution.py:210
  178.7 9.9 %collective-permute-start.23 = (f32[1,256,256]{2,1,0:T(8,128)S(1)}, f32[1,256,256]{2,1,0:T(8,128)S(1)}, u32[]{:S(2)}, u32[]{:S(2)}) collective-permute-start(f32[1,256,256]{2,1,0:T(8,128)S(1)} %slice.73), channel_id=1, source_target_pairs={{0,240},{16,32},{32,16},{48,64},{64,48},{80,96},{96,80},{112,128},... | collective-permute-start | bytes 786440 | tf_op jit(solution)/shard_map/ppermute | solution.py:215
  182.5 11.3 %collective-permute-start.24 = (f32[1,256,256]{2,1,0:T(8,128)S(1)}, f32[1,256,256]{2,1,0:T(8,128)S(1)}, u32[]{:S(2)}, u32[]{:S(2)}) collective-permute-start(f32[1,256,256]{2,1,0:T(8,128)S(1)} %slice.87), channel_id=1, source_target_pairs={{0,32},{16,240},{32,64},{48,16},{64,96},{80,48},{96,128},{112,80},... | collective-permute-start | bytes 786440 | tf_op jit(solution)/shard_map/ppermute | solution.py:216
  182.6 15.0 %collective-permute-start.16 = (f32[2,256,256]{2,1,0:T(8,128)S(1)}, f32[2,256,256]{2,1,0:T(8,128)S(1)}, u32[]{:S(2)}, u32[]{:S(2)}) collective-permute-start(f32[2,256,256]{2,1,0:T(8,128)S(1)} %get-tuple-element.98.refs_0_), channel_id=1, source_target_pairs={{0,16},{16,0},{32,48},{48,32},{64,80},{80,64},{96,112},{112,96},{1... | collective-permute-start | bytes 1572872 | tf_op jit(solution)/shard_map/ppermute | solution.py:210
  184.6 13.1 %collective-permute-start.20 = (f32[1,256,256]{2,1,0:T(8,128)S(1)}, f32[1,256,256]{2,1,0:T(8,128)S(1)}, u32[]{:S(2)}, u32[]{:S(2)}) collective-permute-start(f32[1,256,256]{2,1,0:T(8,128)S(1)} %slice.70), channel_id=1, source_target_pairs={{0,240},{16,32},{32,16},{48,64},{64,48},{80,96},{96,80},{112,128},... | collective-permute-start | bytes 786440 | tf_op jit(solution)/shard_map/ppermute | solution.py:215
  188.5 11.1 %collective-permute-start.21 = (f32[1,256,256]{2,1,0:T(8,128)S(1)}, f32[1,256,256]{2,1,0:T(8,128)S(1)}, u32[]{:S(2)}, u32[]{:S(2)}) collective-permute-start(f32[1,256,256]{2,1,0:T(8,128)S(1)} %slice.85), channel_id=1, source_target_pairs={{0,32},{16,240},{32,64},{48,16},{64,96},{80,48},{96,128},{112,80},... | collective-permute-start | bytes 786440 | tf_op jit(solution)/shard_map/ppermute | solution.py:216
  195.5 6.5 %collective-permute-start.25 = (f32[256,256]{1,0:T(8,128)S(1)}, f32[256,256]{1,0:T(8,128)S(1)}, u32[]{:S(2)}, u32[]{:S(2)}) collective-permute-start(f32[256,256]{1,0:T(8,128)S(1)} %get-tuple-element.105), channel_id=1, source_target_pairs={{1,0},{2,1},{3,2},{4,3},{5,4},{6,5},{7,6},{0,7},{9,8},{10,9},{11,1... | collective-permute-start | bytes 786440 | tf_op jit(solution)/shard_map/ppermute | solution.py:206
  196.6 7.6 %collective-permute-start.28 = (f32[256,256]{1,0:T(8,128)S(1)}, f32[256,256]{1,0:T(8,128)S(1)}, u32[]{:S(2)}, u32[]{:S(2)}) collective-permute-start(f32[256,256]{1,0:T(8,128)S(1)} %get-tuple-element.106), channel_id=1, source_target_pairs={{7,0},{0,1},{1,2},{2,3},{3,4},{4,5},{5,6},{6,7},{15,8},{8,9},{9,10... | collective-permute-start | bytes 786440 | tf_op jit(solution)/shard_map/ppermute | solution.py:206
  197.6 8.8 %collective-permute-start.13 = (f32[2,256,256]{2,1,0:T(8,128)S(1)}, f32[2,256,256]{2,1,0:T(8,128)S(1)}, u32[]{:S(2)}, u32[]{:S(2)}) collective-permute-start(f32[2,256,256]{2,1,0:T(8,128)S(1)} %get-tuple-element.94.refs_0_), channel_id=1, source_target_pairs={{0,16},{16,0},{32,48},{48,32},{64,80},{80,64},{96,112},{112,96},{1... | collective-permute-start | bytes 1572872 | tf_op jit(solution)/shard_map/ppermute | solution.py:210
  197.6 11.5 %collective-permute-start.17 = (f32[1,256,256]{2,1,0:T(8,128)S(1)}, f32[1,256,256]{2,1,0:T(8,128)S(1)}, u32[]{:S(2)}, u32[]{:S(2)}) collective-permute-start(f32[1,256,256]{2,1,0:T(8,128)S(1)} %slice.67), channel_id=1, source_target_pairs={{0,240},{16,32},{32,16},{48,64},{64,48},{80,96},{96,80},{112,128},... | collective-permute-start | bytes 786440 | tf_op jit(solution)/shard_map/ppermute | solution.py:215
  199.6 10.4 %collective-permute-start.18 = (f32[1,256,256]{2,1,0:T(8,128)S(1)}, f32[1,256,256]{2,1,0:T(8,128)S(1)}, u32[]{:S(2)}, u32[]{:S(2)}) collective-permute-start(f32[1,256,256]{2,1,0:T(8,128)S(1)} %slice.83), channel_id=1, source_target_pairs={{0,32},{16,240},{32,64},{48,16},{64,96},{80,48},{96,128},{112,80},... | collective-permute-start | bytes 786440 | tf_op jit(solution)/shard_map/ppermute | solution.py:216
  204.2 9.0 %collective-permute-start.26 = (f32[256,256]{1,0:T(8,128)S(1)}, f32[256,256]{1,0:T(8,128)S(1)}, u32[]{:S(2)}, u32[]{:S(2)}) collective-permute-start(f32[256,256]{1,0:T(8,128)S(1)} %get-tuple-element.103), channel_id=1, source_target_pairs={{1,0},{2,1},{3,2},{4,3},{5,4},{6,5},{7,6},{0,7},{9,8},{10,9},{11,1... | collective-permute-start | bytes 786440 | tf_op jit(solution)/shard_map/ppermute | solution.py:206
  204.6 9.0 %collective-permute-start.29 = (f32[256,256]{1,0:T(8,128)S(1)}, f32[256,256]{1,0:T(8,128)S(1)}, u32[]{:S(2)}, u32[]{:S(2)}) collective-permute-start(f32[256,256]{1,0:T(8,128)S(1)} %get-tuple-element.104), channel_id=1, source_target_pairs={{7,0},{0,1},{1,2},{2,3},{3,4},{4,5},{5,6},{6,7},{15,8},{8,9},{9,10... | collective-permute-start | bytes 786440 | tf_op jit(solution)/shard_map/ppermute | solution.py:206
  206.4 9.5 %collective-permute-start.14 = (f32[1,256,256]{2,1,0:T(8,128)S(1)}, f32[1,256,256]{2,1,0:T(8,128)S(1)}, u32[]{:S(2)}, u32[]{:S(2)}) collective-permute-start(f32[1,256,256]{2,1,0:T(8,128)S(1)} %slice.64), channel_id=1, source_target_pairs={{0,240},{16,32},{32,16},{48,64},{64,48},{80,96},{96,80},{112,128},... | collective-permute-start | bytes 786440 | tf_op jit(solution)/shard_map/ppermute | solution.py:215
  209.2 10.1 %collective-permute-start.15 = (f32[1,256,256]{2,1,0:T(8,128)S(1)}, f32[1,256,256]{2,1,0:T(8,128)S(1)}, u32[]{:S(2)}, u32[]{:S(2)}) collective-permute-start(f32[1,256,256]{2,1,0:T(8,128)S(1)} %slice.81), channel_id=1, source_target_pairs={{0,32},{16,240},{32,64},{48,16},{64,96},{80,48},{96,128},{112,80},... | collective-permute-start | bytes 786440 | tf_op jit(solution)/shard_map/ppermute | solution.py:216
  213.7 10.0 %collective-permute-start.30 = (f32[256,256]{1,0:T(8,128)S(1)}, f32[256,256]{1,0:T(8,128)S(1)}, u32[]{:S(2)}, u32[]{:S(2)}) collective-permute-start(f32[256,256]{1,0:T(8,128)S(1)} %get-tuple-element.102), channel_id=1, source_target_pairs={{7,0},{0,1},{1,2},{2,3},{3,4},{4,5},{5,6},{6,7},{15,8},{8,9},{9,10... | collective-permute-start | bytes 786440 | tf_op jit(solution)/shard_map/ppermute | solution.py:206
  220.8 6.5 %collective-permute-start.27 = (f32[256,256]{1,0:T(8,128)S(1)}, f32[256,256]{1,0:T(8,128)S(1)}, u32[]{:S(2)}, u32[]{:S(2)}) collective-permute-start(f32[256,256]{1,0:T(8,128)S(1)} %get-tuple-element.101), channel_id=1, source_target_pairs={{1,0},{2,1},{3,2},{4,3},{5,4},{6,5},{7,6},{0,7},{9,8},{10,9},{11,1... | collective-permute-start | bytes 786440 | tf_op jit(solution)/shard_map/ppermute | solution.py:206
  223.7 9.8 %collective-permute-start.31 = (f32[256,256]{1,0:T(8,128)S(1)}, f32[256,256]{1,0:T(8,128)S(1)}, u32[]{:S(2)}, u32[]{:S(2)}) collective-permute-start(f32[256,256]{1,0:T(8,128)S(1)} %fusion.2), channel_id=1, source_target_pairs={{7,0},{0,1},{1,2},{2,3},{3,4},{4,5},{5,6},{6,7},{15,8},{8,9},{9,10... | collective-permute-start | bytes 786440 | tf_op jit(solution)/shard_map/ppermute | solution.py:206
